TPU v7x, 32 devices: a whole 2x2x4 slice. The times are simulated.
32 devices in a mesh: rows: 2 (over core), blk: 16 (over z, y, x).
Axes of the slice: x: 2, y: 2, z: 4, core: 2. Of those that a mesh axis runs over, the one named last changes fastest.
Arguments:
- inputs: bfloat16 [2, 2, 2048, 768], P(None, 'rows', 'blk'), may hold values from -6 to 6
- doc_lengths: int32 [2, 2, 6], P(None, 'rows'), may hold values from 1 to 2043, as said below
- attn_gain: bfloat16 [768], P(('rows', 'blk')), may hold values from 0.25 to 1.75
- w_query: bfloat16 [768, 768], P(('rows', 'blk')), may hold values from -0.0546875 to 0.0546875
- w_key: bfloat16 [768, 768], P(('rows', 'blk')), may hold values from -0.21875 to 0.21875
- w_value: bfloat16 [768, 768], P(('rows', 'blk')), may hold values from -0.21875 to 0.21875
- w_out: bfloat16 [768, 768], P(None, ('rows', 'blk')), may hold values from -1.25 to 1.25
- ff_gain: bfloat16 [768], P(('rows', 'blk')), may hold values from 0.25 to 1.75
- w_gate: bfloat16 [768, 2048], P(('rows', 'blk')), may hold values from -0.21875 to 0.21875
- w_up: bfloat16 [768, 2048], P(('rows', 'blk')), may hold values from -0.21875 to 0.21875
- w_down: bfloat16 [2048, 768], P(None, ('rows', 'blk')), may hold values from -0.125 to 0.125
- rel_table: bfloat16 [32, 12], replicated, may hold values from -4 to 4
- cotangent: bfloat16 [2, 2, 2048, 768], P(None, 'rows', 'blk'), may hold values from -6 to 6
Outputs:
- output: bfloat16 [2, 2, 2048, 768], P(None, 'rows', 'blk')
- input_grad: float32 [2, 2, 2048, 768], P(None, 'rows', 'blk')
- attn_gain_grad: float32 [768], P(('rows', 'blk'))
- query_grad: float32 [768, 768], P(('rows', 'blk'))
- key_grad: float32 [768, 768], P(('rows', 'blk'))
- value_grad: float32 [768, 768], P(('rows', 'blk'))
- out_grad: float32 [768, 768], P(None, ('rows', 'blk'))
- ff_gain_grad: float32 [768], P(('rows', 'blk'))
- gate_grad: float32 [768, 2048], P(('rows', 'blk'))
- up_grad: float32 [768, 2048], P(('rows', 'blk'))
- down_grad: float32 [2048, 768], P(None, ('rows', 'blk'))
- table_grad: float32 [32, 12], replicated
Inputs may be any that keep to these rules, and one draw needn't show every extreme that they name: `doc_lengths`: in every row the 6 pieces sum to 2048. The last piece is padding. One of the other pieces, drawn for each row, starts within the row's first 128 positions and ends within its last 128; every other piece is at most 21 long.
All inputs are finite; a program needn't handle non-finite values.
Results may differ from a plain program's by a relative error of at most 0.02.
Values may be sent and summed in bfloat16 or wider, within the bound.
No kernel may reach another device: no remote copies, remote signals or barrier semaphores. Data moves between devices by JAX's collectives and lax.ppermute only.
A program may use at most 256 MiB of HBM per device.

v0:
```python
import jax
import jax.numpy as jnp
from jax import lax
from jax.sharding import PartitionSpec as P

bucket_edges = (12, 16, 23, 32, 46, 64, 91)
norm_eps = 1e-06
masked_score = -1e30


def passed_along(array, axis, by):
    count = lax.axis_size(axis)
    return lax.ppermute(array, axis, [(i, (i + by) % count) for i in range(count)])


def bucket_of(relative, total_buckets):
    half = total_buckets // 2
    exact = half // 2
    distance = jnp.abs(relative)
    far_bucket = exact + sum(((distance >= edge).astype(jnp.int32) for edge in bucket_edges))
    return jnp.where(relative > 0, half, 0) + jnp.where(distance < exact, distance, far_bucket)


def segments_at(lengths_row, positions):
    bounds = jnp.cumsum(lengths_row)
    return jnp.sum((positions[:, None] >= bounds[None, :]).astype(jnp.int32), axis=1)


def rms_norm(hidden, gain):
    return hidden * lax.rsqrt(jnp.mean(hidden * hidden, axis=-1, keepdims=True) + norm_eps) * gain


def gated(gate, up):
    return jax.nn.gelu(gate, approximate=True) * up


def tdot(left, right):
    return lax.dot_general(
        left, right, (((0,), (0,)), ((), ())), preferred_element_type=jnp.float32
    )


def ndot(left, right):
    return lax.dot_general(
        left, right, (((1,), (1,)), ((), ())), preferred_element_type=jnp.float32
    )


def fetch_weights(attn_gain, w_query, w_key, w_value, ff_gain, w_gate, w_up, w_out, w_down):
    front = (
        lax.all_gather(attn_gain, ("rows", "blk"), axis=0, tiled=True),
        lax.all_gather(w_query, ("rows", "blk"), axis=0, tiled=True),
        lax.all_gather(w_key, ("rows", "blk"), axis=0, tiled=True),
        lax.all_gather(w_value, ("rows", "blk"), axis=0, tiled=True),
        lax.all_gather(ff_gain, ("rows", "blk"), axis=0, tiled=True),
        lax.all_gather(w_gate, ("rows", "blk"), axis=0, tiled=True),
        lax.all_gather(w_up, ("rows", "blk"), axis=0, tiled=True),
    )
    back = (
        lax.all_gather(w_out, ("rows", "blk"), axis=1, tiled=True),
        lax.all_gather(w_down, ("rows", "blk"), axis=1, tiled=True),
    )
    return (front, back)


def pass_grads(pair):
    return passed_along(pair.astype(jnp.bfloat16), "blk", 1).astype(pair.dtype)


def block_scores(queries_h, keys_piece, query_pos, key_pos, query_seg, key_seg, table):
    count = keys_piece.shape[0]
    heads = queries_h.shape[1]
    keys_h = keys_piece.reshape(count, heads, -1)
    raw = jnp.einsum("ihd,jhd->ihj", queries_h, keys_h, preferred_element_type=jnp.float32)
    bucket = bucket_of(key_pos[None, :] - query_pos[:, None], table.shape[0])
    onehot = (
        lax.broadcasted_iota(jnp.int32, (table.shape[0],) + bucket.shape, 0) == bucket[None]
    ).astype(jnp.bfloat16)
    bias = jnp.einsum("bij,bh->ihj", onehot, table, preferred_element_type=jnp.float32)
    allowed = (query_seg[:, None] == key_seg[None, :])[:, None, :]
    return (jnp.where(allowed, raw + bias, masked_score), allowed, onehot, keys_h)


def make_forward_fold(queries_h, query_pos, query_seg, lengths_row, table):

    def fold(carry, piece, start):
        top, total, summed = carry
        keys_piece, values_piece = piece
        count = keys_piece.shape[0]
        key_pos = lax.broadcasted_iota(jnp.int32, (count,), 0)
        key_seg = segments_at(lengths_row, key_pos)
        scores, allowed, onehot, keys_h = block_scores(
            queries_h, keys_piece, query_pos, key_pos, query_seg, key_seg, table
        )
        new_top = jnp.maximum(top, jnp.max(scores, axis=-1))
        probs = jnp.where(allowed, jnp.exp(scores - new_top[..., None]), 0.0)
        values_h = values_piece.reshape(count, queries_h.shape[1], -1)
        summed = jnp.einsum(
            "ihj,jhd->ihd", probs.astype(jnp.bfloat16), values_h, preferred_element_type=jnp.float32
        )
        return (new_top, jnp.sum(probs, axis=-1), summed)

    return fold


def attention_terms(
    queries_h,
    grad_context_h,
    log_total,
    delta,
    query_pos,
    query_seg,
    keys_piece,
    values_piece,
    key_pos,
    key_seg,
    table,
):
    count = keys_piece.shape[0]
    scores, allowed, onehot, keys_h = block_scores(
        queries_h, keys_piece, query_pos, key_pos, query_seg, key_seg, table
    )
    probs = jnp.where(allowed, jnp.exp(scores - log_total[..., None]), 0.0)
    values_h = values_piece.reshape(count, queries_h.shape[1], -1)
    grad_probs = jnp.einsum(
        "ihd,jhd->ihj", grad_context_h, values_h, preferred_element_type=jnp.float32
    )
    grad_scores = (probs * (grad_probs - delta[..., None])).astype(jnp.bfloat16)
    grad_queries = jnp.einsum(
        "ihj,jhd->ihd", grad_scores, keys_h, preferred_element_type=jnp.float32
    )
    grad_keys = jnp.einsum(
        "ihj,ihd->jhd", grad_scores, queries_h, preferred_element_type=jnp.float32
    ).reshape(count, -1)
    grad_values = jnp.einsum(
        "ihj,ihd->jhd",
        probs.astype(jnp.bfloat16),
        grad_context_h,
        preferred_element_type=jnp.float32,
    ).reshape(count, -1)
    grad_table = jnp.einsum("ihj,bij->bh", grad_scores, onehot, preferred_element_type=jnp.float32)
    return (grad_queries, grad_keys, grad_values, grad_table)


def make_backward_block(
    queries_h, grad_context_h, log_total, delta, query_pos, query_seg, lengths_row, table
):

    def block(keys_piece, values_piece, start):
        count = keys_piece.shape[0]
        key_pos = start + lax.broadcasted_iota(jnp.int32, (count,), 0)
        key_seg = segments_at(lengths_row, key_pos)
        return attention_terms(
            queries_h,
            grad_context_h,
            log_total,
            delta,
            query_pos,
            query_seg,
            keys_piece,
            values_piece,
            key_pos,
            key_seg,
            table,
        )

    return block


def body(
    inputs,
    doc_lengths,
    attn_gain,
    w_query,
    w_key,
    w_value,
    w_out,
    ff_gain,
    w_gate,
    w_up,
    w_down,
    rel_table,
    cotangent,
):
    micro = inputs.shape[0]
    tok = inputs.shape[2]
    width = inputs.shape[3]
    inner_width = w_query.shape[1]
    hidden_units = w_gate.shape[1]
    heads = rel_table.shape[1]
    head_size = inner_width // heads
    blocks = lax.axis_size("blk")
    my_block = lax.axis_index("blk")
    query_pos = my_block * tok + lax.broadcasted_iota(jnp.int32, (tok,), 0)
    f32 = jnp.float32
    bf16 = jnp.bfloat16
    acc_gain_a = jnp.zeros((width,), f32)
    acc_query = jnp.zeros((width, inner_width), f32)
    acc_key = jnp.zeros((width, inner_width), f32)
    acc_value = jnp.zeros((width, inner_width), f32)
    acc_out = jnp.zeros((inner_width, width), f32)
    acc_gain_f = jnp.zeros((width,), f32)
    acc_gate = jnp.zeros((width, hidden_units), f32)
    acc_up = jnp.zeros((width, hidden_units), f32)
    acc_down = jnp.zeros((hidden_units, width), f32)
    acc_table = jnp.zeros(rel_table.shape, f32)
    outputs = []
    input_grads = []
    for micro_index in range(micro):
        front, back = fetch_weights(
            attn_gain, w_query, w_key, w_value, ff_gain, w_gate, w_up, w_out, w_down
        )
        gain_a = front[0].astype(f32)
        query_full, key_full, value_full = (front[1], front[2], front[3])
        gain_f = front[4].astype(f32)
        gate_full, up_full = (front[5], front[6])
        out_full, down_full = (back[0], back[1])
        hidden = inputs[micro_index, 0].astype(f32)
        lengths_row = doc_lengths[micro_index, 0]
        query_seg = segments_at(lengths_row, query_pos)
        normed_a = rms_norm(hidden, gain_a).astype(bf16)
        queries = jnp.dot(normed_a, query_full, preferred_element_type=f32).astype(bf16)
        keys = jnp.dot(normed_a, key_full, preferred_element_type=f32).astype(bf16)
        values = jnp.dot(normed_a, value_full, preferred_element_type=f32).astype(bf16)
        queries_h = queries.reshape(tok, heads, head_size)
        fold = make_forward_fold(queries_h, query_pos, query_seg, lengths_row, rel_table)
        start_carry = (
            jnp.full((tok, heads), masked_score, f32),
            jnp.zeros((tok, heads), f32),
            jnp.zeros((tok, heads, head_size), f32),
        )
        top, total, summed = fold(
            start_carry,
            (
                lax.all_gather(keys, "blk", axis=0, tiled=True),
                lax.all_gather(values, "blk", axis=0, tiled=True),
            ),
            jnp.int32(0),
        )
        log_total = top + jnp.log(total)
        context = summed / total[..., None]
        context_b = context.reshape(tok, inner_width).astype(bf16)
        mid = hidden + jnp.dot(context_b, out_full, preferred_element_type=f32)
        normed_f = rms_norm(mid, gain_f).astype(bf16)
        gate = jnp.dot(normed_f, gate_full, preferred_element_type=f32)
        up = jnp.dot(normed_f, up_full, preferred_element_type=f32)
        inner_b = gated(gate, up).astype(bf16)
        result = mid + jnp.dot(inner_b, down_full, preferred_element_type=f32)
        out_rows = [result.astype(bf16)]
        grad_out_b = cotangent[micro_index, 0]
        grad_out = grad_out_b.astype(f32)
        acc_down = acc_down + tdot(inner_b, grad_out_b)
        grad_inner = ndot(grad_out_b, down_full)
        unused_value, gated_pullback = jax.vjp(gated, gate, up)
        grad_gate, grad_up = gated_pullback(grad_inner)
        grad_gate_b = grad_gate.astype(bf16)
        grad_up_b = grad_up.astype(bf16)
        acc_gate = acc_gate + tdot(normed_f, grad_gate_b)
        acc_up = acc_up + tdot(normed_f, grad_up_b)
        grad_normed_f = ndot(grad_gate_b, gate_full) + ndot(grad_up_b, up_full)
        unused_norm, norm_pullback = jax.vjp(rms_norm, mid, gain_f)
        grad_mid_norm, grad_gain_f = norm_pullback(grad_normed_f)
        acc_gain_f = acc_gain_f + grad_gain_f
        grad_mid = grad_out + grad_mid_norm
        grad_branch_b = grad_mid.astype(bf16)
        acc_out = acc_out + tdot(context_b, grad_branch_b)
        grad_context_b = ndot(grad_branch_b, out_full).astype(bf16)
        grad_context_h = grad_context_b.reshape(tok, heads, head_size)
        delta = jnp.sum(grad_context_h.astype(f32) * context, axis=-1)
        zero_q = jnp.zeros((tok, heads, head_size), f32)
        zero_t = jnp.zeros(rel_table.shape, f32)
        block = make_backward_block(
            queries_h,
            grad_context_h,
            log_total,
            delta,
            query_pos,
            query_seg,
            lengths_row,
            rel_table,
        )

        def cycle_back(index, state):
            held, carried, grad_q, table_sum = state
            anchor = (my_block - index) % blocks
            add_q, add_k, add_v, add_t = block(held[0], held[1], anchor * tok)
            carried = pass_grads(carried + jnp.stack([add_k, add_v]))
            held = passed_along(held, "blk", 1)
            return (held, carried, grad_q + add_q, table_sum + add_t)

        held_start = jnp.stack([keys, values])
        carried_start = jnp.zeros((2, tok, inner_width), f32)
        held, carried, grad_q, table_sum = lax.fori_loop(
            0, blocks - 1, cycle_back, (held_start, carried_start, zero_q, zero_t)
        )
        anchor = (my_block - (blocks - 1)) % blocks
        add_q, add_k, add_v, add_t = block(held[0], held[1], anchor * tok)
        carried = pass_grads(carried + jnp.stack([add_k, add_v]))
        grad_q = grad_q + add_q
        table_sum = table_sum + add_t
        grad_keys = carried[0]
        grad_values = carried[1]
        acc_table = acc_table + table_sum
        grad_queries_b = grad_q.reshape(tok, inner_width).astype(bf16)
        grad_keys_b = grad_keys.astype(bf16)
        grad_values_b = grad_values.astype(bf16)
        acc_query = acc_query + tdot(normed_a, grad_queries_b)
        acc_key = acc_key + tdot(normed_a, grad_keys_b)
        acc_value = acc_value + tdot(normed_a, grad_values_b)
        grad_normed_a = (
            ndot(grad_queries_b, query_full)
            + ndot(grad_keys_b, key_full)
            + ndot(grad_values_b, value_full)
        )
        unused_first, first_pullback = jax.vjp(rms_norm, hidden, gain_a)
        grad_hidden_norm, grad_gain_a = first_pullback(grad_normed_a)
        acc_gain_a = acc_gain_a + grad_gain_a
        grad_rows = [grad_mid + grad_hidden_norm]
        outputs.append(jnp.stack(out_rows))
        input_grads.append(jnp.stack(grad_rows))
    front_grads = (
        lax.psum_scatter(acc_gain_a, ("rows", "blk"), scatter_dimension=0, tiled=True),
        lax.psum_scatter(acc_query, ("rows", "blk"), scatter_dimension=0, tiled=True),
        lax.psum_scatter(acc_key, ("rows", "blk"), scatter_dimension=0, tiled=True),
        lax.psum_scatter(acc_value, ("rows", "blk"), scatter_dimension=0, tiled=True),
        lax.psum_scatter(acc_gain_f, ("rows", "blk"), scatter_dimension=0, tiled=True),
        lax.psum_scatter(acc_gate, ("rows", "blk"), scatter_dimension=0, tiled=True),
        lax.psum_scatter(acc_up, ("rows", "blk"), scatter_dimension=0, tiled=True),
    )
    back_grads = (
        lax.psum_scatter(acc_out, ("rows", "blk"), scatter_dimension=1, tiled=True),
        lax.psum_scatter(acc_down, ("rows", "blk"), scatter_dimension=1, tiled=True),
    )
    table_grad = lax.psum(acc_table, ("rows", "blk"))
    return (
        jnp.stack(outputs),
        jnp.stack(input_grads),
        front_grads[0],
        front_grads[1],
        front_grads[2],
        front_grads[3],
        back_grads[0],
        front_grads[4],
        front_grads[5],
        front_grads[6],
        back_grads[1],
        table_grad,
    )


def solution(mesh):
    in_specs = (
        P(None, "rows", "blk", None),
        P(None, "rows", None),
        P(("rows", "blk")),
        P(("rows", "blk"), None),
        P(("rows", "blk"), None),
        P(("rows", "blk"), None),
        P(None, ("rows", "blk")),
        P(("rows", "blk")),
        P(("rows", "blk"), None),
        P(("rows", "blk"), None),
        P(None, ("rows", "blk")),
        P(),
        P(None, "rows", "blk", None),
    )
    out_specs = (
        P(None, "rows", "blk", None),
        P(None, "rows", "blk", None),
        P(("rows", "blk")),
        P(("rows", "blk"), None),
        P(("rows", "blk"), None),
        P(("rows", "blk"), None),
        P(None, ("rows", "blk")),
        P(("rows", "blk")),
        P(("rows", "blk"), None),
        P(("rows", "blk"), None),
        P(None, ("rows", "blk")),
        P(),
    )
    return jax.shard_map(body, mesh=mesh, in_specs=in_specs, out_specs=out_specs, check_vma=False)
```

profile of v0, /device:TPU:0, one launch (start us, length us, event | category | flops | bytes accessed | tf_op | source)
XLA Modules:
  0.0 2175.9 jit_solution(4540261327617196650)
XLA Ops:
  11.2 42.1 %all-reduce.5 = (bf16[768]{0:T(1024)(128)(2,1)S(1)}, bf16[768]{0:T(1024)(128)(2,1)S(1)}) all-reduce(bf16[768]{0:T(1024)(128)(2,1)S(1)} %dynamic-update-slice, bf16[768]{0:T(1024)(128)(2,1)S(1)} %dynamic-update-slice.1), channel_id=1, replica_groups=mesh['rows'=2,'blk'=16] {'rows','blk'}, use_global_device_ids=true, to_apply=%add | all-reduce | flops 1536 | bytes 6144
  54.6 13.2 all-gather.16.cloned.1.call-done
  72.8 50.8 %all-gather.12.cloned.1.call-done = bf16[768,768]{1,0:T(8,128)(2,1)} async-done(((bf16[24,768]{1,0:T(8,128)(2,1)}), bf16[768,768]{1,0:T(8,128)(2,1)}) %all-gather.12.cloned.1.call-update) | async-done | bytes 1179664 | tf_op jit(solution)/shard_map/all_gather | solution.py:54
  133.8 8.7 fusion.58
  142.5 16.8 copy.140
  165.9 13.6 all-gather.20.cloned.1.call-done
  185.2 64.7 %all-gather.18.cloned.1.call-done = bf16[2048,768]{1,0:T(8,128)(2,1)} async-done(((bf16[128,768]{1,0:T(8,128)(2,1)}), bf16[2048,768]{1,0:T(8,128)(2,1)}) %all-gather.18.cloned.1.call-update) | async-done | bytes 3145744 | tf_op jit(solution)/shard_map/all_gather | solution.py:235
  249.9 4.7 copy.138
  254.6 8.6 fusion.250
  263.2 4.6 copy-done
  270.0 49.8 %all-gather.32.cloned.1.call-done = bf16[2048,768]{1,0:T(8,128)(2,1)} async-done(((bf16[128,768]{1,0:T(8,128)(2,1)}), bf16[2048,768]{1,0:T(8,128)(2,1)}) %all-gather.32.cloned.1.call-update) | async-done | bytes 3145744 | tf_op jit(solution)/shard_map/all_gather | solution.py:235
  319.8 4.7 copy.143
  324.4 65.2 %all-gather.30.cloned.1.call-done = bf16[2048,768]{1,0:T(8,128)(2,1)} async-done(((bf16[128,768]{1,0:T(8,128)(2,1)}), bf16[2048,768]{1,0:T(8,128)(2,1)}) %all-gather.30.cloned.1.call-update) | async-done | bytes 3145744 | tf_op jit(solution)/shard_map/all_gather | solution.py:236
  389.6 4.8 copy.142
  394.4 65.2 %all-gather.14.cloned.1.call-done = bf16[2048,768]{1,0:T(8,128)(2,1)} async-done(((bf16[128,768]{1,0:T(8,128)(2,1)}), bf16[2048,768]{1,0:T(8,128)(2,1)}) %all-gather.14.cloned.1.call-update) | async-done | bytes 3145744 | tf_op jit(solution)/shard_map/all_gather | solution.py:236
  459.7 5.1 copy.137
  464.7 8.6 fusion.251
  473.3 41.8 %all-gather.22.cloned.1.call-done = bf16[768,768]{0,1:T(8,128)(2,1)} async-done(((bf16[768,24]{0,1:T(8,128)(2,1)}), bf16[768,768]{0,1:T(8,128)(2,1)}) %all-gather.22.cloned.1.call-update) | async-done | bytes 1179664 | tf_op jit(solution)/shard_map/all_gather | solution.py:60
  517.1 8.6 fusion.248
  527.9 5.2 fusion.249
  536.2 39.8 %all-gather.24.cloned.1.call-done = bf16[768,2048]{1,0:T(8,128)(2,1)} async-done(((bf16[24,2048]{1,0:T(8,128)(2,1)}), bf16[768,2048]{1,0:T(8,128)(2,1)}) %all-gather.24.cloned.1.call-update) | async-done | bytes 3145744 | tf_op jit(solution)/shard_map/all_gather | solution.py:56
  579.5 57.1 %all-gather.26.cloned.1.call-done = bf16[768,2048]{1,0:T(8,128)(2,1)} async-done(((bf16[24,2048]{1,0:T(8,128)(2,1)}), bf16[768,2048]{1,0:T(8,128)(2,1)}) %all-gather.26.cloned.1.call-update) | async-done | bytes 3145744 | tf_op jit(solution)/shard_map/all_gather | solution.py:57
  640.1 57.3 %all-gather.28.cloned.1.call-done = bf16[2048,768]{0,1:T(8,128)(2,1)} async-done(((bf16[2048,24]{0,1:T(8,128)(2,1)}), bf16[2048,768]{0,1:T(8,128)(2,1)}) %all-gather.28.cloned.1.call-update) | async-done | bytes 3145744 | tf_op jit(solution)/shard_map/all_gather | solution.py:61
  697.4 4.9 multiply_convert_fusion.1
  716.8 344.5 %while.45 = (s32[]{:T(128)}, bf16[2,128,768]{1,2,0:T(8,128)(2,1)}, f32[2,128,768]{1,2,0:T(8,128)}, f32[128,12,64]{0,2,1:T(8,128)}, f32[32,12]{0,1:T(8,128)}, /*i...) while((s32[]{:T(128)}, bf16[2,128,768]{1,2,0:T(8,128)(2,1)}, ...), condition=%wide.region_27.28_spmd.clone, body=%wide.region_25.27_spmd.clone.sunk | while | flops 155274384 | bytes 25756016 | solution.py:293
  727.5 13.6 collective-permute-done.3
  750.1 15.4 collective-permute-done.3
  774.3 14.8 collective-permute-done.3
  797.9 13.8 collective-permute-done.3
  820.5 13.8 collective-permute-done.3
  843.1 13.8 collective-permute-done.3
  865.7 13.8 collective-permute-done.3
  888.3 13.8 collective-permute-done.3
  910.9 13.8 collective-permute-done.3
  933.5 13.8 collective-permute-done.3
  956.1 13.8 collective-permute-done.3
  978.7 13.8 collective-permute-done.3
  1001.3 13.8 collective-permute-done.3
  1023.9 13.8 collective-permute-done.3
  1046.5 13.8 collective-permute-done.3
  1065.1 325.5 %while.44 = (s32[]{:T(128)}, bf16[2,128,768]{1,2,0:T(8,128)(2,1)}, f32[2,128,768]{1,2,0:T(8,128)}, f32[128,12,64]{0,2,1:T(8,128)}, f32[32,12]{0,1:T(8,128)}, /*i...) while((s32[]{:T(128)}, bf16[2,128,768]{1,2,0:T(8,128)(2,1)}, ...), condition=%wide.region_19.20_spmd.clone, body=%wide.region_17.19_spmd.clone.sunk | while | flops 155274384 | bytes 25231672 | solution.py:293
  1071.0 16.1 collective-permute-done.1
  1094.7 15.2 collective-permute-done.1
  1117.5 14.2 collective-permute-done.1
  1139.4 13.3 collective-permute-done.1
  1160.3 12.4 collective-permute-done.1
  1180.3 11.5 collective-permute-done.1
  1199.4 11.0 collective-permute-done.1
  1218.1 11.9 collective-permute-done.1
  1237.6 13.0 collective-permute-done.1
  1258.2 14.1 collective-permute-done.1
  1280.0 15.2 collective-permute-done.1
  1302.8 16.3 collective-permute-done.1
  1326.6 17.3 collective-permute-done.1
  1351.6 18.5 collective-permute-done.1
  1377.7 11.0 collective-permute-done.1
  1407.3 9.3 collective-permute-done.5
  1456.3 37.3 %all-reduce.4 = (f32[768]{0:T(1024)S(1)}, f32[768]{0:T(1024)S(1)}, f32[32,12]{0,1:T(8,128)}) all-reduce(f32[768]{0:T(1024)S(1)} %add.831, f32[768]{0:T(1024)S(1)} %add.836, f32[32,12]{0,1:T(8,128)S(1)} %fusion.112), channel_id=2, replica_groups=mesh['rows'=2,'blk'=16] {'rows','blk'}, use_global_device_ids=true, to_apply=%region_32.33.clone | all-reduce | flops 1920 | bytes 15360
  1496.0 104.8 %reduce-scatter.14.cloned.1.call-done = f32[768,24]{0,1:T(8,128)} async-done(((f32[768,768]{0,1:T(8,128)}), f32[768,24]{0,1:T(8,128)}) %reduce-scatter.14.cloned.1.call-update) | async-done | bytes 73744 | tf_op jit(solution)/shard_map/reduce_scatter | solution.py:331
  1600.7 103.8 %reduce-scatter.10.cloned.1.call-done = f32[24,768]{1,0:T(8,128)} async-done(((f32[768,768]{1,0:T(8,128)}), f32[24,768]{1,0:T(8,128)}) %reduce-scatter.10.cloned.1.call-update) | async-done | bytes 73744 | tf_op jit(solution)/shard_map/reduce_scatter | solution.py:324
  1704.5 104.6 %reduce-scatter.12.cloned.1.call-done = f32[24,768]{1,0:T(8,128)} async-done(((f32[768,768]{1,0:T(8,128)}), f32[24,768]{1,0:T(8,128)}) %reduce-scatter.12.cloned.1.call-update) | async-done | bytes 73744 | tf_op jit(solution)/shard_map/reduce_scatter | solution.py:325
  1809.2 119.4 %reduce-scatter.16.cloned.1.call-done = f32[24,2048]{1,0:T(8,128)} async-done(((f32[768,2048]{1,0:T(8,128)}), f32[24,2048]{1,0:T(8,128)}) %reduce-scatter.16.cloned.1.call-update) | async-done | bytes 196624 | tf_op jit(solution)/shard_map/reduce_scatter | solution.py:327
  1928.6 120.5 %reduce-scatter.18.cloned.1.call-done = f32[24,2048]{1,0:T(8,128)} async-done(((f32[768,2048]{1,0:T(8,128)}), f32[24,2048]{1,0:T(8,128)}) %reduce-scatter.18.cloned.1.call-update) | async-done | bytes 196624 | tf_op jit(solution)/shard_map/reduce_scatter | solution.py:328
  2049.1 119.5 %reduce-scatter.20.cloned.1.call-done = f32[2048,24]{0,1:T(8,128)} async-done(((f32[2048,768]{0,1:T(8,128)}), f32[2048,24]{0,1:T(8,128)}) %reduce-scatter.20.cloned.1.call-update) | async-done | bytes 196624 | tf_op jit(solution)/shard_map/reduce_scatter | solution.py:332
  (1343 shorter events, 368.3 us)
Async XLA Ops:
  7.2 60.6 %all-gather.16.cloned.1.call-start = ((), (), s32[]{:S(2)}) async-start(), calls=%async_computation.9 | async-start | bytes 1216512 | tf_op jit(solution)/shard_map/all_gather | solution.py:53
  7.9 115.7 %all-gather.12.cloned.1.call-start = ((), (), s32[]{:S(2)}) async-start(), calls=%async_computation.7 | async-start | bytes 1216512 | tf_op jit(solution)/shard_map/all_gather | solution.py:54
  8.7 170.9 %all-gather.20.cloned.1.call-start = ((), (), s32[]{:S(2)}) async-start(), calls=%async_computation.11 | async-start | bytes 1216512 | tf_op jit(solution)/shard_map/all_gather | solution.py:52
  9.4 240.5 %all-gather.18.cloned.1.call-start = ((), (), s32[]{:S(2)}) async-start(), calls=%async_computation.10 | async-start | bytes 3342336 | tf_op jit(solution)/shard_map/all_gather | solution.py:235
  70.2 249.5 %all-gather.32.cloned.1.call-start = ((), (), s32[]{:S(2)}) async-start(), calls=%async_computation.17 | async-start | bytes 3342336 | tf_op jit(solution)/shard_map/all_gather | solution.py:235
  72.8 316.9 %all-gather.30.cloned.1.call-start = ((), (), s32[]{:S(2)}) async-start(), calls=%async_computation.16 | async-start | bytes 3342336 | tf_op jit(solution)/shard_map/all_gather | solution.py:236
  126.0 333.7 %all-gather.14.cloned.1.call-start = ((), (), s32[]{:S(2)}) async-start(), calls=%async_computation.8 | async-start | bytes 3342336 | tf_op jit(solution)/shard_map/all_gather | solution.py:236
  128.4 386.8 %all-gather.22.cloned.1.call-start = ((), (), s32[]{:S(2)}) async-start(), calls=%async_computation.12 | async-start | bytes 1216512 | tf_op jit(solution)/shard_map/all_gather | solution.py:60
  129.1 446.9 %all-gather.24.cloned.1.call-start = ((), (), s32[]{:S(2)}) async-start(), calls=%async_computation.13 | async-start | bytes 3244032 | tf_op jit(solution)/shard_map/all_gather | solution.py:56
  129.8 506.8 %all-gather.26.cloned.1.call-start = ((), (), s32[]{:S(2)}) async-start(), calls=%async_computation.14 | async-start | bytes 3244032 | tf_op jit(solution)/shard_map/all_gather | solution.py:57
  130.4 567.0 %all-gather.28.cloned.1.call-start = ((), (), s32[]{:S(2)}) async-start(), calls=%async_computation.15 | async-start | bytes 3244032 | tf_op jit(solution)/shard_map/all_gather | solution.py:61
  131.2 1364.8 %reduce-scatter.8.cloned.1.call-start = ((), (), s32[]{:S(2)}) async-start(), calls=%async_computation.18 | async-start | bytes 2433024 | tf_op jit(solution)/shard_map/reduce_scatter | solution.py:323
  717.8 24.3 %collective-permute-start.2 = (bf16[2,128,768]{1,2,0:T(8,128)(2,1)S(1)}, bf16[2,128,768]{1,2,0:T(8,128)(2,1)}, u32[]{:S(2)}, u32[]{:S(2)}) collective-permute-start(bf16[2,128,768]{1,2,0:T(8,128)(2,1)S(1)} %copy.189), channel_id=1, source_target_pairs={{0,1},{1,2},{2,3},{3,4},{4,5},{5,6},{6,7},{7,8},{8,9},{9,10},{10,1... | collective-permute-start | bytes 1179656 | tf_op jit(solution)/shard_map/while/body/eval_jaxpr/ppermute | solution.py:13
  724.8 16.2 collective-permute-start.3
  743.0 23.4 %collective-permute-start.2 = (bf16[2,128,768]{1,2,0:T(8,128)(2,1)S(1)}, bf16[2,128,768]{1,2,0:T(8,128)(2,1)}, u32[]{:S(2)}, u32[]{:S(2)}) collective-permute-start(bf16[2,128,768]{1,2,0:T(8,128)(2,1)S(1)} %copy.189), channel_id=1, source_target_pairs={{0,1},{1,2},{2,3},{3,4},{4,5},{5,6},{6,7},{7,8},{8,9},{9,10},{10,1... | collective-permute-start | bytes 1179656 | tf_op jit(solution)/shard_map/while/body/eval_jaxpr/ppermute | solution.py:13
  748.7 16.9 collective-permute-start.3
  767.5 22.5 %collective-permute-start.2 = (bf16[2,128,768]{1,2,0:T(8,128)(2,1)S(1)}, bf16[2,128,768]{1,2,0:T(8,128)(2,1)}, u32[]{:S(2)}, u32[]{:S(2)}) collective-permute-start(bf16[2,128,768]{1,2,0:T(8,128)(2,1)S(1)} %copy.189), channel_id=1, source_target_pairs={{0,1},{1,2},{2,3},{3,4},{4,5},{5,6},{6,7},{7,8},{8,9},{9,10},{10,1... | collective-permute-start | bytes 1179656 | tf_op jit(solution)/shard_map/while/body/eval_jaxpr/ppermute | solution.py:13
  773.1 15.9 collective-permute-start.3
  791.0 21.6 collective-permute-start.2
  796.7 15.0 collective-permute-start.3
  813.7 21.6 collective-permute-start.2
  819.3 15.0 collective-permute-start.3
  836.3 21.6 collective-permute-start.2
  858.9 21.6 collective-permute-start.2
  881.5 21.6 collective-permute-start.2
  887.1 15.0 collective-permute-start.3
  904.1 21.6 collective-permute-start.2
  926.7 21.6 collective-permute-start.2
  949.3 21.6 collective-permute-start.2
  954.9 15.0 collective-permute-start.3
  971.9 21.6 collective-permute-start.2
  994.5 21.6 collective-permute-start.2
  1017.1 21.6 collective-permute-start.2
  1022.7 15.0 collective-permute-start.3
  1039.7 21.6 collective-permute-start.2
  1066.4 22.7 %collective-permute-start = (bf16[2,128,768]{1,2,0:T(8,128)(2,1)S(1)}, bf16[2,128,768]{1,2,0:T(8,128)(2,1)}, u32[]{:S(2)}, u32[]{:S(2)}) collective-permute-start(bf16[2,128,768]{1,2,0:T(8,128)(2,1)S(1)} %copy.204), channel_id=1, source_target_pairs={{0,1},{1,2},{2,3},{3,4},{4,5},{5,6},{6,7},{7,8},{8,9},{9,10},{10,1... | collective-permute-start | bytes 1179656 | tf_op jit(solution)/shard_map/while/body/eval_jaxpr/ppermute | solution.py:13
  1069.9 17.3 collective-permute-start.1
  1090.1 21.8 collective-permute-start
  1093.6 16.3 collective-permute-start.1
  1112.8 20.8 collective-permute-start
  1116.3 15.4 collective-permute-start.1
  1134.7 19.9 collective-permute-start
  1155.6 19.0 collective-permute-start
  1175.6 18.1 collective-permute-start
  1194.7 17.6 collective-permute-start
  1213.4 18.5 collective-permute-start
  1232.9 19.6 collective-permute-start
  1253.6 20.7 collective-permute-start
  1257.1 15.3 collective-permute-start.1
  1275.3 21.8 %collective-permute-start = (bf16[2,128,768]{1,2,0:T(8,128)(2,1)S(1)}, bf16[2,128,768]{1,2,0:T(8,128)(2,1)}, u32[]{:S(2)}, u32[]{:S(2)}) collective-permute-start(bf16[2,128,768]{1,2,0:T(8,128)(2,1)S(1)} %copy.204), channel_id=1, source_target_pairs={{0,1},{1,2},{2,3},{3,4},{4,5},{5,6},{6,7},{7,8},{8,9},{9,10},{10,1... | collective-permute-start | bytes 1179656 | tf_op jit(solution)/shard_map/while/body/eval_jaxpr/ppermute | solution.py:13
  1278.8 16.3 collective-permute-start.1
  1298.1 22.9 %collective-permute-start = (bf16[2,128,768]{1,2,0:T(8,128)(2,1)S(1)}, bf16[2,128,768]{1,2,0:T(8,128)(2,1)}, u32[]{:S(2)}, u32[]{:S(2)}) collective-permute-start(bf16[2,128,768]{1,2,0:T(8,128)(2,1)S(1)} %copy.204), channel_id=1, source_target_pairs={{0,1},{1,2},{2,3},{3,4},{4,5},{5,6},{6,7},{7,8},{8,9},{9,10},{10,1... | collective-permute-start | bytes 1179656 | tf_op jit(solution)/shard_map/while/body/eval_jaxpr/ppermute | solution.py:13
  1301.6 17.4 collective-permute-start.1
  1322.0 23.9 %collective-permute-start = (bf16[2,128,768]{1,2,0:T(8,128)(2,1)S(1)}, bf16[2,128,768]{1,2,0:T(8,128)(2,1)}, u32[]{:S(2)}, u32[]{:S(2)}) collective-permute-start(bf16[2,128,768]{1,2,0:T(8,128)(2,1)S(1)} %copy.204), channel_id=1, source_target_pairs={{0,1},{1,2},{2,3},{3,4},{4,5},{5,6},{6,7},{7,8},{8,9},{9,10},{10,1... | collective-permute-start | bytes 1179656 | tf_op jit(solution)/shard_map/while/body/eval_jaxpr/ppermute | solution.py:13
  1325.5 18.5 collective-permute-start.1
  1346.9 25.1 %collective-permute-start = (bf16[2,128,768]{1,2,0:T(8,128)(2,1)S(1)}, bf16[2,128,768]{1,2,0:T(8,128)(2,1)}, u32[]{:S(2)}, u32[]{:S(2)}) collective-permute-start(bf16[2,128,768]{1,2,0:T(8,128)(2,1)S(1)} %copy.204), channel_id=1, source_target_pairs={{0,1},{1,2},{2,3},{3,4},{4,5},{5,6},{6,7},{7,8},{8,9},{9,10},{10,1... | collective-permute-start | bytes 1179656 | tf_op jit(solution)/shard_map/while/body/eval_jaxpr/ppermute | solution.py:13
  1350.4 19.7 collective-permute-start.1
  1373.0 17.6 collective-permute-start
  1399.1 201.6 %reduce-scatter.14.cloned.1.call-start = ((), (), s32[]{:S(2)}) async-start(), calls=%async_computation.21 | async-start | bytes 2433024 | tf_op jit(solution)/shard_map/reduce_scatter | solution.py:331
  1402.1 302.5 %reduce-scatter.10.cloned.1.call-start = ((), (), s32[]{:S(2)}) async-start(), calls=%async_computation.19 | async-start | bytes 2433024 | tf_op jit(solution)/shard_map/reduce_scatter | solution.py:324
  1422.9 386.3 %reduce-scatter.12.cloned.1.call-start = ((), (), s32[]{:S(2)}) async-start(), calls=%async_computation.20 | async-start | bytes 2433024 | tf_op jit(solution)/shard_map/reduce_scatter | solution.py:325
  1425.6 503.0 %reduce-scatter.16.cloned.1.call-start = ((), (), s32[]{:S(2)}) async-start(), calls=%async_computation.22 | async-start | bytes 6488064 | tf_op jit(solution)/shard_map/reduce_scatter | solution.py:327
  1430.4 618.7 %reduce-scatter.18.cloned.1.call-start = ((), (), s32[]{:S(2)}) async-start(), calls=%async_computation.23 | async-start | bytes 6488064 | tf_op jit(solution)/shard_map/reduce_scatter | solution.py:328
  1436.2 732.4 %reduce-scatter.20.cloned.1.call-start = ((), (), s32[]{:S(2)}) async-start(), calls=%async_computation.24 | async-start | bytes 6488064 | tf_op jit(solution)/shard_map/reduce_scatter | solution.py:332
  (292 other events, 3160.6 us)
Sparse Core Ops, SparseCore 0:
  10.9 56.8 all-gather.15
  70.7 52.9 all-gather.11
  126.5 52.9 all-gather.19
  182.8 67.0 all-gather.17
  253.1 66.6 all-gather.31
  323.0 66.6 all-gather.29
  393.0 66.6 all-gather.13
  462.5 52.5 all-gather.21
  518.0 57.9 all-gather.23
  578.8 57.8 all-gather.25
  639.5 57.8 all-gather.27
  1399.2 96.6 reduce-scatter.7
  1502.6 98.0 reduce-scatter.13
  1606.5 98.0 reduce-scatter.9
  1711.1 98.0 reduce-scatter.11
  1815.2 113.2 reduce-scatter.15
  1935.5 113.4 reduce-scatter.17
  2055.1 113.4 reduce-scatter.19
where the time goes:
time: 2180 us
  waiting for transfers between devices  1630 us (75%)
  matrix products  206 us (9%)
  other arithmetic  118 us (5%)
  local copies, waits for them, and re-layouts  116 us (5%)
  blocking collectives  79.4 us (4%)
    ppermute x62, waiting for transfers between devices, passed_along(): lax.ppermute(array, axis, [(i, (i + by) % count) for i in range(count)])  434 us
    all_gather x2, waiting for transfers between devices, body(): lax.all_gather(values, 'blk', axis=0, tiled=True)  130 us
    reduce_scatter x1, waiting for transfers between devices, body(): lax.psum_scatter(acc_up, ('rows', 'blk'), scatter_dimension=0, tiled=True)  121 us
    reduce_scatter x1, waiting for transfers between devices, body(): lax.psum_scatter(acc_down, ('rows', 'blk'), scatter_dimension=1, tiled=True)  120 us
    reduce_scatter x1, waiting for transfers between devices, body(): lax.psum_scatter(acc_gate, ('rows', 'blk'), scatter_dimension=0, tiled=True)  119 us
    all_gather x2, waiting for transfers between devices, body(): lax.all_gather(keys, 'blk', axis=0, tiled=True)  114 us
    reduce_scatter x1, waiting for transfers between devices, body(): lax.psum_scatter(acc_out, ('rows', 'blk'), scatter_dimension=1, tiled=True)  105 us
    reduce_scatter x1, waiting for transfers between devices, body(): lax.psum_scatter(acc_value, ('rows', 'blk'), scatter_dimension=0, tiled=T...  105 us
  transfers between devices with their start and end apart: 80, of which 49 were waited for; matrix products, arithmetic and copies ran while one was open for 17% of the time, Pallas kernels for 0%

commit v1 on v0

v1 whole, which is shorter than its diff:
```python
import functools

import jax
import jax.numpy as jnp
from jax import lax
from jax.experimental import pallas as pl
from jax.experimental.pallas import tpu as pltpu
from jax.sharding import PartitionSpec as P

bucket_edges = (12, 16, 23, 32, 46, 64, 91)
norm_eps = 1e-06
masked_score = -1e30
f32 = jnp.float32
bf16 = jnp.bfloat16
both = ("rows", "blk")
chunk = 256
vmem_bytes = 56 * 1024 * 1024


def bucket_of(relative, total_buckets):
    half = total_buckets // 2
    exact = half // 2
    distance = jnp.abs(relative)
    far_bucket = exact + sum(((distance >= edge).astype(jnp.int32) for edge in bucket_edges))
    return jnp.where(relative > 0, half, 0) + jnp.where(distance < exact, distance, far_bucket)


def rms_norm(hidden, gain):
    return hidden * lax.rsqrt(jnp.mean(hidden * hidden, axis=-1, keepdims=True) + norm_eps) * gain


def gated(gate, up):
    return jax.nn.gelu(gate, approximate=True) * up


def dot_on(left, right, left_dim, right_dim):
    return lax.dot_general(
        left, right, (((left_dim,), (right_dim,)), ((), ())), preferred_element_type=f32
    )


def flip(array, axis, bit):
    count = lax.axis_size(axis)
    return lax.ppermute(array, axis, [(i, i ^ bit) for i in range(count)])


def bits_of(count):
    return [1 << k for k in range(count.bit_length() - 1)]


def segments_at(bounds, positions):
    total = jnp.zeros(positions.shape, jnp.int32)
    for bound in bounds:
        total = total + (positions >= bound).astype(jnp.int32)
    return total


def gather_steps(shard, order):
    blocks = lax.axis_size("blk")
    bits = bits_of(blocks)
    spots = len(bits)
    me = lax.axis_index("blk")
    held = shard.reshape((1,) * spots + shard.shape)
    for bit in order:
        dim = spots - 1 - bits.index(bit)
        other = flip(held, "blk", bit)
        high = (me & bit) != 0
        held = jnp.where(
            high, jnp.concatenate([other, held], dim), jnp.concatenate([held, other], dim)
        )
    held = held.reshape((1, blocks) + shard.shape)
    rows = lax.axis_size("rows")
    mine = lax.axis_index("rows")
    held = held.reshape((1,) * len(bits_of(rows)) + (blocks,) + shard.shape)
    for k, bit in enumerate(bits_of(rows)):
        dim = len(bits_of(rows)) - 1 - k
        other = flip(held, "rows", bit)
        high = (mine & bit) != 0
        held = jnp.where(
            high, jnp.concatenate([other, held], dim), jnp.concatenate([held, other], dim)
        )
    return held.reshape((rows * blocks * shard.shape[0],) + shard.shape[1:])


def scatter_steps(total, order):
    blocks = lax.axis_size("blk")
    rows = lax.axis_size("rows")
    bits = bits_of(blocks)
    spots = len(bits)
    row_bits = bits_of(rows)
    share = total.shape[0] // (rows * blocks)
    held = total.reshape((2,) * (len(row_bits) + spots) + (share,) + total.shape[1:])

    def halve(held, axis, bit, dim):
        high = (lax.axis_index(axis) & bit) != 0
        low_half = lax.slice_in_dim(held, 0, 1, axis=dim)
        high_half = lax.slice_in_dim(held, 1, 2, axis=dim)
        keep = jnp.where(high, high_half, low_half)
        send = jnp.where(high, low_half, high_half)
        return keep + flip(send, axis, bit)

    for k, bit in enumerate(row_bits):
        held = halve(held, "rows", bit, len(row_bits) - 1 - k)
    for bit in order:
        held = halve(held, "blk", bit, len(row_bits) + spots - 1 - bits.index(bit))
    return held.reshape((share,) + total.shape[1:])


def gather_orders(blocks):
    bits = bits_of(blocks)
    high = bits[2:]
    return (high + [bits[0], bits[1]], high + [bits[1], bits[0]])


def tile_rows(ref, index, start, stop):
    return jnp.concatenate(
        [ref[2 * index, start:stop, :], ref[2 * index + 1, start:stop, :]], axis=1
    )


def attend_kernel(
    size, blocks, docs, bounds_ref, table_ref, taken_ref, band_ref,
    sent_ref, context_ref, expo_ref, scale_ref, keys_ref, query_ref, score_ref,
):
    micro_index, block = pl.program_id(0), pl.program_id(1)
    chunks = blocks // 2
    tok = chunk // 2
    bounds = [bounds_ref[micro_index, d] for d in range(docs)]

    @pl.when(block == 0)
    def _():
        for s in range(blocks):
            position = s * tok + lax.broadcasted_iota(jnp.int32, (1, tok), 1)
            segment = segments_at(bounds, position)
            row = lax.broadcasted_iota(jnp.int32, (16, tok), 0)
            own = jnp.where(row == segment, 1.0, 0.0)
            part = jnp.where(row == s // 2, 1.0, 0.0)
            tall = jnp.concatenate(
                [
                    taken_ref[s, size : 2 * size, :].astype(f32),
                    own,
                    part,
                    jnp.zeros((2 * size - size - 32, tok), f32),
                ],
                axis=0,
            )
            keys_ref[s * tok : (s + 1) * tok, :] = tall.T.astype(bf16)
        query_ref[size:, :] = jnp.zeros((size, chunk), bf16)

    position = block * chunk + lax.broadcasted_iota(jnp.int32, (1, chunk), 1)
    segment = segments_at(bounds, position)
    row = lax.broadcasted_iota(jnp.int32, (16, chunk), 0)
    query_ref[:size, :] = tile_rows(taken_ref, block, 0, size)
    query_ref[size : size + 16, :] = jnp.where(row == segment, 0.0, masked_score).astype(bf16)
    far = jnp.where(
        row <= block - 2, table_ref[0], jnp.where(row >= block + 2, table_ref[1], 0.0)
    )
    query_ref[size + 16 : size + 32, :] = far.astype(bf16)
    query = query_ref[...]
    top = jnp.full((8, chunk), masked_score, f32)
    for c in range(chunks):
        scores = jnp.dot(
            keys_ref[c * chunk : (c + 1) * chunk, :], query, preferred_element_type=f32
        )
        score_ref[c * chunk : (c + 1) * chunk, :] = scores
        top = jnp.maximum(top, jnp.max(scores.reshape(chunk // 8, 8, chunk), axis=0))
    for j in (-1, 0, 1):

        @pl.when((block + j >= 0) & (block + j < chunks))
        def _():
            spot = pl.ds(pl.multiple_of((block + j) * chunk, chunk), chunk)
            score_ref[spot, :] = score_ref[spot, :] + band_ref[j + 1]

    top = jnp.max(top, axis=0, keepdims=True) + table_ref[2]
    total = jnp.zeros((8, chunk), f32)
    context = jnp.zeros((size, chunk), f32)
    for c in range(chunks):
        expo = jnp.exp(score_ref[c * chunk : (c + 1) * chunk, :] - top)
        total = total + jnp.sum(expo.reshape(chunk // 8, 8, chunk), axis=0)
        low = expo.astype(bf16)
        expo_ref[c * chunk : (c + 1) * chunk, :] = low
        context = context + jnp.dot(
            tile_rows(taken_ref, c, 2 * size, 3 * size), low, preferred_element_type=f32
        )
    scale = 1.0 / jnp.sum(total, axis=0, keepdims=True)
    context = context * scale
    context_ref[...] = context
    scale_ref[...] = scale
    sent_ref[0] = context[:, :tok].astype(bf16)
    sent_ref[1] = context[:, tok:].astype(bf16)


def attend(taken, bounds, scalars, band, blocks, micro, size):
    length = blocks * taken.shape[2] // micro
    tok = length // blocks
    smem = pl.BlockSpec(memory_space=pltpu.SMEM)
    return pl.pallas_call(
        functools.partial(attend_kernel, size, blocks, bounds.shape[1]),
        grid=(micro, blocks // 2),
        in_specs=[
            smem,
            smem,
            pl.BlockSpec((blocks, 3 * size, tok), lambda m, q: (0, 0, m)),
            pl.BlockSpec((3, chunk, chunk), lambda m, q: (0, 0, 0)),
        ],
        out_specs=[
            pl.BlockSpec((2, size, tok), lambda m, q: (q, 0, m)),
            pl.BlockSpec((None, size, chunk), lambda m, q: (m, 0, q)),
            pl.BlockSpec((None, length, chunk), lambda m, q: (m, 0, q)),
            pl.BlockSpec((None, 1, chunk), lambda m, q: (m, 0, q)),
        ],
        out_shape=[
            jax.ShapeDtypeStruct((blocks, size, micro * tok), bf16),
            jax.ShapeDtypeStruct((micro, size, length), f32),
            jax.ShapeDtypeStruct((micro, length, length), bf16),
            jax.ShapeDtypeStruct((micro, 1, length), f32),
        ],
        scratch_shapes=[
            pltpu.VMEM((length, 2 * size), bf16),
            pltpu.VMEM((2 * size, chunk), bf16),
            pltpu.VMEM((length, chunk), f32),
        ],
        compiler_params=pltpu.CompilerParams(vmem_limit_bytes=vmem_bytes),
        name="attend",
    )(bounds, scalars, taken, band)


def attend_back_kernel(
    size, blocks, taken_ref, grad_ref, context_ref, expo_ref, scale_ref,
    sent_ref, band_ref, far_ref,
    queries_ref, tall_ref, wide_ref, delta_ref, grad_queries_ref, grad_scores_ref,
):
    micro_index, c = pl.program_id(0), pl.program_id(1)
    chunks = blocks // 2
    tok = chunk // 2
    length = blocks * tok

    @pl.when(c == 0)
    def _():
        for s in range(blocks):
            spot = slice(s * tok, (s + 1) * tok)
            scaled = grad_ref[s].astype(f32) * scale_ref[:, spot]
            wide_ref[:, spot] = scaled.astype(bf16)
            tall_ref[spot, :] = scaled.T.astype(bf16)
            delta_ref[:, spot] = jnp.sum(scaled * context_ref[:, spot], axis=0, keepdims=True)
            queries_ref[spot, :] = taken_ref[s, :size, :].astype(f32).T.astype(bf16)
        grad_queries_ref[...] = jnp.zeros_like(grad_queries_ref)

    @pl.when((c == 0) & (micro_index == 0))
    def _():
        band_ref[...] = jnp.zeros_like(band_ref)
        far_ref[...] = jnp.zeros_like(far_ref)

    values = tile_rows(taken_ref, c, 2 * size, 3 * size).astype(f32).T.astype(bf16)
    for q in range(chunks):
        spot = slice(q * chunk, (q + 1) * chunk)
        grad_weights = jnp.dot(values, wide_ref[:, spot], preferred_element_type=f32)
        weights = expo_ref[:, spot].astype(f32)
        grad_scores_ref[:, spot] = (weights * (grad_weights - delta_ref[:, spot])).astype(bf16)
    grad_values = jnp.dot(expo_ref[...], tall_ref[...], preferred_element_type=f32).T.astype(bf16)
    grad_keys = jnp.dot(
        grad_scores_ref[...], queries_ref[...], preferred_element_type=f32
    ).T.astype(bf16)
    for t in range(2):
        sent_ref[2 * c + t, size : 2 * size, :] = grad_keys[:, t * tok : (t + 1) * tok]
        sent_ref[2 * c + t, 2 * size :, :] = grad_values[:, t * tok : (t + 1) * tok]
    keys = jnp.concatenate(
        [tile_rows(taken_ref, c, size, 2 * size), jnp.ones((16, chunk), bf16)], axis=0
    )
    for q in range(chunks):
        spot = slice(q * chunk, (q + 1) * chunk)
        part = jnp.dot(keys, grad_scores_ref[:, spot], preferred_element_type=f32)
        grad_queries_ref[:, spot] = grad_queries_ref[:, spot] + part[:size]
        sums = part[size : size + 8]
        far_ref[0, :, spot] = far_ref[0, :, spot] + jnp.where(c <= q - 2, sums, 0.0)
        far_ref[1, :, spot] = far_ref[1, :, spot] + jnp.where(c >= q + 2, sums, 0.0)
    for j in (-1, 0, 1):

        @pl.when((c - j >= 0) & (c - j < chunks))
        def _():
            spot = pl.ds(pl.multiple_of((c - j) * chunk, chunk), chunk)
            band_ref[j + 1] = band_ref[j + 1] + grad_scores_ref[:, spot].astype(f32)

    @pl.when(c == chunks - 1)
    def _():
        for s in range(blocks):
            sent_ref[s, :size, :] = grad_queries_ref[:, s * tok : (s + 1) * tok].astype(bf16)


def attend_back(taken, grads, context, expo, scale, blocks, micro, size):
    length = expo.shape[1]
    tok = length // blocks
    return pl.pallas_call(
        functools.partial(attend_back_kernel, size, blocks),
        grid=(micro, blocks // 2),
        in_specs=[
            pl.BlockSpec((blocks, 3 * size, tok), lambda m, c: (0, 0, m)),
            pl.BlockSpec((blocks, size, tok), lambda m, c: (0, 0, m)),
            pl.BlockSpec((None, size, length), lambda m, c: (m, 0, 0)),
            pl.BlockSpec((None, chunk, length), lambda m, c: (m, c, 0)),
            pl.BlockSpec((None, 1, length), lambda m, c: (m, 0, 0)),
        ],
        out_specs=[
            pl.BlockSpec((blocks, 3 * size, tok), lambda m, c: (0, 0, m)),
            pl.BlockSpec((3, chunk, chunk), lambda m, c: (0, 0, 0)),
            pl.BlockSpec((2, 8, length), lambda m, c: (0, 0, 0)),
        ],
        out_shape=[
            jax.ShapeDtypeStruct((blocks, 3 * size, micro * tok), bf16),
            jax.ShapeDtypeStruct((3, chunk, chunk), f32),
            jax.ShapeDtypeStruct((2, 8, length), f32),
        ],
        scratch_shapes=[
            pltpu.VMEM((length, size), bf16),
            pltpu.VMEM((length, size), bf16),
            pltpu.VMEM((size, length), bf16),
            pltpu.VMEM((1, length), f32),
            pltpu.VMEM((size, length), f32),
            pltpu.VMEM((chunk, length), bf16),
        ],
        compiler_params=pltpu.CompilerParams(vmem_limit_bytes=vmem_bytes),
        name="attend_back",
    )(taken, grads, context, expo, scale)


def body(
    inputs, doc_lengths, attn_gain, w_query, w_key, w_value, w_out, ff_gain,
    w_gate, w_up, w_down, rel_table, cotangent,
):
    micro, _, tok, width = inputs.shape
    inner_width = w_query.shape[1]
    hidden_units = w_gate.shape[1]
    buckets, heads = rel_table.shape
    size = inner_width // heads
    blocks = lax.axis_size("blk")
    rows = lax.axis_size("rows")
    me = lax.axis_index("blk")
    share = w_query.shape[0]
    here = micro * tok
    orders = gather_orders(blocks)

    with jax.named_scope("weights"):
        grouped = jnp.concatenate(
            [w.reshape(share, heads, size) for w in (w_query, w_key, w_value)], axis=2
        ).reshape(share, 3 * inner_width)
        front = jnp.concatenate(
            [
                grouped,
                attn_gain[:, None],
                ff_gain[:, None],
                jnp.zeros((share, 254), bf16),
            ],
            axis=1,
        )
        half = front.shape[1] // 2
        front_full = jnp.concatenate(
            [gather_steps(front[:, :half], orders[0]), gather_steps(front[:, half:], orders[1])],
            axis=1,
        )
        back = jnp.concatenate([w_out.T, w_gate, w_up, w_down.T], axis=1)
        back_full = lax.all_gather(back, both, axis=0, tiled=True)
        qkv_full = front_full[:, : 3 * inner_width]
        gain_a = front_full[:, 3 * inner_width].astype(f32)
        gain_f = front_full[:, 3 * inner_width + 1].astype(f32)
        out_t = back_full[:, :inner_width]
        gate_full = back_full[:, inner_width : inner_width + hidden_units]
        up_full = back_full[:, inner_width + hidden_units : inner_width + 2 * hidden_units]
        down_t = back_full[:, inner_width + 2 * hidden_units :]

    with jax.named_scope("bias"):
        head = jnp.minimum(me, heads - 1)
        column = lax.dynamic_slice_in_dim(rel_table, head, 1, axis=1)[:, 0].astype(f32)
        shape = (3, chunk, chunk)
        relative = (
            lax.broadcasted_iota(jnp.int32, shape, 1)
            - lax.broadcasted_iota(jnp.int32, shape, 2)
            + (lax.broadcasted_iota(jnp.int32, shape, 0) - 1) * chunk
        )
        bucket = bucket_of(relative, buckets)
        band = jnp.zeros(shape, f32)
        for b in range(buckets):
            band = jnp.where(bucket == b, column[b], band)
        scalars = jnp.stack(
            [column[buckets // 2 - 1], column[buckets - 1], jnp.maximum(jnp.max(column), 0.0)]
        )
        bounds = jnp.cumsum(doc_lengths[:, 0], axis=1).astype(jnp.int32)

    with jax.named_scope("project"):
        hidden = inputs.reshape(here, width).astype(f32)
        normed_a = rms_norm(hidden, gain_a).astype(bf16)
        qkv = dot_on(qkv_full, normed_a, 0, 1).astype(bf16)
        qkv = jnp.pad(qkv, ((0, (blocks - heads) * 3 * size), (0, 0)))
        qkv = qkv.reshape(blocks, 3 * size, here)
        taken = lax.all_to_all(qkv, "blk", 0, 0, tiled=True)

    sent, context, expo, scale = attend(taken, bounds, scalars, band, blocks, micro, size)
    with jax.named_scope("context"):
        context_t = lax.all_to_all(sent, "blk", 0, 0, tiled=True)
        context_t = context_t.reshape(blocks * size, here)[:inner_width]

    with jax.named_scope("forward"):
        mid = hidden + dot_on(context_t, out_t, 0, 1)
        normed_f = rms_norm(mid, gain_f).astype(bf16)
        gate = jnp.dot(normed_f, gate_full, preferred_element_type=f32)
        up = jnp.dot(normed_f, up_full, preferred_element_type=f32)
        inner = gated(gate, up).astype(bf16)
        result = (mid + dot_on(inner, down_t, 1, 1)).astype(bf16)

    with jax.named_scope("backward"):
        grad_out_b = cotangent.reshape(here, width)
        grad_out = grad_out_b.astype(f32)
        down_grad = dot_on(grad_out_b, inner, 0, 0)
        grad_inner = jnp.dot(grad_out_b, down_t, preferred_element_type=f32)
        _, gated_pullback = jax.vjp(gated, gate, up)
        grad_gate, grad_up = gated_pullback(grad_inner)
        grad_gate_b = grad_gate.astype(bf16)
        grad_up_b = grad_up.astype(bf16)
        gate_grad = dot_on(normed_f, grad_gate_b, 0, 0)
        up_grad = dot_on(normed_f, grad_up_b, 0, 0)
        grad_normed_f = dot_on(grad_gate_b, gate_full, 1, 1) + dot_on(grad_up_b, up_full, 1, 1)
        _, norm_pullback = jax.vjp(rms_norm, mid, gain_f)
        grad_mid_norm, grad_gain_f = norm_pullback(grad_normed_f)
        grad_mid = grad_out + grad_mid_norm
        grad_branch = grad_mid.astype(bf16)
        out_grad = dot_on(grad_branch, context_t, 0, 1)
        grad_context = dot_on(out_t, grad_branch, 0, 1).astype(bf16)
        grad_context = jnp.pad(grad_context, ((0, (blocks - heads) * size), (0, 0)))
        grad_context = grad_context.reshape(blocks, size, here)
        grads = lax.all_to_all(grad_context, "blk", 0, 0, tiled=True)

    with jax.named_scope("back_grads"):
        back_sum = jnp.concatenate([out_grad, gate_grad, up_grad, down_grad], axis=1).astype(bf16)
        back_grad = lax.psum_scatter(back_sum, both, scatter_dimension=0, tiled=True).astype(f32)

    returned, band_grad, far_grad = attend_back(
        taken, grads, context, expo, scale, blocks, micro, size
    )
    with jax.named_scope("table"):
        sums = [jnp.sum(jnp.where(bucket == b, band_grad, 0.0)) for b in range(buckets)]
        sums[buckets // 2 - 1] = sums[buckets // 2 - 1] + jnp.sum(far_grad[0, 0])
        sums[buckets - 1] = sums[buckets - 1] + jnp.sum(far_grad[1, 0])
        mine = lax.broadcasted_iota(jnp.int32, (buckets, heads), 1) == me
        table_grad = lax.psum(jnp.where(mine, jnp.stack(sums)[:, None], 0.0), both)

    with jax.named_scope("input"):
        grad_qkv = lax.all_to_all(returned, "blk", 0, 0, tiled=True)
        grad_qkv = grad_qkv.reshape(blocks * 3 * size, here)[: 3 * inner_width]
        front_sum = dot_on(normed_a, grad_qkv, 0, 1)
        grad_normed_a = dot_on(grad_qkv, qkv_full, 0, 1)
        _, first_pullback = jax.vjp(rms_norm, hidden, gain_a)
        grad_hidden_norm, grad_gain_a = first_pullback(grad_normed_a)
        input_grad = grad_mid + grad_hidden_norm

    with jax.named_scope("front_grads"):
        front_sum = jnp.concatenate(
            [
                front_sum,
                grad_gain_a[:, None],
                grad_gain_f[:, None],
                jnp.zeros((width, 254), f32),
            ],
            axis=1,
        ).astype(bf16)
        half = front_sum.shape[1] // 2
        front_grad = jnp.concatenate(
            [
                scatter_steps(front_sum[:, :half], orders[0][::-1]),
                scatter_steps(front_sum[:, half:], orders[1][::-1]),
            ],
            axis=1,
        ).astype(f32)
        parts = front_grad[:, : 3 * inner_width].reshape(share, heads, 3, size)
        query_grad, key_grad, value_grad = (
            parts[:, :, k].reshape(share, inner_width) for k in range(3)
        )
        cut = inner_width + hidden_units

    return (
        result.reshape(micro, 1, tok, width),
        input_grad.reshape(micro, 1, tok, width),
        front_grad[:, 3 * inner_width],
        query_grad,
        key_grad,
        value_grad,
        back_grad[:, :inner_width].T,
        front_grad[:, 3 * inner_width + 1],
        back_grad[:, inner_width:cut],
        back_grad[:, cut : cut + hidden_units],
        back_grad[:, cut + hidden_units :].T,
        table_grad,
    )


def solution(mesh):
    weight_rows = P(both, None)
    weight_columns = P(None, both)
    tokens = P(None, "rows", "blk", None)
    in_specs = (
        tokens, P(None, "rows", None), P(both), weight_rows, weight_rows, weight_rows,
        weight_columns, P(both), weight_rows, weight_rows, weight_columns, P(), tokens,
    )
    out_specs = (
        tokens, tokens, P(both), weight_rows, weight_rows, weight_rows,
        weight_columns, P(both), weight_rows, weight_rows, weight_columns, P(),
    )
    return jax.shard_map(body, mesh=mesh, in_specs=in_specs, out_specs=out_specs, check_vma=False)
```

time: 2180 us -> 415 us (0.19)
  waiting for transfers between devices: 1630 us -> 104 us
  matrix products: 206 us -> 33.4 us
  local copies, waits for them, and re-layouts: 116 us -> 47.9 us
  other arithmetic: 118 us -> 53.2 us
  starting transfers between devices: 4.41 us -> 58.4 us
  Pallas kernels: 0 us -> 47.7 us
  blocking collectives: 79.4 us -> 49 us
    reduce_scatter x7 -> x1, waiting for transfers between devices: 673 us -> 0.01 us  [body(): lax.psum_scatter(back_sum, both, scatter_dimension=0, tiled=True)]
    all_gather x11 -> x1, waiting for transfers between devices: 519 us -> 0.02 us  [body(): back_full = lax.all_gather(back, both, axis=0, tiled=True)]
    ppermute x62 -> x20, waiting for transfers between devices: 434 us -> 69.3 us  [flip(): return lax.ppermute(array, axis, [(i, i ^ bit) for i in range(count)])]
    dot_general x266 -> x13, matrix products: 198 us -> 27 us  [the longest x12 23.4 us: dot_on(): lax.dot_general(left, right, (((left_dim,), (right_dim,)), ((), ())), pre...]
    unnamed x2 -> x0, blocking collectives: 79.4 us -> none
    convert_element_type x64 -> x7, other arithmetic: 68.4 us -> 3.47 us  [the longest x1 1.29 us: body(): lax.dynamic_slice_in_dim(rel_table, head, 1, axis=1)[:, 0].astype(f32)]
    psum x0 -> x1, blocking collectives: none -> 49 us  [body(): table_grad = lax.psum(jnp.where(mine, jnp.stack(sums)[:, None], 0.0), both)]
    pallas_call x0 -> x2, Pallas kernels: none -> 47.7 us  [the longest x1 25.5 us: attend_back(): pl.pallas_call(functools.partial(attend_back_kernel, size, blocks), grid=...]
  transfers between devices with their start and end apart: 80 -> 26, of which waited for: 49 -> 19; matrix products, arithmetic and copies ran while one was open for 17% -> 25% of each run, Pallas kernels for 0% -> 12%
where the time goes in v1:
time: 415 us; the launch traced here: 412 us
  waiting for transfers between devices  104 us (25%)
  starting transfers between devices  58.4 us (14%)
  other arithmetic  53.2 us (13%)
  blocking collectives  49 us (12%)
  local copies, waits for them, and re-layouts  47.9 us (12%)
  Pallas kernels  47.7 us (11%)
  matrix products  33.4 us (8%)
  between operations  18 us (4%)
    ppermute x20, waiting for transfers between devices, flip(): return lax.ppermute(array, axis, [(i, i ^ bit) for i in range(count)])  69.3 us
    psum x1, blocking collectives, body(): table_grad = lax.psum(jnp.where(mine, jnp.stack(sums)[:, None], 0.0), both)  49 us
    pallas_call x1, Pallas kernels, attend_back(): pl.pallas_call(functools.partial(attend_back_kernel, size, blocks), grid=...  25.5 us
    select_n x1, other arithmetic, body(): band = jnp.where(bucket == b, column[b], band)  23.7 us
    dot_general x12, matrix products, dot_on(): lax.dot_general(left, right, (((left_dim,), (right_dim,)), ((), ())), pre...  23.4 us
    pallas_call x1, Pallas kernels, attend(): pl.pallas_call(functools.partial(attend_kernel, size, blocks, bounds.shap...  22.2 us
    ppermute x20, starting transfers between devices, flip(): return lax.ppermute(array, axis, [(i, i ^ bit) for i in range(count)])  20.9 us
    another operation x1, local copies, waits for them, and re-layouts, body(): table_grad = lax.psum(jnp.where(mine, jnp.stack(sums)[:, None], 0.0), both)  19.5 us
  transfers between devices with their start and end apart: 26, of which 19 were waited for; matrix products, arithmetic and copies ran while one was open for 25% of the time, Pallas kernels for 12%

profile of v1, /device:TPU:0, one launch (start us, length us, event | category | flops | bytes accessed | tf_op | source)
XLA Modules:
  0.0 412.1 jit_solution(9042753612819629448)
XLA Ops:
  7.2 1.7 pad_maximum_fusion.4
  12.3 3.1 collective-permute-start.5
  15.5 2.1 collective-permute-done.5
  17.6 3.5 collective-permute-start.6
  21.2 4.6 %collective-permute-done.6 = bf16[1,2,1,1,24,1280]{5,4,1,0,3,2:T(8,128)(2,1)S(1)} collective-permute-done((bf16[1,2,1,1,24,1280]{5,4,1,0,3,2:T(8,128)(2,1)S(1)}, bf16[1,2,1,1,24,1280]{5,4,1,0,3,2:T(8,128)(2,1)S(1)}, u32[]{:S(2)}, u32[]{:S(2)}) %collective-permute-start.6) | collective-permute-done | bytes 122912 | tf_op jit(solution)/shard_map/weights/ppermute | solution.py:44
  25.8 1.6 collective-permute-start.7
  27.4 2.1 collective-permute-start.1
  29.6 2.5 collective-permute-done.7
  32.2 1.6 collective-permute-start.8
  33.8 2.5 collective-permute-done.1
  36.3 1.5 collective-permute-start.2
  37.8 7.7 %collective-permute-done.8 = bf16[2,2,2,1,24,1280]{5,4,1,0,3,2:T(8,128)(2,1)S(1)} collective-permute-done((bf16[2,2,2,1,24,1280]{5,4,1,0,3,2:T(8,128)(2,1)S(1)}, bf16[2,2,2,1,24,1280]{5,4,1,0,3,2:T(8,128)(2,1)S(1)}, u32[]{:S(2)}, u32[]{:S(2)}) %collective-permute-start.8) | collective-permute-done | bytes 491552 | tf_op jit(solution)/shard_map/weights/ppermute | solution.py:44
  45.8 6.8 %collective-permute-done.2 = bf16[2,2,1,1,24,1280]{5,4,1,0,3,2:T(8,128)(2,1)S(1)} collective-permute-done((bf16[2,2,1,1,24,1280]{5,4,1,0,3,2:T(8,128)(2,1)S(1)}, bf16[2,2,1,1,24,1280]{5,4,1,0,3,2:T(8,128)(2,1)S(1)}, u32[]{:S(2)}, u32[]{:S(2)}) %collective-permute-start.2) | collective-permute-done | bytes 245792 | tf_op jit(solution)/shard_map/weights/ppermute | solution.py:44
  52.9 9.0 %collective-permute-done.3 = bf16[2,2,1,2,24,1280]{5,4,1,0,3,2:T(8,128)(2,1)S(1)} collective-permute-done((bf16[2,2,1,2,24,1280]{5,4,1,0,3,2:T(8,128)(2,1)S(1)}, bf16[2,2,1,2,24,1280]{5,4,1,0,3,2:T(8,128)(2,1)S(1)}, u32[]{:S(2)}, u32[]{:S(2)}) %collective-permute-start.3) | collective-permute-done | bytes 491552 | tf_op jit(solution)/shard_map/weights/ppermute | solution.py:44
  62.5 1.2 copy-done.11
  64.9 1.8 maximum_select_fusion
  66.7 1.2 convolution_convert_fusion.1
  67.9 1.2 pad.8
  69.2 19.4 %all-to-all-start = ((bf16[16,192,256]{2,1,0:T(8,128)(2,1)}), bf16[16,192,256]{2,1,0:T(8,128)(2,1)S(1)}, u32[]{:S(2)}, u32[]{:S(2)}) async-start(bf16[16,192,256]{2,1,0:T(8,128)(2,1)} %bitcast.28), calls=%async_computation | async-start | bytes 3145728 | tf_op jit(solution)/shard_map/project/all_to_all | solution.py:394
  89.3 1.3 fusion.67
  92.0 1.9 pad_maximum_fusion.6.table_ref
  94.6 23.7 %select_select_fusion.band_ref = f32[3,256,256]{2,1,0:T(8,128)} fusion(f32[]{:T(128)} %bitcast.60, f32[]{:T(128)} %bitcast.59, f32[]{:T(128)} %bitcast.58, f32[]{:T(128)} %bitcast.57, f32[]{:T(128)} %bitcast.56, f32[]{:T(128)} %bitcast.55, f32[]{:T(128)} %bitcast.54, f32[]{:T(128)} %bitcast.53, f32[]{:T(128)} %bitcast.52, f32[]{:T(128)} %bitcast.51, ...), kind=kLoop, calls=%fused_computation.105 | loop fusion | flops 18284544 | bytes 786572 | tf_op jit(solution)/shard_map/bias/jit(_where)/select_n | solution.py:382
  118.3 15.9 %all-to-all-done.taken_ref = bf16[16,192,256]{2,1,0:T(8,128)(2,1)S(1)} async-done(((bf16[16,192,256]{2,1,0:T(8,128)(2,1)}), bf16[16,192,256]{2,1,0:T(8,128)(2,1)S(1)}, u32[]{:S(2)}, u32[]{:S(2)}) %all-to-all-start) | async-done | bytes 1572896 | tf_op jit(solution)/shard_map/project/all_to_all | solution.py:394
  134.2 1.2 copy-done.1
  135.4 22.2 %attend.1 = (bf16[16,64,256]{2,1,0:T(8,128)(2,1)}, f32[2,64,2048]{2,1,0:T(8,128)}, bf16[2,2048,2048]{2,1,0:T(8,128)(2,1)}, f32[2,1,2048]{2,1,0:T(1,128)}) custom-call(s32[2,6]{1,0:T(2,128)} %reduce_window_sum.11.bounds_ref, f32[3]{0:T(128)} %pad_maximum_fusion.6.table_ref, bf16[16,192,256]{2,1,0:T(8,128)(2,1)} %copy-done.1, ...), custom_call_target="tpu_custom_call" | custom-call | tf_op jit(solution)/shard_map/attend/pallas_call | solution.py:197
  157.6 9.7 %all-to-all-start.1 = ((bf16[16,64,256]{2,1,0:T(8,128)(2,1)}), bf16[16,64,256]{2,1,0:T(8,128)(2,1)S(1)}, u32[]{:S(2)}, u32[]{:S(2)}) async-start(bf16[16,64,256]{2,1,0:T(8,128)(2,1)} %get-tuple-element.19), calls=%async_computation.1 | async-start | bytes 1048576 | tf_op jit(solution)/shard_map/context/all_to_all | solution.py:398
  167.4 14.9 %all-to-all-done.1 = bf16[16,64,256]{2,1,0:T(8,128)(2,1)S(1)} async-done(((bf16[16,64,256]{2,1,0:T(8,128)(2,1)}), bf16[16,64,256]{2,1,0:T(8,128)(2,1)S(1)}, u32[]{:S(2)}, u32[]{:S(2)}) %all-to-all-start.1) | async-done | bytes 524320 | tf_op jit(solution)/shard_map/context/all_to_all | solution.py:398
  182.4 2.0 multiply_reduce_fusion.2
  184.5 3.0 fusion.7
  187.6 3.6 fusion.13
  191.2 3.5 fusion.22
  195.7 2.8 convolution_convert_fusion.3
  199.5 1.7 multiply_reduce_fusion
  202.2 1.5 convolution_convert_fusion.5
  205.0 4.2 %all-to-all-start.2 = ((bf16[16,64,256]{2,1,0:T(8,128)(2,1)}), bf16[16,64,256]{2,1,0:T(8,128)(2,1)}, u32[]{:S(2)}, u32[]{:S(2)}) async-start(bf16[16,64,256]{2,1,0:T(8,128)(2,1)} %bitcast.192), calls=%async_computation.2 | async-start | bytes 1048576 | tf_op jit(solution)/shard_map/backward/all_to_all | solution.py:429
  209.3 2.4 copy.93
  211.7 2.5 fusion
  214.4 4.7 %pad_maximum_fusion = bf16[768,6912]{1,0:T(8,128)(2,1)} fusion(bf16[768,2048]{1,0:T(8,128)(2,1)S(1)} %fusion, bf16[768,2048]{1,0:T(8,128)(2,1)S(1)} %copy-done, bf16[768,2048]{1,0:T(8,128)(2,1)S(1)} %convolution_convert_fusion.4, bf16[768,768]{1,0:T(8,128)(2,1)S(1)} %copy-done.7), kind=kLoop, calls=%fused_computation | loop fusion | flops 42467328 | bytes 21233664 | tf_op jit(solution)/shard_map/back_grads/concatenate | solution.py:432
  219.1 4.4 %all-to-all-done.2.grad_ref = bf16[16,64,256]{2,1,0:T(8,128)(2,1)} async-done(((bf16[16,64,256]{2,1,0:T(8,128)(2,1)}), bf16[16,64,256]{2,1,0:T(8,128)(2,1)}, u32[]{:S(2)}, u32[]{:S(2)}) %all-to-all-start.2) | async-done | bytes 524320 | tf_op jit(solution)/shard_map/backward/all_to_all | solution.py:429
  223.5 25.5 %attend_back.1 = (bf16[16,192,256]{2,1,0:T(8,128)(2,1)}, f32[3,256,256]{2,1,0:T(8,128)}, f32[2,8,2048]{2,1,0:T(8,128)}) custom-call(bf16[16,192,256]{2,1,0:T(8,128)(2,1)} %copy-done.1, bf16[16,64,256]{2,1,0:T(8,128)(2,1)} %all-to-all-done.2.grad_ref, f32[2,64,2048]{2,1,0:T(8,128)} %get-tuple-element.20.context_ref, ...), custom_call_target="tpu_custom_call" | custom-call | tf_op jit(solution)/shard_map/attend_back/pallas_call | solution.py:293
  249.0 4.1 %all-to-all-start.3 = ((bf16[16,192,256]{2,1,0:T(8,128)(2,1)}), bf16[16,192,256]{2,1,0:T(8,128)(2,1)S(1)}, u32[]{:S(2)}, u32[]{:S(2)}) async-start(bf16[16,192,256]{2,1,0:T(8,128)(2,1)} %get-tuple-element.23), calls=%async_computation.3 | async-start | bytes 3145728 | tf_op jit(solution)/shard_map/input/all_to_all | solution.py:446
  254.9 4.3 %fusion.30 = bf16[256,768]{1,0:T(8,128)(2,1)} fusion(f32[256,768]{1,0:T(8,128)S(1)} %copy-done.10, bf16[256,2048]{1,0:T(8,128)(2,1)} %get-tuple-element.119, bf16[768,6912]{1,0:T(8,128)(2,1)} %all-gather.2.cloned.1.call-done), kind=kOutput, calls=%fused_computation.41 | convolution fusion | flops 805699584 | bytes 5373952 | tf_op jit(solution)/shard_map/forward/dot_general | solution.py:37
  259.2 1.6 slice_reduce_fusion.3
  260.8 4.4 %select_reduce_fusion = (f32[]{:T(128)}, f32[]{:T(128)}, f32[]{:T(128)}, f32[]{:T(128)}, f32[]{:T(128)}, /*index=5*/f32[]{:T(128)}, f32[]{:T(128)}, f32[]{:T(128...) fusion(f32[3,256,256]{2,1,0:T(8,128)S(1)} %copy-done.19, ...), kind=kLoop, calls=%fused_computation.69 | loop fusion | flops 24575980 | bytes 786572 | tf_op jit(solution)/shard_map/table/reduce_sum | solution.py:439
  267.6 19.5 %stack.139 = f32[32]{0:T(128)S(1)} concatenate(f32[1]{0:T(128)} %bitcast.82, f32[1]{0:T(128)} %bitcast.83, f32[1]{0:T(128)} %bitcast.84, f32[1]{0:T(128)} %bitcast.85, f32[1]{0:T(128)} %bitcast.86, f32[1]{0:T(128)} %bitcast.87, f32[1]{0:T(128)} %bitcast.88, f32[1]{0:T(128)} %bitcast.89, f32[1]{0:T(128)} %bitcast.90, f32[1]{0:T(128)} %bitcast.91, f32[1]{0:T(128)} %bitcast.92, ...), dimensions={0} | concatenate | bytes 256 | tf_op jit(solution)/shard_map/table/stack | solution.py:443
  287.2 49.0 %psum.7 = f32[32,12]{0,1:T(8,128)} all-reduce(f32[32,12]{0,1:T(8,128)S(1)} %broadcast_select_fusion.12), channel_id=1, replica_groups=mesh['rows'=2,'blk'=16] {'rows','blk'}, use_global_device_ids=true, to_apply=%region_43.44 | all-reduce | flops 384 | bytes 3072 | tf_op jit(solution)/shard_map/table/psum | solution.py:443
  336.3 2.3 convolution_convert_fusion
  338.6 1.4 broadcast_select_fusion.2
  341.0 2.6 fusion.41
  345.3 5.7 %concatenate.435 = bf16[768,2560]{1,0:T(8,128)(2,1)} concatenate(bf16[768,2304]{1,0:T(8,128)(2,1)S(1)} %convolution_convert_fusion, bf16[768,1]{1,0:T(8,128)(2,1)} %broadcast_in_dim.230, bf16[768,1]{1,0:T(8,128)(2,1)} %broadcast_in_dim.231, bf16[768,254]{1,0:T(8,128)(2,1)} %broadcast_in_dim.227), dimensions={1} | concatenate | bytes 7864320 | tf_op jit(solution)/shard_map/front_grads/concatenate | solution.py:455
  351.0 1.8 broadcast_select_fusion
  353.0 1.6 add.1280
  354.7 2.7 collective-permute-start.11
  359.6 12.0 %collective-permute-done.11 = bf16[1,2,2,1,2,24,1280]{6,5,4,3,2,1,0:T(8,128)(2,1)S(1)} collective-permute-done((bf16[1,2,2,1,2,24,1280]{6,5,4,3,2,1,0:T(8,128)(2,1)S(1)}, bf16[1,2,2,1,2,24,1280]{6,5,4,3,2,1,0:T(8,128)(2,1)S(1)}, u32[]{:S(2)}, u32[]{:S(2)}) %collective-permute-start.11) | collective-permute-done | bytes 491552 | tf_op jit(solution)/shard_map/front_grads/ppermute | solution.py:44
  371.7 1.4 collective-permute-start.12
  373.1 1.6 collective-permute-done.16
  375.1 4.7 %collective-permute-done.12 = bf16[1,2,2,1,1,24,1280]{6,5,4,3,2,1,0:T(8,128)(2,1)S(1)} collective-permute-done((bf16[1,2,2,1,1,24,1280]{6,5,4,3,2,1,0:T(8,128)(2,1)S(1)}, bf16[1,2,2,1,1,24,1280]{6,5,4,3,2,1,0:T(8,128)(2,1)S(1)}, u32[]{:S(2)}, u32[]{:S(2)}) %collective-permute-start.12) | collective-permute-done | bytes 245792 | tf_op jit(solution)/shard_map/front_grads/ppermute | solution.py:44
  380.8 1.2 collective-permute-done.17
  383.0 7.4 %collective-permute-done.13 = bf16[1,1,2,1,1,24,1280]{6,5,4,3,2,1,0:T(8,128)(2,1)S(1)} collective-permute-done((bf16[1,1,2,1,1,24,1280]{6,5,4,3,2,1,0:T(8,128)(2,1)S(1)}, bf16[1,1,2,1,1,24,1280]{6,5,4,3,2,1,0:T(8,128)(2,1)S(1)}, u32[]{:S(2)}, u32[]{:S(2)}) %collective-permute-start.13) | collective-permute-done | bytes 122912 | tf_op jit(solution)/shard_map/front_grads/ppermute | solution.py:44
  390.6 2.4 collective-permute-done.18
  393.1 1.7 collective-permute-done.14
  394.8 2.5 collective-permute-done.19
  397.7 1.3 slice_reduce_fusion
  403.5 1.8 fusion.71
  (163 shorter events, 27.6 us)
Async XLA Ops:
  7.2 4.8 %copy-start.26 = (bf16[24]{0:T(256)(128)(2,1)S(1)}, bf16[24]{0:T(256)(128)(2,1)}, u32[]{:S(2)}) copy-start(bf16[24]{0:T(256)(128)(2,1)} %param.15) | copy-start | bytes 148
  7.2 4.9 %copy-start.27 = (bf16[24]{0:T(256)(128)(2,1)S(1)}, bf16[24]{0:T(256)(128)(2,1)}, u32[]{:S(2)}) copy-start(bf16[24]{0:T(256)(128)(2,1)} %param.20) | copy-start | bytes 148
  7.2 175.1 %all-gather.2.cloned.1.call-start = ((), (), s32[]{:S(2)}) async-start(), calls=%async_computation.5 | async-start | bytes 10948608 | tf_op jit(solution)/shard_map/weights/all_gather | solution.py:361
  12.3 5.3 %collective-permute-start.5 = (bf16[1,1,1,1,24,1280]{5,4,1,0,3,2:T(8,128)(2,1)S(1)}, bf16[1,1,1,1,24,1280]{5,4,1,0,3,2:T(8,128)(2,1)S(1)}, u32[]{:S(2)}, u32[]{:S(2)}) collective-permute-start(bf16[1,1,1,1,24,1280]{5,4,1,0,3,2:T(8,128)(2,1)S(1)} %get-tuple-element.133), channel_id=1, source_target_pairs={{0,4},{1,5},{2,6},{3,7},{4,0},{5,1},{6,2},{7,3},{8,12},{9,13},{10,... | collective-permute-start | bytes 184328 | tf_op jit(solution)/shard_map/weights/ppermute | solution.py:44
  15.4 12.0 %collective-permute-start = (bf16[1,1,1,1,24,1280]{5,4,3,2,1,0:T(8,128)(2,1)S(1)}, bf16[1,1,1,1,24,1280]{5,4,3,2,1,0:T(8,128)(2,1)S(1)}, u32[]{:S(2)}, u32[]{:S(2)}) collective-permute-start(bf16[1,1,1,1,24,1280]{5,4,3,2,1,0:T(8,128)(2,1)S(1)} %get-tuple-element.135), channel_id=1, source_target_pairs={{0,4},{1,5},{2,6},{3,7},{4,0},{5,1},{6,2},{7,3},{8,12},{9,13},{10,... | collective-permute-start | bytes 184328 | tf_op jit(solution)/shard_map/weights/ppermute | solution.py:44
  17.6 8.1 %collective-permute-start.6 = (bf16[1,2,1,1,24,1280]{5,4,1,0,3,2:T(8,128)(2,1)S(1)}, bf16[1,2,1,1,24,1280]{5,4,1,0,3,2:T(8,128)(2,1)S(1)}, u32[]{:S(2)}, u32[]{:S(2)}) collective-permute-start(bf16[1,2,1,1,24,1280]{5,4,1,0,3,2:T(8,128)(2,1)S(1)} %maximum_select_fusion.11), channel_id=1, source_target_pairs={{0,8},{1,9},{2,10},{3,11},{4,12},{5,13},{6,14},{7,15},{8,0},{9,1},... | collective-permute-start | bytes 368648 | tf_op jit(solution)/shard_map/weights/ppermute | solution.py:44
  25.8 6.3 %collective-permute-start.7 = (bf16[2,2,1,1,24,1280]{5,4,1,0,3,2:T(8,128)(2,1)S(1)}, bf16[2,2,1,1,24,1280]{5,4,1,0,3,2:T(8,128)(2,1)S(1)}, u32[]{:S(2)}, u32[]{:S(2)}) collective-permute-start(bf16[2,2,1,1,24,1280]{5,4,1,0,3,2:T(8,128)(2,1)S(1)} %maximum_select_fusion.8), channel_id=1, source_target_pairs={{0,2},{1,3},{2,0},{3,1},{4,6},{5,7},{6,4},{7,5},{8,10},{9,11},{10,... | collective-permute-start | bytes 737288 | tf_op jit(solution)/shard_map/weights/ppermute | solution.py:44
  27.4 8.8 %collective-permute-start.1 = (bf16[1,2,1,1,24,1280]{5,4,1,0,3,2:T(8,128)(2,1)S(1)}, bf16[1,2,1,1,24,1280]{5,4,1,0,3,2:T(8,128)(2,1)S(1)}, u32[]{:S(2)}, u32[]{:S(2)}) collective-permute-start(bf16[1,2,1,1,24,1280]{5,4,1,0,3,2:T(8,128)(2,1)S(1)} %fusion.59), channel_id=1, source_target_pairs={{0,8},{1,9},{2,10},{3,11},{4,12},{5,13},{6,14},{7,15},{8,0},{9,1},... | collective-permute-start | bytes 368648 | tf_op jit(solution)/shard_map/weights/ppermute | solution.py:44
  32.2 13.3 %collective-permute-start.8 = (bf16[2,2,2,1,24,1280]{5,4,1,0,3,2:T(8,128)(2,1)S(1)}, bf16[2,2,2,1,24,1280]{5,4,1,0,3,2:T(8,128)(2,1)S(1)}, u32[]{:S(2)}, u32[]{:S(2)}) collective-permute-start(bf16[2,2,2,1,24,1280]{5,4,1,0,3,2:T(8,128)(2,1)S(1)} %maximum_select_fusion.5), channel_id=1, source_target_pairs={{0,1},{1,0},{2,3},{3,2},{4,5},{5,4},{6,7},{7,6},{8,9},{9,8},{10,11... | collective-permute-start | bytes 1474568 | tf_op jit(solution)/shard_map/weights/ppermute | solution.py:44
  36.3 16.3 %collective-permute-start.2 = (bf16[2,2,1,1,24,1280]{5,4,1,0,3,2:T(8,128)(2,1)S(1)}, bf16[2,2,1,1,24,1280]{5,4,1,0,3,2:T(8,128)(2,1)S(1)}, u32[]{:S(2)}, u32[]{:S(2)}) collective-permute-start(bf16[2,2,1,1,24,1280]{5,4,1,0,3,2:T(8,128)(2,1)S(1)} %maximum_select_fusion.6), channel_id=1, source_target_pairs={{0,1},{1,0},{2,3},{3,2},{4,5},{5,4},{6,7},{7,6},{8,9},{9,8},{10,11... | collective-permute-start | bytes 737288 | tf_op jit(solution)/shard_map/weights/ppermute | solution.py:44
  37.8 14.9 %copy-start.4 = (bf16[2,1,128,768]{3,2,1,0:T(8,128)(2,1)S(1)}, bf16[2,1,128,768]{3,2,1,0:T(8,128)(2,1)}, u32[]{:S(2)}) copy-start(bf16[2,1,128,768]{3,2,1,0:T(8,128)(2,1)} %param.13) | copy-start | bytes 1179652
  45.7 16.5 %collective-permute-start.9 = (bf16[1,16,24,1280]{3,2,1,0:T(8,128)(2,1)S(1)}, bf16[1,16,24,1280]{3,2,1,0:T(8,128)(2,1)S(1)}, u32[]{:S(2)}, u32[]{:S(2)}) collective-permute-start(bf16[1,16,24,1280]{3,2,1,0:T(8,128)(2,1)S(1)} %bitcast.182), channel_id=1, source_target_pairs={{0,16},{16,0},{1,17},{17,1},{2,18},{18,2},{3,19},{19,3},{4,20},{20... | collective-permute-start | bytes 2949128 | tf_op jit(solution)/shard_map/weights/ppermute | solution.py:44
  52.6 9.2 %collective-permute-start.3 = (bf16[2,2,1,2,24,1280]{5,4,1,0,3,2:T(8,128)(2,1)S(1)}, bf16[2,2,1,2,24,1280]{5,4,1,0,3,2:T(8,128)(2,1)S(1)}, u32[]{:S(2)}, u32[]{:S(2)}) collective-permute-start(bf16[2,2,1,2,24,1280]{5,4,1,0,3,2:T(8,128)(2,1)S(1)} %maximum_select_fusion.4), channel_id=1, source_target_pairs={{0,2},{1,3},{2,0},{3,1},{4,6},{5,7},{6,4},{7,5},{8,10},{9,11},{10,... | collective-permute-start | bytes 1474568 | tf_op jit(solution)/shard_map/weights/ppermute | solution.py:44
  62.1 2.8 collective-permute-start.4
  62.5 1.3 copy-start.11
  64.2 2.4 copy-start.12
  66.7 1.3 copy-start.14
  69.2 19.4 %copy-start.25 = (s32[2,1,6]{2,1,0:T(1,128)S(1)}, s32[2,1,6]{2,1,0:T(1,128)}, u32[]{:S(2)}) copy-start(s32[2,1,6]{2,1,0:T(1,128)} %param.14) | copy-start | bytes 148
  69.2 65.0 %all-to-all-start = ((bf16[16,192,256]{2,1,0:T(8,128)(2,1)}), bf16[16,192,256]{2,1,0:T(8,128)(2,1)S(1)}, u32[]{:S(2)}, u32[]{:S(2)}) async-start(bf16[16,192,256]{2,1,0:T(8,128)(2,1)} %bitcast.28), calls=%async_computation | async-start | bytes 3145728 | tf_op jit(solution)/shard_map/project/all_to_all | solution.py:394
  91.3 66.3 %copy-start.22 = (s32[3]{0:T(128)}, s32[3]{0:T(128)S(1)}, u32[]{:S(2)}) copy-start(s32[3]{0:T(128)S(1)} %add_multiply_fusion) | copy-start | bytes 40
  134.2 1.2 copy-start.1
  157.6 24.7 %all-to-all-start.1 = ((bf16[16,64,256]{2,1,0:T(8,128)(2,1)}), bf16[16,64,256]{2,1,0:T(8,128)(2,1)S(1)}, u32[]{:S(2)}, u32[]{:S(2)}) async-start(bf16[16,64,256]{2,1,0:T(8,128)(2,1)} %get-tuple-element.19), calls=%async_computation.1 | async-start | bytes 1048576 | tf_op jit(solution)/shard_map/context/all_to_all | solution.py:398
  182.3 2.2 copy-start.17
  184.3 16.9 %copy-start.9 = (f32[256,768]{1,0:T(8,128)}, f32[256,768]{1,0:T(8,128)S(1)}, u32[]{:S(2)}) copy-start(f32[256,768]{1,0:T(8,128)S(1)} %get-tuple-element.171) | copy-start | bytes 2359300
  184.5 3.0 copy-start.16
  184.5 6.7 %copy-start.28 = (bf16[768,6912]{1,0:T(8,128)(2,1)S(1)}, bf16[768,6912]{1,0:T(8,128)(2,1)}, u32[]{:S(2)}) copy-start(bf16[768,6912]{1,0:T(8,128)(2,1)} %all-gather.2.cloned.1.call-done) | copy-start | bytes 31850500
  201.2 1.0 copy-start.18
  202.2 2.0 copy-start.2
  205.0 18.4 %all-to-all-start.2 = ((bf16[16,64,256]{2,1,0:T(8,128)(2,1)}), bf16[16,64,256]{2,1,0:T(8,128)(2,1)}, u32[]{:S(2)}, u32[]{:S(2)}) async-start(bf16[16,64,256]{2,1,0:T(8,128)(2,1)} %bitcast.192), calls=%async_computation.2 | async-start | bytes 1048576 | tf_op jit(solution)/shard_map/backward/all_to_all | solution.py:429
  209.3 192.6 %reduce-scatter.2.cloned.1.call-start = ((), (), s32[]{:S(2)}) async-start(), calls=%async_computation.6 | async-start | bytes 10948608 | tf_op jit(solution)/shard_map/back_grads/reduce_scatter | solution.py:433
  211.7 2.5 copy-start
  211.7 2.6 copy-start.7
  249.0 5.1 %copy-start.21 = (bf16[768]{0:T(1024)(128)(2,1)S(1)}, bf16[768]{0:T(1024)(128)(2,1)}, u32[]{:S(2)}) copy-start(bf16[768]{0:T(1024)(128)(2,1)} %get-tuple-element.74) | copy-start | bytes 4612
  249.0 5.9 %copy-start.10 = (f32[256,768]{1,0:T(8,128)S(1)}, f32[256,768]{1,0:T(8,128)}, u32[]{:S(2)}) copy-start(f32[256,768]{1,0:T(8,128)} %copy-done.9) | copy-start | bytes 2359300
  249.0 87.3 %all-to-all-start.3 = ((bf16[16,192,256]{2,1,0:T(8,128)(2,1)}), bf16[16,192,256]{2,1,0:T(8,128)(2,1)S(1)}, u32[]{:S(2)}, u32[]{:S(2)}) async-start(bf16[16,192,256]{2,1,0:T(8,128)(2,1)} %get-tuple-element.23), calls=%async_computation.3 | async-start | bytes 3145728 | tf_op jit(solution)/shard_map/input/all_to_all | solution.py:446
  254.9 5.9 %copy-start.19 = (f32[3,256,256]{2,1,0:T(8,128)S(1)}, f32[3,256,256]{2,1,0:T(8,128)}, u32[]{:S(2)}) copy-start(f32[3,256,256]{2,1,0:T(8,128)} %get-tuple-element.24) | copy-start | bytes 2359300
  254.9 5.9 %copy-start.23 = (s32[3]{0:T(128)S(1)}, s32[3]{0:T(128)}, u32[]{:S(2)}) copy-start(s32[3]{0:T(128)} %copy-done.22) | copy-start | bytes 40
  336.3 3.7 copy-start.15
  338.6 1.5 copy-start.5
  338.6 2.4 copy-start.13
  340.1 12.9 %collective-permute-start.10 = (bf16[1,2,2,2,2,24,1280]{6,5,4,3,2,1,0:T(8,128)(2,1)}, bf16[1,2,2,2,2,24,1280]{6,5,4,3,2,1,0:T(8,128)(2,1)}, u32[]{:S(2)}, u32[]{:S(2)}) collective-permute-start(bf16[1,2,2,2,2,24,1280]{6,5,4,3,2,1,0:T(8,128)(2,1)} %bitcast.74), channel_id=1, source_target_pairs={{0,16},{16,0},{1,17},{17,1},{2,18},{18,2},{3,19},{19,3},{4,20},{20... | collective-permute-start | bytes 2949128 | tf_op jit(solution)/shard_map/front_grads/ppermute | solution.py:44
  351.0 1.9 copy-start.24
  351.0 1.9 copy-start.8
  352.8 5.7 %collective-permute-start.15 = (bf16[1,2,2,2,2,24,1280]{6,5,4,3,2,1,0:T(8,128)(2,1)S(1)}, bf16[1,2,2,2,2,24,1280]{6,5,4,3,2,1,0:T(8,128)(2,1)S(1)}, u32[]{:S(2)}, u32[]{:S(2)}) collective-permute-start(bf16[1,2,2,2,2,24,1280]{6,5,4,3,2,1,0:T(8,128)(2,1)S(1)} %bitcast.199), channel_id=1, source_target_pairs={{0,16},{16,0},{1,17},{17,1},{2,18},{18,2},{3,19},{19,3},{4,20},{20... | collective-permute-start | bytes 2949128 | tf_op jit(solution)/shard_map/front_grads/ppermute | solution.py:44
  352.9 4.4 %copy-start.3 = (f32[256,768]{1,0:T(8,128)S(1)}, f32[256,768]{1,0:T(8,128)}, u32[]{:S(2)}) copy-start(f32[256,768]{1,0:T(8,128)} %copy-done.2) | copy-start | bytes 2359300
  352.9 4.4 %copy-start.6 = (bf16[2,1,128,768]{3,2,1,0:T(8,128)(2,1)S(1)}, bf16[2,1,128,768]{3,2,1,0:T(8,128)(2,1)}, u32[]{:S(2)}) copy-start(bf16[2,1,128,768]{3,2,1,0:T(8,128)(2,1)} %param.13) | copy-start | bytes 1179652
  353.0 4.4 %copy-start.20 = (f32[256,768]{1,0:T(8,128)S(1)}, f32[256,768]{1,0:T(8,128)}, u32[]{:S(2)}) copy-start(f32[256,768]{1,0:T(8,128)} %get-tuple-element.173) | copy-start | bytes 2359300
  354.7 16.9 %collective-permute-start.11 = (bf16[1,2,2,1,2,24,1280]{6,5,4,3,2,1,0:T(8,128)(2,1)S(1)}, bf16[1,2,2,1,2,24,1280]{6,5,4,3,2,1,0:T(8,128)(2,1)S(1)}, u32[]{:S(2)}, u32[]{:S(2)}) collective-permute-start(bf16[1,2,2,1,2,24,1280]{6,5,4,3,2,1,0:T(8,128)(2,1)S(1)} %broadcast_select_fusion.5), channel_id=1, source_target_pairs={{0,2},{1,3},{2,0},{3,1},{4,6},{5,7},{6,4},{7,5},{8,10},{9,11},{10,... | collective-permute-start | bytes 1474568 | tf_op jit(solution)/shard_map/front_grads/ppermute | solution.py:44
  358.8 15.9 %collective-permute-start.16 = (bf16[1,2,2,2,1,24,1280]{6,5,4,3,2,1,0:T(8,128)(2,1)S(1)}, bf16[1,2,2,2,1,24,1280]{6,5,4,3,2,1,0:T(8,128)(2,1)S(1)}, u32[]{:S(2)}, u32[]{:S(2)}) collective-permute-start(bf16[1,2,2,2,1,24,1280]{6,5,4,3,2,1,0:T(8,128)(2,1)S(1)} %broadcast_select_fusion.4), channel_id=1, source_target_pairs={{0,1},{1,0},{2,3},{3,2},{4,5},{5,4},{6,7},{7,6},{8,9},{9,8},{10,11... | collective-permute-start | bytes 1474568 | tf_op jit(solution)/shard_map/front_grads/ppermute | solution.py:44
  371.7 8.1 %collective-permute-start.12 = (bf16[1,2,2,1,1,24,1280]{6,5,4,3,2,1,0:T(8,128)(2,1)S(1)}, bf16[1,2,2,1,1,24,1280]{6,5,4,3,2,1,0:T(8,128)(2,1)S(1)}, u32[]{:S(2)}, u32[]{:S(2)}) collective-permute-start(bf16[1,2,2,1,1,24,1280]{6,5,4,3,2,1,0:T(8,128)(2,1)S(1)} %broadcast_select_fusion.7), channel_id=1, source_target_pairs={{0,1},{1,0},{2,3},{3,2},{4,5},{5,4},{6,7},{7,6},{8,9},{9,8},{10,11... | collective-permute-start | bytes 737288 | tf_op jit(solution)/shard_map/front_grads/ppermute | solution.py:44
  374.8 7.2 %collective-permute-start.17 = (bf16[1,2,2,1,1,24,1280]{6,5,4,3,2,1,0:T(8,128)(2,1)S(1)}, bf16[1,2,2,1,1,24,1280]{6,5,4,3,2,1,0:T(8,128)(2,1)S(1)}, u32[]{:S(2)}, u32[]{:S(2)}) collective-permute-start(bf16[1,2,2,1,1,24,1280]{6,5,4,3,2,1,0:T(8,128)(2,1)S(1)} %broadcast_select_fusion.6), channel_id=1, source_target_pairs={{0,2},{1,3},{2,0},{3,1},{4,6},{5,7},{6,4},{7,5},{8,10},{9,11},{10,... | collective-permute-start | bytes 737288 | tf_op jit(solution)/shard_map/front_grads/ppermute | solution.py:44
  379.9 10.5 %collective-permute-start.13 = (bf16[1,1,2,1,1,24,1280]{6,5,4,3,2,1,0:T(8,128)(2,1)S(1)}, bf16[1,1,2,1,1,24,1280]{6,5,4,3,2,1,0:T(8,128)(2,1)S(1)}, u32[]{:S(2)}, u32[]{:S(2)}) collective-permute-start(bf16[1,1,2,1,1,24,1280]{6,5,4,3,2,1,0:T(8,128)(2,1)S(1)} %broadcast_select_fusion.9), channel_id=1, source_target_pairs={{0,8},{1,9},{2,10},{3,11},{4,12},{5,13},{6,14},{7,15},{8,0},{9,1},... | collective-permute-start | bytes 368648 | tf_op jit(solution)/shard_map/front_grads/ppermute | solution.py:44
  382.1 10.9 %collective-permute-start.18 = (bf16[1,1,2,1,1,24,1280]{6,5,4,3,2,1,0:T(8,128)(2,1)S(1)}, bf16[1,1,2,1,1,24,1280]{6,5,4,3,2,1,0:T(8,128)(2,1)S(1)}, u32[]{:S(2)}, u32[]{:S(2)}) collective-permute-start(bf16[1,1,2,1,1,24,1280]{6,5,4,3,2,1,0:T(8,128)(2,1)S(1)} %broadcast_select_fusion.8), channel_id=1, source_target_pairs={{0,8},{1,9},{2,10},{3,11},{4,12},{5,13},{6,14},{7,15},{8,0},{9,1},... | collective-permute-start | bytes 368648 | tf_op jit(solution)/shard_map/front_grads/ppermute | solution.py:44
  390.5 4.3 %collective-permute-start.14 = (bf16[1,1,1,1,1,24,1280]{6,5,4,3,2,1,0:T(8,128)(2,1)S(1)}, bf16[1,1,1,1,1,24,1280]{6,5,4,3,2,1,0:T(8,128)(2,1)S(1)}, u32[]{:S(2)}, u32[]{:S(2)}) collective-permute-start(bf16[1,1,1,1,1,24,1280]{6,5,4,3,2,1,0:T(8,128)(2,1)S(1)} %broadcast_select_fusion.11), channel_id=1, source_target_pairs={{0,4},{1,5},{2,6},{3,7},{4,0},{5,1},{6,2},{7,3},{8,12},{9,13},{10,... | collective-permute-start | bytes 184328 | tf_op jit(solution)/shard_map/front_grads/ppermute | solution.py:44
  393.0 4.3 %collective-permute-start.19 = (bf16[1,1,1,1,1,24,1280]{6,5,4,3,2,1,0:T(8,128)(2,1)S(1)}, bf16[1,1,1,1,1,24,1280]{6,5,4,3,2,1,0:T(8,128)(2,1)S(1)}, u32[]{:S(2)}, u32[]{:S(2)}) collective-permute-start(bf16[1,1,1,1,1,24,1280]{6,5,4,3,2,1,0:T(8,128)(2,1)S(1)} %broadcast_select_fusion.10), channel_id=1, source_target_pairs={{0,4},{1,5},{2,6},{3,7},{4,0},{5,1},{6,2},{7,3},{8,12},{9,13},{10,... | collective-permute-start | bytes 184328 | tf_op jit(solution)/shard_map/front_grads/ppermute | solution.py:44
Sparse Core Ops, SparseCore 0:
  10.9 119.3 all-gather.1
  219.2 161.5 reduce-scatter.1

commit v2 on v1

v2 whole, which is shorter than its diff:
```python
import functools

import jax
import jax.numpy as jnp
import numpy as np
from jax import lax
from jax.experimental import pallas as pl
from jax.experimental.pallas import tpu as pltpu
from jax.sharding import PartitionSpec as P

bucket_edges = (12, 16, 23, 32, 46, 64, 91)
norm_eps = 1e-06
masked_score = -1e30
f32 = jnp.float32
bf16 = jnp.bfloat16
both = ("rows", "blk")
chunk = 256
vmem_bytes = 56 * 1024 * 1024


def bucket_of(relative, total_buckets):
    half = total_buckets // 2
    exact = half // 2
    distance = jnp.abs(relative)
    far_bucket = exact + sum(((distance >= edge).astype(jnp.int32) for edge in bucket_edges))
    return jnp.where(relative > 0, half, 0) + jnp.where(distance < exact, distance, far_bucket)


def rms_norm(hidden, gain):
    return hidden * lax.rsqrt(jnp.mean(hidden * hidden, axis=-1, keepdims=True) + norm_eps) * gain


def gated(gate, up):
    return jax.nn.gelu(gate, approximate=True) * up


def dot_on(left, right, left_dim, right_dim):
    return lax.dot_general(
        left, right, (((left_dim,), (right_dim,)), ((), ())), preferred_element_type=f32
    )


def flip(array, axis, bit):
    count = lax.axis_size(axis)
    return lax.ppermute(array, axis, [(i, i ^ bit) for i in range(count)])


def bits_of(count):
    return [1 << k for k in range(count.bit_length() - 1)]


def segments_at(bounds, positions):
    total = jnp.zeros(positions.shape, jnp.int32)
    for bound in bounds:
        total = total + (positions >= bound).astype(jnp.int32)
    return total


def groups_of(blocks):
    near = 4
    far = blocks // near
    across = [[f * near + n for f in range(far)] for n in range(near)]
    within = [[f * near + n for n in range(near)] for f in range(far)]
    return far, near, across, within


def staged(rows, blocks, share):
    return rows == 2 and blocks % 4 == 0 and share % 8 == 0


def stage_matrix(rows, blocks, share):
    place = np.arange(rows * blocks * share)
    taken = place
    if staged(rows, blocks, share):
        far, near, _, _ = groups_of(blocks)
        slab = place // share
        half, inner = slab // blocks, slab % blocks
        taken = (half * blocks + inner % far * near + inner // far) * share + place % share
    return jnp.asarray((place[:, None] == taken[None, :]).astype(np.float32), bf16)


def tie_kernel(*refs):
    pass


def tie(value, *after):
    space = pl.BlockSpec(memory_space=pl.ANY)
    return pl.pallas_call(
        tie_kernel,
        in_specs=[space] * (1 + len(after)),
        out_specs=space,
        out_shape=jax.ShapeDtypeStruct(value.shape, value.dtype),
        input_output_aliases={0: 0},
        name="tie",
    )(value, *after)


def exchange(array, groups):
    return lax.all_to_all(array, "blk", 0, 0, tiled=True, axis_index_groups=groups)


def halves_of_whole(whole):
    half = whole.shape[0] // 2
    return whole[:half], whole[half:]


def pack_kernel(query_ref, key_ref, value_ref, gain_a_ref, gain_f_ref, out_ref):
    share = query_ref.shape[0]
    spread = lax.broadcasted_iota(jnp.int32, (share, share), 0) == lax.broadcasted_iota(
        jnp.int32, (share, share), 1
    )
    lane = lax.broadcasted_iota(jnp.int32, (share, 128), 1)
    gains = jnp.zeros((share, 128), f32)
    for k, ref in enumerate((gain_a_ref, gain_f_ref)):
        column = jnp.where(spread, ref[...].astype(f32), 0.0)
        gains = jnp.where(lane == k, jnp.sum(column, axis=1, keepdims=True), gains)
    parts = [query_ref[...], key_ref[...], value_ref[...], gains.astype(bf16)]
    packed = jnp.concatenate(parts, axis=1)
    for copy in range(out_ref.shape[0]):
        out_ref[copy] = packed


def pack(query, key, value, gain_a, gain_f, copies):
    shape = (copies, query.shape[0], 3 * query.shape[1] + 128)
    return pl.pallas_call(
        pack_kernel,
        out_shape=jax.ShapeDtypeStruct(shape, bf16),
        compiler_params=pltpu.CompilerParams(vmem_limit_bytes=vmem_bytes),
        name="pack",
    )(query, key, value, gain_a[None, :], gain_f[None, :])


def gather_front(*parts):
    blocks, rows = lax.axis_size("blk"), lax.axis_size("rows")
    if not staged(rows, blocks, parts[0].shape[0]):
        shard = pack(*parts, 1)[0]
        return halves_of_whole(lax.all_gather(shard, both, axis=0, tiled=True))
    far, near, across, within = groups_of(blocks)
    packed = pack(*parts, far)
    first = exchange(packed.reshape(-1, packed.shape[2]), across)
    own = exchange(jnp.tile(first, (near, 1)), within)
    return own, flip(own, "rows", 1)


def gather_back(shard, after):
    blocks, rows = lax.axis_size("blk"), lax.axis_size("rows")
    if not staged(rows, blocks, shard.shape[0]):
        return lax.all_gather(shard, both, axis=0, tiled=True)
    far, near, across, within = groups_of(blocks)
    own = lax.all_gather(shard, "blk", axis=0, tiled=True, axis_index_groups=across)
    own = tie(own, after)
    return lax.all_gather(own, "blk", axis=0, tiled=True, axis_index_groups=within)


def gather_other(own, after):
    blocks, rows = lax.axis_size("blk"), lax.axis_size("rows")
    if not staged(rows, blocks, own.shape[0] // blocks):
        return halves_of_whole(own)
    own = tie(own, after)
    return own, flip(own, "rows", 1)


def scatter_front(own, share):
    far, near, _, within = groups_of(lax.axis_size("blk"))
    held = exchange(own, within).reshape(near, far * share, own.shape[1])
    return jnp.sum(held.astype(f32), axis=0).astype(bf16)


def scatter_front_end(held, share, *after):
    far, _, across, _ = groups_of(lax.axis_size("blk"))
    return exchange(tie(held, *after), across).reshape(far, share, held.shape[1])


def scatter_back(own):
    _, _, _, within = groups_of(lax.axis_size("blk"))
    return lax.psum_scatter(
        own, "blk", scatter_dimension=0, axis_index_groups=within, tiled=True
    )


def scatter_back_end(part, after):
    _, _, across, _ = groups_of(lax.axis_size("blk"))
    return lax.psum_scatter(
        tie(part, after), "blk", scatter_dimension=0, axis_index_groups=across, tiled=True
    )


def scatter_whole(own, other):
    whole = jnp.concatenate([own, other], axis=0)
    return lax.psum_scatter(whole, both, scatter_dimension=0, tiled=True)


def side(flipped, half):
    return (
        pl.ds(pl.multiple_of(flipped * half, half), half),
        pl.ds(pl.multiple_of((1 - flipped) * half, half), half),
    )


def cost(micros):
    return pl.CostEstimate(flops=int(micros * 1e9), bytes_accessed=0, transcendentals=0)


def tile_rows(ref, index, start, stop):
    return jnp.concatenate(
        [ref[2 * index, start:stop, :], ref[2 * index + 1, start:stop, :]], axis=1
    )


def steps_of(buckets):
    half = buckets // 2
    exact = half // 2
    lows = list(range(1, exact)) + [exact] + list(bucket_edges)
    places = [(1 - low, k) for k, low in reversed(list(enumerate(lows)))]
    return half - 1, places + [(low, half + 1 + k) for k, low in enumerate(lows)]


def relative_tile(j):
    shape = (chunk, chunk)
    return (
        lax.broadcasted_iota(jnp.int32, shape, 0)
        - lax.broadcasted_iota(jnp.int32, shape, 1)
        + j * chunk
    )


def bias_kernel(buckets, heads, head_ref, table_ref, band_ref):
    first, places = steps_of(buckets)
    value = lambda bucket: table_ref[bucket * heads + head_ref[0]]
    for j in (-1, 0, 1):
        relative = relative_tile(j)
        tile = jnp.full((chunk, chunk), value(first), f32)
        for place, bucket in places:
            tile = jnp.where(relative >= place, value(bucket), tile)
        band_ref[j + 1] = tile


def bias_tiles(head, table, buckets):
    smem = pl.BlockSpec(memory_space=pltpu.SMEM)
    return pl.pallas_call(
        functools.partial(bias_kernel, buckets, table.shape[0] // buckets),
        in_specs=[smem, smem],
        out_shape=jax.ShapeDtypeStruct((3, chunk, chunk), f32),
        compiler_params=pltpu.CompilerParams(vmem_limit_bytes=vmem_bytes),
        cost_estimate=cost(2),
        name="bias_tiles",
    )(head, table)


def table_pieces(buckets, band_ref, far_ref, sums_ref):
    first, places = steps_of(buckets)
    edge = chunk // 2
    reach = -(-bucket_edges[-1] // 8) * 8
    sums_ref[...] = jnp.zeros_like(sums_ref)
    relative = [relative_tile(j) for j in (-1, 0, 1)]

    def fold(tile):
        return jnp.sum(tile.reshape(-1, 8, tile.shape[1]), axis=0)

    above = fold(band_ref[0]) + fold(band_ref[1]) + fold(band_ref[2])
    for q in range(far_ref.shape[2] // chunk):
        spot = slice(q * chunk, (q + 1) * chunk)
        above = above + far_ref[0, :, spot] * 0.125 + far_ref[1, :, spot] * 0.125
    right = fold(band_ref[2])
    for q in range(far_ref.shape[2] // chunk):
        right = right + far_ref[1, :, q * chunk : (q + 1) * chunk] * 0.125
    corner = band_ref[2, :reach, edge:]
    corner_relative = relative[2][:reach, edge:]
    left_corner = band_ref[0, chunk - reach :, :edge]
    left_relative = relative[0][chunk - reach :, :edge]
    bucket = first
    for place, following in places:
        if place > 0:
            after = right[:, :edge] + right[:, edge:]
            after = after - fold(jnp.where(corner_relative < place, corner, 0.0))
        else:
            after = right[:, :edge] + right[:, edge:]
            after = after + fold(jnp.where(left_relative >= place, left_corner, 0.0))
        part = fold(jnp.where(relative[1] >= place, band_ref[1], 0.0))
        after = after + part[:, :edge] + part[:, edge:]
        if above.shape[1] == chunk:
            above = above[:, :edge] + above[:, edge:]
        sums_ref[bucket : bucket + 1, :] = jnp.sum(above - after, axis=0, keepdims=True)
        above, bucket = after, following
    sums_ref[bucket : bucket + 1, :] = jnp.sum(above, axis=0, keepdims=True)
    found = jnp.sum(sums_ref[...], axis=1, keepdims=True)
    shape = (buckets, edge)
    spread = lax.broadcasted_iota(jnp.int32, shape, 0) == lax.broadcasted_iota(jnp.int32, shape, 1)
    found = jnp.sum(jnp.where(spread, found, 0.0), axis=0, keepdims=True)
    high = found.astype(bf16).astype(f32)
    middle = (found - high).astype(bf16).astype(f32)
    pieces = [high, middle, found - high - middle, jnp.zeros((13, edge), f32)]
    return jnp.concatenate(pieces, axis=0).astype(bf16)


def attend_kernel(
    size, blocks, docs, buckets, bounds_ref, head_ref, table_ref, taken_ref, band_ref, *refs
):
    sent_ref, context_ref, expo_ref, scale_ref, keys_ref, query_ref, score_ref = refs[-7:]
    block = pl.program_id(0)
    chunks = blocks // 2
    tok = chunk // 2
    bounds = [bounds_ref[0]]
    for d in range(1, docs):
        bounds.append(bounds[-1] + bounds_ref[d])
    heads = table_ref.shape[0] // buckets
    entry = lambda bucket: table_ref[bucket * heads + head_ref[0]]
    highest = jnp.float32(0.0)
    for bucket in range(buckets):
        highest = jnp.maximum(highest, entry(bucket))

    @pl.when(block == 0)
    def _():
        for s in range(blocks):
            position = s * tok + lax.broadcasted_iota(jnp.int32, (1, tok), 1)
            segment = segments_at(bounds, position)
            row = lax.broadcasted_iota(jnp.int32, (16, tok), 0)
            own = jnp.where(row == segment, 1.0, 0.0)
            part = jnp.where(row == s // 2, 1.0, 0.0)
            tall = jnp.concatenate(
                [
                    taken_ref[s, size : 2 * size, :].astype(f32),
                    own,
                    part,
                    jnp.zeros((size - 32, tok), f32),
                ],
                axis=0,
            )
            keys_ref[s * tok : (s + 1) * tok, :] = tall.T.astype(bf16)
        query_ref[size:, :] = jnp.zeros((size, chunk), bf16)

    position = block * chunk + lax.broadcasted_iota(jnp.int32, (1, chunk), 1)
    segment = segments_at(bounds, position)
    row = lax.broadcasted_iota(jnp.int32, (16, chunk), 0)
    query_ref[:size, :] = tile_rows(taken_ref, block, 0, size)
    query_ref[size : size + 16, :] = jnp.where(row == segment, 0.0, masked_score).astype(bf16)
    far = jnp.where(
        row <= block - 2,
        entry(buckets // 2 - 1),
        jnp.where(row >= block + 2, entry(buckets - 1), 0.0),
    )
    query_ref[size + 16 : size + 32, :] = far.astype(bf16)
    query = query_ref[...]
    top = jnp.full((8, chunk), masked_score, f32)
    for c in range(chunks):
        scores = jnp.dot(
            keys_ref[c * chunk : (c + 1) * chunk, :], query, preferred_element_type=f32
        )
        score_ref[c * chunk : (c + 1) * chunk, :] = scores
        top = jnp.maximum(top, jnp.max(scores.reshape(chunk // 8, 8, chunk), axis=0))
    for j in (-1, 0, 1):

        @pl.when((block + j >= 0) & (block + j < chunks))
        def _():
            spot = pl.ds(pl.multiple_of((block + j) * chunk, chunk), chunk)
            score_ref[spot, :] = score_ref[spot, :] + band_ref[j + 1]

    top = jnp.max(top, axis=0, keepdims=True) + highest
    total = jnp.zeros((8, chunk), f32)
    context = jnp.zeros((size, chunk), f32)
    for c in range(chunks):
        expo = jnp.exp(score_ref[c * chunk : (c + 1) * chunk, :] - top)
        total = total + jnp.sum(expo.reshape(chunk // 8, 8, chunk), axis=0)
        low = expo.astype(bf16)
        expo_ref[c * chunk : (c + 1) * chunk, :] = low
        context = context + jnp.dot(
            tile_rows(taken_ref, c, 2 * size, 3 * size), low, preferred_element_type=f32
        )
    scale = 1.0 / jnp.sum(total, axis=0, keepdims=True)
    context = context * scale
    context_ref[...] = context
    scale_ref[...] = scale
    sent_ref[0] = context[:, :tok].astype(bf16)
    sent_ref[1] = context[:, tok:].astype(bf16)


def attend(taken, lengths, head, table, band, buckets, *after):
    blocks, size, tok = taken.shape
    size = size // 3
    length = blocks * tok
    smem = pl.BlockSpec(memory_space=pltpu.SMEM)
    return pl.pallas_call(
        functools.partial(attend_kernel, size, blocks, lengths.shape[0], buckets),
        grid=(blocks // 2,),
        in_specs=[
            smem,
            smem,
            smem,
            pl.BlockSpec((blocks, 3 * size, tok), lambda q: (0, 0, 0)),
            pl.BlockSpec((3, chunk, chunk), lambda q: (0, 0, 0)),
        ]
        + [pl.BlockSpec(memory_space=pl.ANY)] * len(after),
        out_specs=[
            pl.BlockSpec((2, size, tok), lambda q: (q, 0, 0)),
            pl.BlockSpec((size, chunk), lambda q: (0, q)),
            pl.BlockSpec((length, chunk), lambda q: (0, q)),
            pl.BlockSpec((1, chunk), lambda q: (0, q)),
        ],
        out_shape=[
            jax.ShapeDtypeStruct((blocks, size, tok), bf16),
            jax.ShapeDtypeStruct((size, length), f32),
            jax.ShapeDtypeStruct((length, length), bf16),
            jax.ShapeDtypeStruct((1, length), f32),
        ],
        scratch_shapes=[
            pltpu.VMEM((length, 2 * size), bf16),
            pltpu.VMEM((2 * size, chunk), bf16),
            pltpu.VMEM((length, chunk), f32),
        ],
        compiler_params=pltpu.CompilerParams(vmem_limit_bytes=vmem_bytes),
        cost_estimate=cost(11),
        name="attend",
    )(lengths, head, table, taken, band, *after)


def attend_back_kernel(
    size, blocks, buckets, after, taken_ref, grad_ref, context_ref, expo_ref, scale_ref, *refs
):
    sent_ref, band_ref, far_ref, sums_ref, *refs = refs[after:]
    attend_back_steps(
        size, blocks, buckets, taken_ref, grad_ref, context_ref, expo_ref, scale_ref,
        sent_ref, band_ref, far_ref, sums_ref, *refs,
    )


def attend_back_steps(
    size, blocks, buckets, taken_ref, grad_ref, context_ref, expo_ref, scale_ref,
    sent_ref, band_ref, far_ref, sums_ref,
    queries_ref, tall_ref, wide_ref, delta_ref, grad_queries_ref, grad_scores_ref,
):
    c = pl.program_id(0)
    chunks = blocks // 2
    tok = chunk // 2

    @pl.when(c == 0)
    def _():
        for s in range(blocks):
            spot = slice(s * tok, (s + 1) * tok)
            scaled = grad_ref[s].astype(f32) * scale_ref[:, spot]
            wide_ref[:, spot] = scaled.astype(bf16)
            tall_ref[spot, :] = scaled.T.astype(bf16)
            delta_ref[:, spot] = jnp.sum(scaled * context_ref[:, spot], axis=0, keepdims=True)
            queries_ref[spot, :] = taken_ref[s, :size, :].astype(f32).T.astype(bf16)
        grad_queries_ref[...] = jnp.zeros_like(grad_queries_ref)
        band_ref[...] = jnp.zeros_like(band_ref)
        far_ref[...] = jnp.zeros_like(far_ref)

    values = tile_rows(taken_ref, c, 2 * size, 3 * size).astype(f32).T.astype(bf16)
    for q in range(chunks):
        spot = slice(q * chunk, (q + 1) * chunk)
        grad_weights = jnp.dot(values, wide_ref[:, spot], preferred_element_type=f32)
        weights = expo_ref[:, spot].astype(f32)
        grad_scores_ref[:, spot] = (weights * (grad_weights - delta_ref[:, spot])).astype(bf16)
    grad_values = jnp.dot(expo_ref[...], tall_ref[...], preferred_element_type=f32).T.astype(bf16)
    grad_keys = jnp.dot(
        grad_scores_ref[...], queries_ref[...], preferred_element_type=f32
    ).T.astype(bf16)
    for t in range(2):
        sent_ref[2 * c + t, size : 2 * size, :] = grad_keys[:, t * tok : (t + 1) * tok]
        sent_ref[2 * c + t, 2 * size : 3 * size, :] = grad_values[:, t * tok : (t + 1) * tok]
    keys = jnp.concatenate(
        [tile_rows(taken_ref, c, size, 2 * size), jnp.ones((16, chunk), bf16)], axis=0
    )
    for q in range(chunks):
        spot = slice(q * chunk, (q + 1) * chunk)
        part = jnp.dot(keys, grad_scores_ref[:, spot], preferred_element_type=f32)
        grad_queries_ref[:, spot] = grad_queries_ref[:, spot] + part[:size]
        sums = part[size : size + 8]
        far_ref[0, :, spot] = far_ref[0, :, spot] + jnp.where(c <= q - 2, sums, 0.0)
        far_ref[1, :, spot] = far_ref[1, :, spot] + jnp.where(c >= q + 2, sums, 0.0)
    for j in (-1, 0, 1):

        @pl.when((c - j >= 0) & (c - j < chunks))
        def _():
            spot = pl.ds(pl.multiple_of((c - j) * chunk, chunk), chunk)
            band_ref[j + 1] = band_ref[j + 1] + grad_scores_ref[:, spot].astype(f32)

    @pl.when(c == chunks - 1)
    def _():
        for s in range(blocks):
            sent_ref[s, :size, :] = grad_queries_ref[:, s * tok : (s + 1) * tok].astype(bf16)
        pieces = table_pieces(buckets, band_ref, far_ref, sums_ref)
        for s in range(blocks):
            sent_ref[s, 3 * size :, :] = pieces


def attend_back(taken, grads, context, expo, scale, buckets, *after):
    blocks, size, tok = grads.shape
    length = expo.shape[0]
    return pl.pallas_call(
        functools.partial(attend_back_kernel, size, blocks, buckets, len(after)),
        grid=(blocks // 2,),
        in_specs=[
            pl.BlockSpec((blocks, 3 * size, tok), lambda c: (0, 0, 0)),
            pl.BlockSpec((blocks, size, tok), lambda c: (0, 0, 0)),
            pl.BlockSpec((size, length), lambda c: (0, 0)),
            pl.BlockSpec((chunk, length), lambda c: (c, 0)),
            pl.BlockSpec((1, length), lambda c: (0, 0)),
        ]
        + [pl.BlockSpec(memory_space=pl.ANY)] * len(after),
        out_specs=pl.BlockSpec((blocks, 3 * size + 16, tok), lambda c: (0, 0, 0)),
        out_shape=jax.ShapeDtypeStruct((blocks, 3 * size + 16, tok), bf16),
        scratch_shapes=[
            pltpu.VMEM((3, chunk, chunk), f32),
            pltpu.VMEM((2, 8, length), f32),
            pltpu.VMEM((buckets, chunk // 2), f32),
            pltpu.VMEM((length, size), bf16),
            pltpu.VMEM((length, size), bf16),
            pltpu.VMEM((size, length), bf16),
            pltpu.VMEM((1, length), f32),
            pltpu.VMEM((size, length), f32),
            pltpu.VMEM((chunk, length), bf16),
        ],
        compiler_params=pltpu.CompilerParams(vmem_limit_bytes=vmem_bytes),
        cost_estimate=cost(13),
        name="attend_back",
    )(taken, grads, context, expo, scale, *after)


def feed_kernel(
    heads, steps, flipped_ref, matrix_ref, hidden_ref, context_ref, given_ref, gain_ref, *refs
):
    outs, gates, ups, downs = (refs[2 * k : 2 * k + 2] for k in range(4))
    (
        result_ref, grad_mid_ref, grad_context_ref, packet_ref, left_ref,
        normed_ref, branch_ref, cot_ref, mid_ref, total_ref, grad_ref,
    ) = refs[-11:]
    units = steps * chunk
    lead = packet_ref.shape[1] - 3 * units - context_ref.shape[0] * context_ref.shape[1]
    j = pl.program_id(0)
    size, tok = context_ref.shape[1:]
    sides = side(flipped_ref[0], hidden_ref.shape[1] // 2)

    @pl.when(j == 0)
    def _():
        cot_ref[...] = jnp.dot(
            given_ref[...], matrix_ref[...], preferred_element_type=f32
        ).astype(bf16)
        context = context_ref[...].reshape(-1, tok)
        context = context.astype(f32).T.astype(bf16)
        packet_ref[:, packet_ref.shape[1] - context.shape[1] :] = context
        context = context[:, : heads * size]
        for lanes, ref in zip(sides, outs):
            mid_ref[:, lanes] = dot_on(context, ref[...], 1, 1)
        mid = hidden_ref[...].astype(f32) + mid_ref[...]
        mid_ref[...] = mid
        total_ref[...] = mid
        normed_ref[...] = rms_norm(mid, gain_ref[...]).astype(bf16)
        grad_ref[...] = jnp.zeros_like(grad_ref)

    def over_width(left_ref, rights):
        own, other = (
            jnp.dot(left_ref[:, lanes], ref[...], preferred_element_type=f32)
            for lanes, ref in zip(sides, rights)
        )
        return own + other

    gate = over_width(normed_ref, gates)
    up = over_width(normed_ref, ups)
    grad_inner = over_width(cot_ref, downs)
    slope = 0.7978845608028654
    square = gate * gate
    bent = jnp.tanh(slope * (gate + 0.044715 * (square * gate)))
    half = 0.5 * (1.0 + bent)
    gelu = gate * half
    gelu_grad = half + (0.5 * gate) * (1.0 - bent * bent) * (
        slope * (1.0 + (3 * 0.044715) * square)
    )
    inner = (gelu * up).astype(bf16)
    grad_gate = (grad_inner * up * gelu_grad).astype(bf16)
    grad_up = (grad_inner * gelu).astype(bf16)
    for k, part in enumerate((grad_gate, grad_up, inner)):
        packet_ref[:, pl.ds(pl.multiple_of(lead + k * units + j * chunk, chunk), chunk)] = part
    for k, lanes in enumerate(sides):
        total_ref[:, lanes] = total_ref[:, lanes] + dot_on(inner, downs[k][...], 1, 1)
        grad_ref[:, lanes] = (
            grad_ref[:, lanes]
            + dot_on(grad_gate, gates[k][...], 1, 1)
            + dot_on(grad_up, ups[k][...], 1, 1)
        )

    @pl.when(j == steps - 1)
    def _():
        result_ref[...] = dot_on(total_ref[...].astype(bf16), matrix_ref[...], 1, 1).astype(bf16)
        mid = mid_ref[...]
        scale = lax.rsqrt(jnp.mean(mid * mid, axis=-1, keepdims=True) + norm_eps)
        grad_normed = grad_ref[...]
        gained = grad_normed * gain_ref[...]
        inward = jnp.mean(gained * mid, axis=-1, keepdims=True)
        grad_mid = cot_ref[...].astype(f32) + scale * gained - mid * (scale * scale * scale * inward)
        grad_mid_ref[...] = grad_mid
        branch_ref[...] = grad_mid.astype(bf16)
        grad_context = over_width(branch_ref, outs).T.astype(bf16)
        grad_context_ref[...] = jnp.zeros_like(grad_context_ref)
        for h in range(heads):
            grad_context_ref[h] = grad_context[h * size : (h + 1) * size, :]
        own, other = sides
        half = hidden_ref.shape[1] // 2
        for k, ref in enumerate((normed_ref, cot_ref, branch_ref)):
            left_ref[:, k * half : (k + 1) * half] = ref[:, own]
            packet_ref[:, k * half : (k + 1) * half] = ref[:, other]
        packet_ref[:, 3 * half : lead] = jnp.zeros((tok, lead - 3 * half), bf16)


def feed(flipped, matrix, hidden, context, cot, gain, weights, heads, *after):
    tok, width = hidden.shape
    blocks, size, _ = context.shape
    inner_width = heads * size
    units = (weights[0].shape[1] - inner_width) // 3
    steps = units // chunk
    first = inner_width // chunk
    whole = lambda *shape: pl.BlockSpec(shape, lambda j: (0,) * len(shape))
    column = lambda offset: pl.BlockSpec((width // 2, chunk), lambda j: (0, offset + j))
    lead = -(-3 * (width // 2) // (2 * chunk)) * 2 * chunk
    packet = lead + 3 * units + blocks * size
    weight_specs = [whole(width // 2, inner_width)] * 2
    for k in range(3):
        weight_specs += [column(first + k * steps)] * 2
    return pl.pallas_call(
        functools.partial(feed_kernel, heads, steps),
        grid=(steps,),
        in_specs=[
            pl.BlockSpec(memory_space=pltpu.SMEM),
            whole(width, width),
            whole(tok, width),
            whole(blocks, size, tok),
            whole(tok, width),
            whole(1, width),
            *weight_specs,
        ]
        + [pl.BlockSpec(memory_space=pl.ANY)] * len(after),
        out_specs=[
            whole(tok, width),
            whole(tok, width),
            whole(blocks, size, tok),
            whole(tok, packet),
            whole(tok, 3 * (width // 2)),
        ],
        out_shape=[
            jax.ShapeDtypeStruct((tok, width), bf16),
            jax.ShapeDtypeStruct((tok, width), f32),
            jax.ShapeDtypeStruct((blocks, size, tok), bf16),
            jax.ShapeDtypeStruct((tok, packet), bf16),
            jax.ShapeDtypeStruct((tok, 3 * (width // 2)), bf16),
        ],
        scratch_shapes=[pltpu.VMEM((tok, width), bf16)] * 3 + [pltpu.VMEM((tok, width), f32)] * 3,
        compiler_params=pltpu.CompilerParams(vmem_limit_bytes=vmem_bytes),
        cost_estimate=cost(8),
        name="feed",
    )(flipped, matrix, hidden, context, cot, gain, *weights * 4, *after)


def store_tall(ref, parts):
    for m, part in enumerate(parts):
        tok = part.shape[0]
        ref[:, m * tok : (m + 1) * tok] = part.astype(f32).T.astype(bf16)


def weight_grad_kernel(counts, parts, half, *refs):
    j = pl.program_id(0)
    out_ref, tall_ref = refs[-2:]
    lefts, rights = refs[:parts], refs[parts : 2 * parts]
    start = 0
    for k, count in counts:

        @pl.when(j == start)
        def _(k=k):
            store_tall(tall_ref, [ref[:, k * half : (k + 1) * half] for ref in lefts])

        start += count
    right = jnp.concatenate([ref[...] for ref in rights], axis=0)
    out_ref[...] = jnp.dot(tall_ref[...], right, preferred_element_type=f32).astype(bf16)


def weight_grads(lefts, rights, half, units, inner_width, *after):
    tok, block = lefts[0].shape[0], 2 * chunk
    steps = units // block
    counts = [(0, 2 * steps), (1, steps), (2, inner_width // block)]
    total = 3 * steps + inner_width // block
    lead = rights[0].shape[1] - total * block
    anywhere = pl.BlockSpec(memory_space=pl.ANY)
    return pl.pallas_call(
        functools.partial(weight_grad_kernel, counts, len(lefts), half),
        grid=(total,),
        in_specs=[
            pl.BlockSpec((tok, min(left.shape[1], lead)), lambda j: (0, 0)) for left in lefts
        ]
        + [pl.BlockSpec((tok, block), lambda j: (0, lead // block + j))] * len(rights)
        + [anywhere] * len(after),
        out_specs=pl.BlockSpec((half, block), lambda j: (0, j)),
        out_shape=jax.ShapeDtypeStruct((half, total * block), bf16),
        scratch_shapes=[pltpu.VMEM((half, len(lefts) * tok), bf16)],
        compiler_params=pltpu.CompilerParams(vmem_limit_bytes=vmem_bytes),
        cost_estimate=cost(10),
        name="weight_grads",
    )(*lefts, *rights, *after)


def project_kernel(
    heads, flipped_ref, matrix_ref, inputs_ref, own_ref, other_ref, after_ref, *refs
):
    micro, tok, width = inputs_ref.shape
    sent, (tokens_ref, normed_ref, gain_a_ref, gain_f_ref, gains_ref) = refs[:micro], refs[micro:]
    inner_width = (own_ref.shape[1] - 128) // 3
    size = inner_width // heads
    sides = side(flipped_ref[0], width // 2)
    for lanes, ref in zip(sides, (own_ref, other_ref)):
        gains_ref[:, lanes] = ref[:, 3 * inner_width :].astype(f32).T[:8]
    gain_a_ref[...] = gains_ref[:1]
    gain_f_ref[...] = gains_ref[1:2]
    hidden = jnp.dot(
        inputs_ref[...].reshape(micro * tok, width), matrix_ref[...], preferred_element_type=f32
    )
    tokens_ref[...] = hidden.astype(bf16).reshape(micro, tok, width)
    normed_ref[...] = rms_norm(hidden, gains_ref[:1]).astype(bf16)
    for ref in sent:
        ref[heads:] = jnp.zeros((ref.shape[0] - heads,) + ref.shape[1:], bf16)
    for k in range(3):
        for half in range(2):
            start = k * inner_width + half * (inner_width // 2)
            own, other = (
                jnp.dot(
                    normed_ref[:, lanes],
                    ref[:, start : start + inner_width // 2],
                    preferred_element_type=f32,
                )
                for lanes, ref in zip(sides, (own_ref, other_ref))
            )
            part = (own + other).T.astype(bf16)
            for h in range(heads // 2):
                for m, ref in enumerate(sent):
                    ref[half * (heads // 2) + h, k * size : (k + 1) * size, :] = part[
                        h * size : (h + 1) * size, m * tok : (m + 1) * tok
                    ]


def project(flipped, matrix, inputs, weights, heads, blocks, after):
    micro, tok, width = inputs.shape
    size = (weights[0].shape[1] - 128) // 3 // heads
    vmem = pl.BlockSpec(memory_space=pltpu.VMEM)
    outs = pl.pallas_call(
        functools.partial(project_kernel, heads),
        in_specs=[
            pl.BlockSpec(memory_space=pltpu.SMEM),
            vmem,
            vmem,
            vmem,
            vmem,
            pl.BlockSpec(memory_space=pl.ANY),
        ],
        out_shape=[jax.ShapeDtypeStruct((blocks, 3 * size, tok), bf16)] * micro
        + [
            jax.ShapeDtypeStruct((micro, tok, width), bf16),
            jax.ShapeDtypeStruct((micro * tok, width), bf16),
            jax.ShapeDtypeStruct((1, width), f32),
            jax.ShapeDtypeStruct((1, width), f32),
        ],
        scratch_shapes=[pltpu.VMEM((8, width), f32)],
        compiler_params=pltpu.CompilerParams(vmem_limit_bytes=vmem_bytes),
        cost_estimate=cost(3),
        name="project",
    )(flipped, matrix, inputs, *weights, after)
    return outs[:micro], *outs[micro:]


def lined(refs, heads, size, lined_ref):
    tok = refs[0].shape[2]
    for m, ref in enumerate(refs):
        for k in range(3):
            for h in range(heads):
                start = (k * heads + h) * size
                lined_ref[start : start + size, m * tok : (m + 1) * tok] = ref[
                    h, k * size : (k + 1) * size, :
                ]


def input_grad_kernel(heads, micro, *refs):
    flipped_ref, matrix_ref, inputs_ref, own_weights, other_weights, gains_ref = refs[:6]
    grads, mids = (refs[6 + k * micro : 6 + (k + 1) * micro] for k in range(2))
    input_grad_ref, wide_ref, lined_ref = refs[-3:]
    tok, width = inputs_ref.shape[1:]
    inner_width = (own_weights.shape[1] - 128) // 3
    sides = side(flipped_ref[0], width // 2)
    lined(grads, heads, inner_width // heads, lined_ref)
    for ref, rows in zip((own_weights, other_weights), sides):
        wide_ref[rows, :] = jnp.dot(
            ref[:, : 3 * inner_width], lined_ref[...], preferred_element_type=f32
        )
    gain = gains_ref[...]
    for m in range(micro):
        grad = wide_ref[:, m * tok : (m + 1) * tok].T
        hidden = inputs_ref[m].astype(f32)
        scale = lax.rsqrt(jnp.mean(hidden * hidden, axis=-1, keepdims=True) + norm_eps)
        gained = grad * gain
        inward = jnp.mean(gained * hidden, axis=-1, keepdims=True)
        found = mids[m][...] + scale * gained - hidden * (scale * scale * scale * inward)
        high = found.astype(bf16)
        rest = found - high.astype(f32)
        middle = rest.astype(bf16)
        low = (rest - middle.astype(f32)).astype(bf16)
        input_grad_ref[m] = sum(
            dot_on(part, matrix_ref[...], 1, 1) for part in (low, middle, high)
        )


def input_grads(flipped, matrix, inputs, weights, gains, grads, mids, heads, *after):
    micro, tok, width = inputs.shape
    inner_width = (weights[0].shape[1] - 128) // 3
    vmem = pl.BlockSpec(memory_space=pltpu.VMEM)
    return pl.pallas_call(
        functools.partial(input_grad_kernel, heads, micro),
        in_specs=[pl.BlockSpec(memory_space=pltpu.SMEM)]
        + [vmem] * (5 + 2 * micro)
        + [pl.BlockSpec(memory_space=pl.ANY)] * len(after),
        out_shape=jax.ShapeDtypeStruct((micro, tok, width), f32),
        scratch_shapes=[
            pltpu.VMEM((width, micro * tok), f32),
            pltpu.VMEM((3 * inner_width, micro * tok), bf16),
        ],
        compiler_params=pltpu.CompilerParams(vmem_limit_bytes=vmem_bytes),
        cost_estimate=cost(6),
        name="input_grads",
    )(flipped, matrix, inputs, *weights, gains, *grads, *mids, *after)


def front_grad_kernel(heads, parts, half, which, *refs):
    flipped_ref = refs[0]
    lefts, grads = refs[1 : 1 + parts], refs[1 + parts : 1 + 2 * parts]
    out_ref, tall_ref, lined_ref = refs[-3:]
    tok = grads[0].shape[2]
    inner_width = out_ref.shape[1] // 3
    lined(grads, heads, inner_width // heads, lined_ref)
    lanes = side(flipped_ref[0], half)[which]
    for p, ref in enumerate(lefts):
        tall = ref[:, lanes].astype(f32).T.astype(bf16)
        tall_ref[:, p * tok : (p + 1) * tok] = tall
    for k in range(3):
        spot = slice(k * inner_width, (k + 1) * inner_width)
        out_ref[:, spot] = dot_on(tall_ref[...], lined_ref[spot, :], 1, 1).astype(bf16)


def front_grads(flipped, lefts, grads, inner_width, heads, which):
    tok, width = lefts[0].shape
    parts = len(lefts)
    vmem = pl.BlockSpec(memory_space=pltpu.VMEM)
    return pl.pallas_call(
        functools.partial(front_grad_kernel, heads, parts, width // 2, which),
        in_specs=[pl.BlockSpec(memory_space=pltpu.SMEM)] + [vmem] * (2 * parts),
        out_shape=jax.ShapeDtypeStruct((width // 2, 3 * inner_width), bf16),
        scratch_shapes=[
            pltpu.VMEM((width // 2, parts * tok), bf16),
            pltpu.VMEM((3 * inner_width, parts * tok), bf16),
        ],
        compiler_params=pltpu.CompilerParams(vmem_limit_bytes=vmem_bytes),
        cost_estimate=cost(5),
        name="front_grads",
    )(flipped, *lefts, *grads)


def row_of(column):
    share = column.shape[0]
    shape = (share, share)
    spread = lax.broadcasted_iota(jnp.int32, shape, 0) == lax.broadcasted_iota(jnp.int32, shape, 1)
    return jnp.sum(jnp.where(spread, column, 0.0), axis=0, keepdims=True)


def gain_grad_of(weights, grads, gain_ref):
    total = sum(
        jnp.sum(weight[...].astype(f32) * grad[...], axis=1, keepdims=True)
        for weight, grad in zip(weights, grads)
    )
    return row_of(total) / gain_ref[...].astype(f32)


def unpack_back_kernel(sums_ref, gate_ref, up_ref, gain_ref, *refs):
    gate_grad_ref, up_grad_ref, down_grad_ref, out_grad_ref, gain_grad_ref = refs
    units = gate_ref.shape[1]
    for k, ref in enumerate((gate_grad_ref, up_grad_ref, down_grad_ref, out_grad_ref)):
        ref[...] = sums_ref[:, k * units : k * units + ref.shape[1]].astype(f32)
    gain_grad_ref[...] = gain_grad_of((gate_ref, up_ref), (gate_grad_ref, up_grad_ref), gain_ref)


def unpack_back(sums, w_gate, w_up, gain, inner_width):
    share, units = w_gate.shape
    shapes = [(share, units)] * 3 + [(share, inner_width), (1, share)]
    gate, up, down, out, gain_grad = pl.pallas_call(
        unpack_back_kernel,
        out_shape=[jax.ShapeDtypeStruct(shape, f32) for shape in shapes],
        compiler_params=pltpu.CompilerParams(vmem_limit_bytes=vmem_bytes),
        name="unpack_back",
    )(sums, w_gate, w_up, gain[None, :])
    return gate, up, down.T, out.T, gain_grad[0]


def unpack_front_kernel(parts_ref, query_ref, key_ref, value_ref, gain_ref, after_ref, *refs):
    grads, gain_grad_ref = refs[:3], refs[3]
    width = query_ref.shape[1]
    for k, ref in enumerate(grads):
        part = parts_ref[:, :, k * width : (k + 1) * width].astype(f32)
        ref[...] = jnp.sum(part, axis=0)
    gain_grad_ref[...] = gain_grad_of((query_ref, key_ref, value_ref), grads, gain_ref)


def unpack_front(parts, w_query, w_key, w_value, gain, after):
    share, width = w_query.shape
    vmem = pl.BlockSpec(memory_space=pltpu.VMEM)
    shapes = [(share, width)] * 3 + [(1, share)]
    query, key, value, gain_grad = pl.pallas_call(
        unpack_front_kernel,
        in_specs=[vmem] * 5 + [pl.BlockSpec(memory_space=pl.ANY)],
        out_shape=[jax.ShapeDtypeStruct(shape, f32) for shape in shapes],
        compiler_params=pltpu.CompilerParams(vmem_limit_bytes=vmem_bytes),
        name="unpack_front",
    )(parts, w_query, w_key, w_value, gain[None, :], after)
    return query, key, value, gain_grad[0]


def body(
    inputs, doc_lengths, attn_gain, w_query, w_key, w_value, w_out, ff_gain,
    w_gate, w_up, w_down, rel_table, cotangent,
):
    micro, _, tok, width = inputs.shape
    inner_width = w_query.shape[1]
    hidden_units = w_gate.shape[1]
    buckets, heads = rel_table.shape
    size = inner_width // heads
    blocks = lax.axis_size("blk")
    rows = lax.axis_size("rows")
    me = lax.axis_index("blk")
    share = w_query.shape[0]
    micros = range(micro)

    flipped = lax.axis_index("rows") if staged(rows, blocks, share) else 0
    flipped = jnp.full((1,), flipped, jnp.int32)
    matrix = stage_matrix(rows, blocks, share)
    head = jnp.minimum(me, heads - 1).astype(jnp.int32).reshape(1)
    table = rel_table.astype(f32).reshape(-1)

    with jax.named_scope("weights"):
        front_full = gather_front(w_query, w_key, w_value, attn_gain, ff_gain)
        back_own = gather_back(jnp.concatenate([w_out.T, w_gate, w_up, w_down.T], axis=1), front_full[0])

    band = bias_tiles(head, table, buckets)
    sent, tokens, normed_a, gain_a, gain_f = project(
        flipped, matrix, inputs[:, 0], front_full, heads, blocks, band
    )
    taken = []
    for m in micros:
        with jax.named_scope("project"):
            part = tie(sent[m], taken[-1]) if m else sent[m]
            taken.append(lax.all_to_all(part, "blk", 0, 0, tiled=True))

    kept, contexts = [], []
    for m in micros:
        part, *rest = attend(
            taken[m], doc_lengths[m, 0], head, table, band, buckets, *[k[0] for k in kept]
        )
        kept.append(rest)
        with jax.named_scope("context"):
            contexts.append(lax.all_to_all(part, "blk", 0, 0, tiled=True))
    with jax.named_scope("weights"):
        back_full = gather_other(back_own, part)

    fed, grads, packets = [], [], []
    fits = staged(rows, blocks, share)
    for m in micros:
        outs = list(
            feed(
                flipped, matrix, tokens[m], contexts[m], cotangent[m, 0], gain_f, back_full, heads,
            )
        )
        with jax.named_scope("grad_context"):
            part = tie(outs[2], *grads) if m else outs[2]
            grads.append(lax.all_to_all(part, "blk", 0, 0, tiled=True))
        if fits:
            with jax.named_scope("packet"):
                outs[3] = tie(outs[3], grads[0]) if m else outs[3]
                packets.append(flip(outs[3], "rows", 1))
        fed.append(outs)
    result, grad_mid, _, mine, left = zip(*fed)

    wide = blocks * size
    with jax.named_scope("back_grads"):
        sizes = width // 2, hidden_units, wide
        if fits:
            own = weight_grads([*left, *packets], [*mine, *packets], *sizes)
            back_grad = scatter_back(own)
        else:
            own, other = (weight_grads(lefts, mine, *sizes) for lefts in (left, mine))
            back_grad = scatter_whole(own, other)
    grad_qkv = []
    for m in micros:
        returned = attend_back(taken[m], grads[m], *kept[m], buckets, own)
        with jax.named_scope("grad_qkv"):
            returned = tie(returned, *grad_qkv) if m else returned
            grad_qkv.append(lax.all_to_all(returned, "blk", 0, 0, tiled=True))

    with jax.named_scope("table"):
        sums = sum(
            jnp.sum(g[:heads, 3 * size : 3 * size + 3, :buckets].astype(f32), axis=1)
            for g in grad_qkv
        )
        table_grad = sums.T
        for bit in bits_of(rows):
            table_grad = table_grad + flip(table_grad, "rows", bit)

    with jax.named_scope("front_grads"):
        normed = [normed_a[m * tok : (m + 1) * tok] for m in micros]
        if fits:
            near_grads = [flip(g, "rows", 1) for g in grad_qkv]
            near_normed = [flip(n, "rows", 1) for n in normed]
            own = front_grads(
                flipped, normed + near_normed, grad_qkv + near_grads, inner_width, heads, 0
            )
            back_grad = scatter_back_end(back_grad, own)
            front_parts = scatter_front(own, share)
        else:
            own, other = (
                front_grads(flipped, normed, grad_qkv, inner_width, heads, which)
                for which in (0, 1)
            )
            front_parts = scatter_whole(own, other)[None]
    input_grad = input_grads(
        flipped, matrix, tokens, front_full, gain_a, grad_qkv, grad_mid, heads, own
    )
    if fits:
        with jax.named_scope("front_grads"):
            front_parts = scatter_front_end(front_parts, share, input_grad)
    gate_grad, up_grad, down_grad, out_grad, ff_gain_grad = unpack_back(
        back_grad, w_gate, w_up, ff_gain, inner_width
    )
    query_grad, key_grad, value_grad, attn_gain_grad = unpack_front(
        front_parts, w_query, w_key, w_value, attn_gain, gate_grad
    )

    return (
        jnp.stack(result).reshape(micro, 1, tok, width),
        input_grad[:, None],
        attn_gain_grad,
        query_grad,
        key_grad,
        value_grad,
        out_grad,
        ff_gain_grad,
        gate_grad,
        up_grad,
        down_grad,
        table_grad,
    )


def solution(mesh):
    weight_rows = P(both, None)
    weight_columns = P(None, both)
    tokens = P(None, "rows", "blk", None)
    in_specs = (
        tokens, P(None, "rows", None), P(both), weight_rows, weight_rows, weight_rows,
        weight_columns, P(both), weight_rows, weight_rows, weight_columns, P(), tokens,
    )
    out_specs = (
        tokens, tokens, P(both), weight_rows, weight_rows, weight_rows,
        weight_columns, P(both), weight_rows, weight_rows, weight_columns, P(),
    )
    return jax.shard_map(body, mesh=mesh, in_specs=in_specs, out_specs=out_specs, check_vma=False)
```

time: 415 us -> 347 us (0.84)
  Pallas kernels: 47.7 us -> 123 us
  other arithmetic: 53.2 us -> 5.81 us
  local copies, waits for them, and re-layouts: 47.9 us -> 12.7 us
  matrix products: 33.4 us -> 0 us
  blocking collectives: 49 us -> 26.2 us
    pallas_call x2 -> x22, Pallas kernels: 47.7 us -> 123 us  [the longest x2 28.9 us: attend_back(): pl.pallas_call(functools.partial(attend_back_kernel, size, blocks, bucket...]
    ppermute x20 -> x9, waiting for transfers between devices: 69.3 us -> 7.9 us  [flip(): return lax.ppermute(array, axis, [(i, i ^ bit) for i in range(count)])]
    psum x1 -> x0, blocking collectives: 49 us -> none  [body(): table_grad = lax.psum(jnp.where(mine, jnp.stack(sums)[:, None], 0.0), both)]
    all_to_all x4 -> x11, waiting for transfers between devices: 35.2 us -> 74.8 us  [the longest x4 34.4 us: exchange(): lax.all_to_all(array, 'blk', 0, 0, tiled=True, axis_index_groups=groups)]
    dot_general x15 -> x0, matrix products: 33.4 us -> none  [the longest x12 23.4 us: dot_on(): lax.dot_general(left, right, (((left_dim,), (right_dim,)), ((), ())), pre...]
    select_n x22 -> x0, other arithmetic: 29.9 us -> none  [the longest x1 23.7 us: body(): band = jnp.where(bucket == b, column[b], band)]
    all_to_all x0 -> x1, blocking collectives: none -> 26.2 us  [body(): taken.append(lax.all_to_all(part, 'blk', 0, 0, tiled=True))]
    all_gather x1 -> x2, waiting for transfers between devices: 0.02 us -> 21.4 us  [the longest x1 19.1 us: gather_back(): lax.all_gather(shard, 'blk', axis=0, tiled=True, axis_index_groups=across)]
  transfers between devices with their start and end apart: 26 -> 24, of which waited for: 19 -> 15; matrix products, arithmetic and copies ran while one was open for 25% -> 3% of each run, Pallas kernels for 12% -> 31%
where the time goes in v2:
time: 347 us; the launch traced here: 344 us
  Pallas kernels  123 us (35%)
  waiting for transfers between devices  104 us (30%)
  starting transfers between devices  58.4 us (17%)
  blocking collectives  26.2 us (8%)
  between operations  14.1 us (4%)
  local copies, waits for them, and re-layouts  12.7 us (4%)
  other arithmetic  5.81 us (2%)
    all_to_all x4, waiting for transfers between devices, exchange(): lax.all_to_all(array, 'blk', 0, 0, tiled=True, axis_index_groups=groups)  34.4 us
    pallas_call x2, Pallas kernels, attend_back(): pl.pallas_call(functools.partial(attend_back_kernel, size, blocks, bucket...  28.9 us
    pallas_call x2, Pallas kernels, feed(): pl.pallas_call(functools.partial(feed_kernel, heads, steps), grid=(steps,...  28.1 us
    all_to_all x1, blocking collectives, body(): taken.append(lax.all_to_all(part, 'blk', 0, 0, tiled=True))  26.2 us
    all_to_all x2, waiting for transfers between devices, body(): grad_qkv.append(lax.all_to_all(returned, 'blk', 0, 0, tiled=True))  25.3 us
    pallas_call x2, Pallas kernels, attend(): pl.pallas_call(functools.partial(attend_kernel, size, blocks, lengths.sha...  24.6 us
    all_gather x1, waiting for transfers between devices, gather_back(): lax.all_gather(shard, 'blk', axis=0, tiled=True, axis_index_groups=across)  19.1 us
    all_to_all x4, starting transfers between devices, exchange(): lax.all_to_all(array, 'blk', 0, 0, tiled=True, axis_index_groups=groups)  17.8 us
  transfers between devices with their start and end apart: 24, of which 15 were waited for; matrix products, arithmetic and copies ran while one was open for 3% of the time, Pallas kernels for 31%

profile of v2, /device:TPU:0, one launch (start us, length us, event | category | flops | bytes accessed | tf_op | source)
XLA Modules:
  0.0 344.3 jit_solution(4232217479442410246)
XLA Ops:
  7.2 1.7 pack.1
  8.9 6.3 %all-to-all-start = ((bf16[4,24,2432]{2,1,0:T(8,128)(2,1)}), bf16[4,24,2432]{2,1,0:T(8,128)(2,1)S(1)}, u32[]{:S(2)}, u32[]{:S(2)}) async-start(bf16[4,24,2432]{2,1,0:T(8,128)(2,1)} %pack.1), calls=%async_computation | async-start | bytes 933888 | tf_op jit(solution)/shard_map/weights/all_to_all | solution.py:99
  15.2 1.7 pad_maximum_fusion
  16.9 11.5 %all-to-all-done = bf16[4,24,2432]{2,1,0:T(8,128)(2,1)S(1)} async-done(((bf16[4,24,2432]{2,1,0:T(8,128)(2,1)}), bf16[4,24,2432]{2,1,0:T(8,128)(2,1)S(1)}, u32[]{:S(2)}, u32[]{:S(2)}) %all-to-all-start) | async-done | bytes 466976 | tf_op jit(solution)/shard_map/weights/all_to_all | solution.py:99
  28.4 1.4 tile.10
  29.8 3.7 %all-to-all-start.1 = ((bf16[4,96,2432]{2,1,0:T(8,128)(2,1)}), bf16[4,96,2432]{2,1,0:T(8,128)(2,1)S(1)}, u32[]{:S(2)}, u32[]{:S(2)}) async-start(bf16[4,96,2432]{2,1,0:T(8,128)(2,1)} %tile.10), calls=%async_computation.1 | async-start | bytes 3735552 | tf_op jit(solution)/shard_map/weights/all_to_all | solution.py:99
  33.5 19.1 %all-gather.3.cloned.1.call-done.refs_0_ = bf16[96,6912]{1,0:T(8,128)(2,1)} async-done(((bf16[24,6912]{1,0:T(8,128)(2,1)}), bf16[96,6912]{1,0:T(8,128)(2,1)}) %all-gather.3.cloned.1.call-update) | async-done | bytes 1327120 | tf_op jit(solution)/shard_map/weights/all_gather | solution.py:150
  52.6 2.7 all-to-all-done.1
  55.3 1.2 copy-done
  56.6 0.6 copy-done.16
  57.3 0.7 reshape.60.table_ref
  58.0 1.9 bias_tiles.1.after_ref.band_ref
  59.9 0.9 collective-permute-done.other_ref.refs_4_
  60.8 7.0 %project.1 = (bf16[16,192,128]{2,1,0:T(8,128)(2,1)}, bf16[16,192,128]{2,1,0:T(8,128)(2,1)}, bf16[2,128,768]{2,1,0:T(8,128)(2,1)}, bf16[256,768]{1,0:T(8,128)(2,1)}, f32[1,768]{1,0:T(1,128)}, /*index=5*/f32[1,768]{1,0:T(1,128)}) custom-call(s32[1]{0:T(128)} %bitcast.flipped_ref.refs_0_, bf16[768,768]{1,0:T(8,128)(2,1)} %constant.17.clone.matrix_ref.refs_1_, ...), custom_call_target="tpu_custom_call" | custom-call | flops 3000000000 | tf_op jit(solution)/shard_map/project/pallas_call | solution.py:741
  67.8 26.2 %all_to_all.72.taken_ref.refs_1_ = bf16[16,192,128]{2,1,0:T(8,128)(2,1)} all-to-all(bf16[16,192,128]{2,1,0:T(8,128)(2,1)} %get-tuple-element.46), channel_id=1, replica_groups=mesh['rows'=2,'blk'=16] {'blk'}, dimensions={0} | all-to-all | bytes 1572864 | tf_op jit(solution)/shard_map/project/all_to_all | solution.py:951
  94.0 3.7 %all-to-all-start.4 = ((bf16[16,192,128]{2,1,0:T(8,128)(2,1)}), bf16[16,192,128]{2,1,0:T(8,128)(2,1)S(1)}, u32[]{:S(2)}, u32[]{:S(2)}) async-start(bf16[16,192,128]{2,1,0:T(8,128)(2,1)} %tie.9), calls=%async_computation.4 | async-start | bytes 1572864 | tf_op jit(solution)/shard_map/project/all_to_all | solution.py:951
  97.7 0.5 slice_bitcast_fusion.5
  98.2 12.3 %attend.2 = (bf16[16,64,128]{2,1,0:T(8,128)(2,1)}, f32[64,2048]{1,0:T(8,128)}, bf16[2048,2048]{1,0:T(8,128)(2,1)}, f32[1,2048]{1,0:T(1,128)}) custom-call(s32[6]{0:T(128)} %get-tuple-element.108.bounds_ref, s32[1]{0:T(128)} %bitcast.6.head_ref, f32[384]{0:T(512)} %reshape.60.table_ref, bf16[16,192,128]{2,1,0:T(8,128)(2,1)} %all_to_all.72.taken_ref.refs_1_, ...), custom_call_target="tpu_custom_call" | custom-call | flops 11000000512 | tf_op jit(solution)/shard_map/attend/pallas_call | solution.py:382
  110.5 6.2 %all-to-all-done.4.taken_ref = bf16[16,192,128]{2,1,0:T(8,128)(2,1)S(1)} async-done(((bf16[16,192,128]{2,1,0:T(8,128)(2,1)}), bf16[16,192,128]{2,1,0:T(8,128)(2,1)S(1)}, u32[]{:S(2)}, u32[]{:S(2)}) %all-to-all-start.4) | async-done | bytes 786464 | tf_op jit(solution)/shard_map/project/all_to_all | solution.py:951
  116.7 0.9 copy-done.7
  117.6 12.3 %attend.3 = (bf16[16,64,128]{2,1,0:T(8,128)(2,1)}, f32[64,2048]{1,0:T(8,128)}, bf16[2048,2048]{1,0:T(8,128)(2,1)}, f32[1,2048]{1,0:T(1,128)}) custom-call(s32[6]{0:T(128)} %get-tuple-element.109.bounds_ref, s32[1]{0:T(128)} %bitcast.6.head_ref, f32[384]{0:T(512)} %reshape.60.table_ref, bf16[16,192,128]{2,1,0:T(8,128)(2,1)} %copy-done.7, ...), custom_call_target="tpu_custom_call" | custom-call | flops 11000000512 | tf_op jit(solution)/shard_map/attend/pallas_call | solution.py:382
  129.9 2.3 all-gather.5.cloned.1.call-done.refs_0_
  132.3 5.8 %all-to-all-start.3 = ((bf16[16,64,128]{2,1,0:T(8,128)(2,1)}), bf16[16,64,128]{2,1,0:T(8,128)(2,1)S(1)}, u32[]{:S(2)}, u32[]{:S(2)}) async-start(bf16[16,64,128]{2,1,0:T(8,128)(2,1)} %get-tuple-element.47), calls=%async_computation.3 | async-start | bytes 524288 | tf_op jit(solution)/shard_map/context/all_to_all | solution.py:960
  138.1 0.8 slice_bitcast_fusion.2
  138.8 0.8 slice_bitcast_fusion.3
  139.6 8.8 %all-to-all-done.3.context_ref = bf16[16,64,128]{2,1,0:T(8,128)(2,1)S(1)} async-done(((bf16[16,64,128]{2,1,0:T(8,128)(2,1)}), bf16[16,64,128]{2,1,0:T(8,128)(2,1)S(1)}, u32[]{:S(2)}, u32[]{:S(2)}) %all-to-all-start.3) | async-done | bytes 262176 | tf_op jit(solution)/shard_map/context/all_to_all | solution.py:960
  148.4 3.5 %all-to-all-start.5 = ((bf16[16,64,128]{2,1,0:T(8,128)(2,1)}), bf16[16,64,128]{2,1,0:T(8,128)(2,1)S(1)}, u32[]{:S(2)}, u32[]{:S(2)}) async-start(bf16[16,64,128]{2,1,0:T(8,128)(2,1)} %get-tuple-element.51.refs_1_), calls=%async_computation.5 | async-start | bytes 524288 | tf_op jit(solution)/shard_map/context/all_to_all | solution.py:960
  152.0 14.1 %feed.2 = (bf16[128,768]{1,0:T(8,128)(2,1)}, f32[128,768]{1,0:T(8,128)}, bf16[16,64,128]{2,1,0:T(8,128)(2,1)}, bf16[128,8704]{1,0:T(8,128)(2,1)}, bf16[128,1152]{1,0:T(8,128)(2,1)}) custom-call(s32[1]{0:T(128)} %bitcast.flipped_ref.refs_0_, bf16[768,768]{1,0:T(8,128)(2,1)} %constant.17.clone.matrix_ref.refs_1_, ...), custom_call_target="tpu_custom_call" | custom-call | flops 8000000000 | tf_op jit(solution)/shard_map/feed/pallas_call | solution.py:619
  166.2 6.9 %all-to-all-start.6 = ((bf16[16,64,128]{2,1,0:T(8,128)(2,1)}), bf16[16,64,128]{2,1,0:T(8,128)(2,1)S(1)}, u32[]{:S(2)}, u32[]{:S(2)}) async-start(bf16[16,64,128]{2,1,0:T(8,128)(2,1)} %get-tuple-element.55), calls=%async_computation.6 | async-start | bytes 524288 | tf_op jit(solution)/shard_map/grad_context/all_to_all | solution.py:974
  173.3 14.0 %feed.3 = (bf16[128,768]{1,0:T(8,128)(2,1)}, f32[128,768]{1,0:T(8,128)}, bf16[16,64,128]{2,1,0:T(8,128)(2,1)}, bf16[128,8704]{1,0:T(8,128)(2,1)}, bf16[128,1152]{1,0:T(8,128)(2,1)}) custom-call(s32[1]{0:T(128)} %bitcast.flipped_ref.refs_0_, bf16[768,768]{1,0:T(8,128)(2,1)} %constant.17.clone.matrix_ref.refs_1_, ...), custom_call_target="tpu_custom_call" | custom-call | flops 8000000000 | tf_op jit(solution)/shard_map/feed/pallas_call | solution.py:619
  187.3 0.7 copy-done.2
  188.2 4.4 %collective-permute-done.3.refs_3_.refs_7_ = bf16[128,8704]{1,0:T(8,128)(2,1)S(1)} collective-permute-done((bf16[128,8704]{1,0:T(8,128)(2,1)}, bf16[128,8704]{1,0:T(8,128)(2,1)S(1)}, u32[]{:S(2)}, u32[]{:S(2)}) %collective-permute-start.3) | collective-permute-done | bytes 2228256 | tf_op jit(solution)/shard_map/packet/ppermute | solution.py:45
  192.6 1.4 copy-done.19
  194.0 13.3 %weight_grads.1.refs_0_ = bf16[384,7168]{1,0:T(8,128)(2,1)} custom-call(bf16[128,1152]{1,0:T(8,128)(2,1)} %get-tuple-element.58.refs_0_, bf16[128,1152]{1,0:T(8,128)(2,1)} %get-tuple-element.59.refs_1_, bf16[128,8704]{1,0:T(8,128)(2,1)} %copy-done.18, bf16[128,8704]{1,0:T(8,128)(2,1)} %copy-done.19, bf16[128,8704]{1,0:T(8,128)(2,1)} %get-tuple-element.60.refs_4_, ...), custom_call_target="tpu_custom_call" | custom-call | flops 10000000000 | tf_op jit(solution)/shard_map/back_grads/weight_grads/pallas_call | solution.py:682
  207.4 6.9 %all-to-all-start.8 = ((bf16[16,64,128]{2,1,0:T(8,128)(2,1)}), bf16[16,64,128]{2,1,0:T(8,128)(2,1)S(1)}, u32[]{:S(2)}, u32[]{:S(2)}) async-start(bf16[16,64,128]{2,1,0:T(8,128)(2,1)} %tie.12), calls=%async_computation.8 | async-start | bytes 524288 | tf_op jit(solution)/shard_map/grad_context/all_to_all | solution.py:974
  214.3 14.8 %attend_back.2 = bf16[16,208,128]{2,1,0:T(8,128)(2,1)} custom-call(bf16[16,192,128]{2,1,0:T(8,128)(2,1)} %all_to_all.72.taken_ref.refs_1_, bf16[16,64,128]{2,1,0:T(8,128)(2,1)} %copy-done.2, f32[64,2048]{1,0:T(8,128)} %get-tuple-element.50.refs_0_.context_ref, bf16[2048,2048]{1,0:T(8,128)(2,1)} %get-tuple-element.56.expo_ref, ...), custom_call_target="tpu_custom_call" | custom-call | flops 12999999488 | tf_op jit(solution)/shard_map/attend_back/pallas_call | solution.py:490
  229.1 6.9 %all-to-all-start.7 = ((bf16[16,208,128]{2,1,0:T(8,128)(2,1)}), bf16[16,208,128]{2,1,0:T(8,128)(2,1)S(1)}, u32[]{:S(2)}, u32[]{:S(2)}) async-start(bf16[16,208,128]{2,1,0:T(8,128)(2,1)} %attend_back.2), calls=%async_computation.7 | async-start | bytes 1703936 | tf_op jit(solution)/shard_map/grad_qkv/all_to_all | solution.py:996
  236.0 14.2 %attend_back.3.refs_0_ = bf16[16,208,128]{2,1,0:T(8,128)(2,1)} custom-call(bf16[16,192,128]{2,1,0:T(8,128)(2,1)} %copy-done.7, bf16[16,64,128]{2,1,0:T(8,128)(2,1)} %copy-done.11, f32[64,2048]{1,0:T(8,128)} %get-tuple-element.63.context_ref, bf16[2048,2048]{1,0:T(8,128)(2,1)} %get-tuple-element.64.expo_ref, f32[1,2048]{1,0:T(1,128)} %get-tuple-element.65.scale_ref, ...), custom_call_target="tpu_custom_call" | custom-call | flops 12999999488 | tf_op jit(solution)/shard_map/attend_back/pallas_call | solution.py:490
  250.2 5.8 %all-to-all-done.7.refs_1_.refs_5_.refs_6_ = bf16[16,208,128]{2,1,0:T(8,128)(2,1)S(1)} async-done(((bf16[16,208,128]{2,1,0:T(8,128)(2,1)}), bf16[16,208,128]{2,1,0:T(8,128)(2,1)S(1)}, u32[]{:S(2)}, u32[]{:S(2)}) %all-to-all-start.7) | async-done | bytes 852000 | tf_op jit(solution)/shard_map/grad_qkv/all_to_all | solution.py:996
  256.0 0.9 copy-done.1
  256.9 5.4 %all-to-all-start.9 = ((bf16[16,208,128]{2,1,0:T(8,128)(2,1)}), bf16[16,208,128]{2,1,0:T(8,128)(2,1)S(1)}, u32[]{:S(2)}, u32[]{:S(2)}) async-start(bf16[16,208,128]{2,1,0:T(8,128)(2,1)} %tie.13), calls=%async_computation.9 | async-start | bytes 1703936 | tf_op jit(solution)/shard_map/grad_qkv/all_to_all | solution.py:996
  262.5 19.4 %all-to-all-done.9.refs_6_.refs_7_ = bf16[16,208,128]{2,1,0:T(8,128)(2,1)S(1)} async-done(((bf16[16,208,128]{2,1,0:T(8,128)(2,1)}), bf16[16,208,128]{2,1,0:T(8,128)(2,1)S(1)}, u32[]{:S(2)}, u32[]{:S(2)}) %all-to-all-start.9) | async-done | bytes 852000 | tf_op jit(solution)/shard_map/grad_qkv/all_to_all | solution.py:996
  282.0 0.6 collective-permute-start.4
  282.6 1.9 collective-permute-done.4.refs_3_
  284.6 0.3 collective-permute-done.5.refs_4_
  284.9 0.4 copy-done.22
  285.2 0.3 copy-done.23
  285.5 0.3 copy-done.20
  285.8 0.9 copy-done.21
  286.7 4.7 %front_grads.1.refs_10_.refs_1_ = bf16[384,2304]{1,0:T(8,128)(2,1)} custom-call(s32[1]{0:T(128)} %bitcast.flipped_ref.refs_0_, bf16[128,768]{1,0:T(8,128)(2,1)} %copy-done.15, bf16[128,768]{1,0:T(8,128)(2,1)} %copy-done.14, bf16[128,768]{1,0:T(8,128)(2,1)} %copy-done.22, bf16[128,768]{1,0:T(8,128)(2,1)} %copy-done.23, bf16[16,208,128]{2,1,0:T(8,128)(2,1)} %copy-done.1, ...), custom_call_target="tpu_custom_call" | custom-call | flops 5000000000 | tf_op jit(solution)/shard_map/front_grads/front_grads/pallas_call | solution.py:846
  291.5 3.8 %all-to-all-start.10 = ((bf16[4,96,2304]{2,1,0:T(8,128)(2,1)}), bf16[4,96,2304]{2,1,0:T(8,128)(2,1)S(1)}, u32[]{:S(2)}, u32[]{:S(2)}) async-start(bf16[4,96,2304]{2,1,0:T(8,128)(2,1)} %bitcast.21), calls=%async_computation.10 | async-start | bytes 3538944 | tf_op jit(solution)/shard_map/front_grads/all_to_all | solution.py:99
  295.3 9.2 %input_grads.1.refs_1_ = f32[2,128,768]{2,1,0:T(8,128)} custom-call(s32[1]{0:T(128)} %bitcast.flipped_ref.refs_0_, bf16[768,768]{1,0:T(8,128)(2,1)} %constant.17.clone.matrix_ref.refs_1_, bf16[2,128,768]{2,1,0:T(8,128)(2,1)} %get-tuple-element.45.refs_2_, bf16[384,2432]{1,0:T(8,128)(2,1)} %bitcast.41, ...), custom_call_target="tpu_custom_call" | custom-call | flops 6000000000 | tf_op jit(solution)/shard_map/input_grads/pallas_call | solution.py:810
  304.4 12.7 %all-to-all-done.10 = bf16[4,96,2304]{2,1,0:T(8,128)(2,1)S(1)} async-done(((bf16[4,96,2304]{2,1,0:T(8,128)(2,1)}), bf16[4,96,2304]{2,1,0:T(8,128)(2,1)S(1)}, u32[]{:S(2)}, u32[]{:S(2)}) %all-to-all-start.10) | async-done | bytes 1769504 | tf_op jit(solution)/shard_map/front_grads/all_to_all | solution.py:99
  317.2 1.2 reduce_sum.30.refs_0_
  318.4 4.0 %all-to-all-start.11 = ((bf16[4,24,2304]{2,1,0:T(8,128)(2,1)}), bf16[4,24,2304]{2,1,0:T(8,128)(2,1)S(1)}, u32[]{:S(2)}, u32[]{:S(2)}) async-start(bf16[4,24,2304]{2,1,0:T(8,128)(2,1)} %bitcast.42), calls=%async_computation.11 | async-start | bytes 884736 | tf_op jit(solution)/shard_map/front_grads/all_to_all | solution.py:99
  322.3 0.8 convert_reduce_fusion.1
  323.1 0.8 convert_reduce_fusion
  324.0 0.8 maximum_bitcast_fusion
  324.8 0.4 collective-permute-done.8
  325.1 0.6 add.16
  325.7 1.9 unpack_back.1
  327.6 7.5 %all-to-all-done.11.parts_ref = bf16[4,24,2304]{2,1,0:T(8,128)(2,1)S(1)} async-done(((bf16[4,24,2304]{2,1,0:T(8,128)(2,1)}), bf16[4,24,2304]{2,1,0:T(8,128)(2,1)S(1)}, u32[]{:S(2)}, u32[]{:S(2)}) %all-to-all-start.11) | async-done | bytes 442400 | tf_op jit(solution)/shard_map/front_grads/all_to_all | solution.py:99
  335.2 0.8 copy-done.3
  335.9 1.8 unpack_front.1
  (73 shorter events, 1.1 us)
Async XLA Ops:
  8.9 19.6 %all-to-all-start = ((bf16[4,24,2432]{2,1,0:T(8,128)(2,1)}), bf16[4,24,2432]{2,1,0:T(8,128)(2,1)S(1)}, u32[]{:S(2)}, u32[]{:S(2)}) async-start(bf16[4,24,2432]{2,1,0:T(8,128)(2,1)} %pack.1), calls=%async_computation | async-start | bytes 933888 | tf_op jit(solution)/shard_map/weights/all_to_all | solution.py:99
  15.2 37.4 %all-gather.3.cloned.1.call-start = ((), (), s32[]{:S(2)}) async-start(), calls=%async_computation.14 | async-start | bytes 1658880 | tf_op jit(solution)/shard_map/weights/all_gather | solution.py:150
  29.8 25.5 %all-to-all-start.1 = ((bf16[4,96,2432]{2,1,0:T(8,128)(2,1)}), bf16[4,96,2432]{2,1,0:T(8,128)(2,1)S(1)}, u32[]{:S(2)}, u32[]{:S(2)}) async-start(bf16[4,96,2432]{2,1,0:T(8,128)(2,1)} %tile.10), calls=%async_computation.1 | async-start | bytes 3735552 | tf_op jit(solution)/shard_map/weights/all_to_all | solution.py:99
  33.5 98.7 %all-gather.5.cloned.1.call-start = ((), (), s32[]{:S(2)}) async-start(), calls=%async_computation.15 | async-start | bytes 6635520 | tf_op jit(solution)/shard_map/weights/all_gather | solution.py:152
  55.3 1.2 copy-start
  56.5 0.7 copy-start.16
  56.6 4.2 %collective-permute-start = (bf16[384,2432]{1,0:T(8,128)(2,1)}, bf16[384,2432]{1,0:T(8,128)(2,1)}, u32[]{:S(2)}, u32[]{:S(2)}) collective-permute-start(bf16[384,2432]{1,0:T(8,128)(2,1)} %bitcast.39), channel_id=1, source_target_pairs={{0,16},{16,0},{1,17},{17,1},{2,18},{18,2},{3,19},{19,3},{4,20},{20... | collective-permute-start | bytes 5603336 | tf_op jit(solution)/shard_map/weights/ppermute | solution.py:45
  94.0 3.8 %copy-start.17 = (s32[2,1,6]{2,1,0:T(1,128)S(1)}, s32[2,1,6]{2,1,0:T(1,128)}, u32[]{:S(2)}) copy-start(s32[2,1,6]{2,1,0:T(1,128)} %param.15) | copy-start | bytes 148
  94.0 22.8 %all-to-all-start.4 = ((bf16[16,192,128]{2,1,0:T(8,128)(2,1)}), bf16[16,192,128]{2,1,0:T(8,128)(2,1)S(1)}, u32[]{:S(2)}, u32[]{:S(2)}) async-start(bf16[16,192,128]{2,1,0:T(8,128)(2,1)} %tie.9), calls=%async_computation.4 | async-start | bytes 1572864 | tf_op jit(solution)/shard_map/project/all_to_all | solution.py:951
  116.7 0.9 copy-start.7
  132.3 5.8 %copy-start.8 = (bf16[2,1,128,768]{3,2,1,0:T(8,128)(2,1)S(1)}, bf16[2,1,128,768]{3,2,1,0:T(8,128)(2,1)}, u32[]{:S(2)}) copy-start(bf16[2,1,128,768]{3,2,1,0:T(8,128)(2,1)} %param.26) | copy-start | bytes 1179652
  132.3 6.6 %copy-start.9 = (bf16[2,128,768]{2,1,0:T(8,128)(2,1)S(1)}, bf16[2,128,768]{2,1,0:T(8,128)(2,1)}, u32[]{:S(2)}) copy-start(bf16[2,128,768]{2,1,0:T(8,128)(2,1)} %get-tuple-element.45.refs_2_) | copy-start | bytes 1179652
  132.3 19.7 %collective-permute-start.1 = (bf16[384,6912]{1,0:T(8,128)(2,1)}, bf16[384,6912]{1,0:T(8,128)(2,1)}, u32[]{:S(2)}, u32[]{:S(2)}) collective-permute-start(bf16[384,6912]{1,0:T(8,128)(2,1)} %tie.10.refs_0_.refs_2_.refs_4_.refs_6_), channel_id=1, source_target_pairs={{0,16},{16,0},{1,17},{17,1},{2,18},{18,2},{3,19},{19,3},{4,20},{20... | collective-permute-start | bytes 15925256 | tf_op jit(solution)/shard_map/weights/ppermute | solution.py:45
  132.3 16.2 %all-to-all-start.3 = ((bf16[16,64,128]{2,1,0:T(8,128)(2,1)}), bf16[16,64,128]{2,1,0:T(8,128)(2,1)S(1)}, u32[]{:S(2)}, u32[]{:S(2)}) async-start(bf16[16,64,128]{2,1,0:T(8,128)(2,1)} %get-tuple-element.47), calls=%async_computation.3 | async-start | bytes 524288 | tf_op jit(solution)/shard_map/context/all_to_all | solution.py:960
  148.4 3.6 %copy-start.5 = (bf16[16,64,128]{2,1,0:T(8,128)(2,1)}, bf16[16,64,128]{2,1,0:T(8,128)(2,1)S(1)}, u32[]{:S(2)}) copy-start(bf16[16,64,128]{2,1,0:T(8,128)(2,1)S(1)} %all-to-all-done.3.context_ref) | copy-start | bytes 786436
  148.4 17.7 %all-to-all-start.5 = ((bf16[16,64,128]{2,1,0:T(8,128)(2,1)}), bf16[16,64,128]{2,1,0:T(8,128)(2,1)S(1)}, u32[]{:S(2)}, u32[]{:S(2)}) async-start(bf16[16,64,128]{2,1,0:T(8,128)(2,1)} %get-tuple-element.51.refs_1_), calls=%async_computation.5 | async-start | bytes 524288 | tf_op jit(solution)/shard_map/context/all_to_all | solution.py:960
  166.1 22.1 %collective-permute-start.2 = (bf16[128,8704]{1,0:T(8,128)(2,1)}, bf16[128,8704]{1,0:T(8,128)(2,1)S(1)}, u32[]{:S(2)}, u32[]{:S(2)}) collective-permute-start(bf16[128,8704]{1,0:T(8,128)(2,1)} %get-tuple-element.60.refs_4_), channel_id=1, source_target_pairs={{0,16},{16,0},{1,17},{17,1},{2,18},{18,2},{3,19},{19,3},{4,20},{20... | collective-permute-start | bytes 6684680 | tf_op jit(solution)/shard_map/packet/ppermute | solution.py:45
  166.2 7.2 %copy-start.4 = (bf16[16,64,128]{2,1,0:T(8,128)(2,1)}, bf16[16,64,128]{2,1,0:T(8,128)(2,1)S(1)}, u32[]{:S(2)}) copy-start(bf16[16,64,128]{2,1,0:T(8,128)(2,1)S(1)} %all-to-all-done.5.context_ref) | copy-start | bytes 786436
  166.2 21.1 %all-to-all-start.6 = ((bf16[16,64,128]{2,1,0:T(8,128)(2,1)}), bf16[16,64,128]{2,1,0:T(8,128)(2,1)S(1)}, u32[]{:S(2)}, u32[]{:S(2)}) async-start(bf16[16,64,128]{2,1,0:T(8,128)(2,1)} %get-tuple-element.55), calls=%async_computation.6 | async-start | bytes 524288 | tf_op jit(solution)/shard_map/grad_context/all_to_all | solution.py:974
  173.1 118.3 %reduce-scatter.3.cloned.1.call-start = ((), (), s32[]{:S(2)}) async-start(), calls=%async_computation.16 | async-start | bytes 6881280 | tf_op jit(solution)/shard_map/back_grads/reduce_scatter | solution.py:176
  187.3 0.7 copy-start.2
  188.0 4.6 %collective-permute-start.3 = (bf16[128,8704]{1,0:T(8,128)(2,1)}, bf16[128,8704]{1,0:T(8,128)(2,1)S(1)}, u32[]{:S(2)}, u32[]{:S(2)}) collective-permute-start(bf16[128,8704]{1,0:T(8,128)(2,1)} %tie.11.refs_5_), channel_id=1, source_target_pairs={{0,16},{16,0},{1,17},{17,1},{2,18},{18,2},{3,19},{19,3},{4,20},{20... | collective-permute-start | bytes 6684680 | tf_op jit(solution)/shard_map/packet/ppermute | solution.py:45
  188.2 4.4 %copy-start.18 = (bf16[128,8704]{1,0:T(8,128)(2,1)}, bf16[128,8704]{1,0:T(8,128)(2,1)S(1)}, u32[]{:S(2)}) copy-start(bf16[128,8704]{1,0:T(8,128)(2,1)S(1)} %collective-permute-done.2.refs_2_.refs_6_) | copy-start | bytes 6684676
  192.6 1.4 copy-start.19
  207.4 21.7 %all-to-all-start.8 = ((bf16[16,64,128]{2,1,0:T(8,128)(2,1)}), bf16[16,64,128]{2,1,0:T(8,128)(2,1)S(1)}, u32[]{:S(2)}, u32[]{:S(2)}) async-start(bf16[16,64,128]{2,1,0:T(8,128)(2,1)} %tie.12), calls=%async_computation.8 | async-start | bytes 524288 | tf_op jit(solution)/shard_map/grad_context/all_to_all | solution.py:974
  229.1 6.9 %copy-start.11 = (bf16[16,64,128]{2,1,0:T(8,128)(2,1)}, bf16[16,64,128]{2,1,0:T(8,128)(2,1)S(1)}, u32[]{:S(2)}) copy-start(bf16[16,64,128]{2,1,0:T(8,128)(2,1)S(1)} %all-to-all-done.8.grad_ref) | copy-start | bytes 786436
  229.1 27.0 %all-to-all-start.7 = ((bf16[16,208,128]{2,1,0:T(8,128)(2,1)}), bf16[16,208,128]{2,1,0:T(8,128)(2,1)S(1)}, u32[]{:S(2)}, u32[]{:S(2)}) async-start(bf16[16,208,128]{2,1,0:T(8,128)(2,1)} %attend_back.2), calls=%async_computation.7 | async-start | bytes 1703936 | tf_op jit(solution)/shard_map/grad_qkv/all_to_all | solution.py:996
  250.2 31.7 %copy-start.10 = (bf16[256,768]{1,0:T(8,128)(2,1)S(1)}, bf16[256,768]{1,0:T(8,128)(2,1)}, u32[]{:S(2)}) copy-start(bf16[256,768]{1,0:T(8,128)(2,1)} %get-tuple-element.68) | copy-start | bytes 1179652
  256.0 0.9 copy-start.1
  256.9 25.0 %all-to-all-start.9 = ((bf16[16,208,128]{2,1,0:T(8,128)(2,1)}), bf16[16,208,128]{2,1,0:T(8,128)(2,1)S(1)}, u32[]{:S(2)}, u32[]{:S(2)}) async-start(bf16[16,208,128]{2,1,0:T(8,128)(2,1)} %tie.13), calls=%async_computation.9 | async-start | bytes 1703936 | tf_op jit(solution)/shard_map/grad_qkv/all_to_all | solution.py:996
  262.3 63.4 %reduce-scatter.5.cloned.1.call-start = ((), (), s32[]{:S(2)}) async-start(), calls=%async_computation.17 | async-start | bytes 1720320 | tf_op jit(solution)/shard_map/front_grads/reduce_scatter | solution.py:183
  262.4 22.5 %collective-permute-start.6 = (bf16[16,208,128]{2,1,0:T(8,128)(2,1)}, bf16[16,208,128]{2,1,0:T(8,128)(2,1)S(1)}, u32[]{:S(2)}, u32[]{:S(2)}) collective-permute-start(bf16[16,208,128]{2,1,0:T(8,128)(2,1)} %copy-done.1), channel_id=1, source_target_pairs={{0,16},{16,0},{1,17},{17,1},{2,18},{18,2},{3,19},{19,3},{4,20},{20... | collective-permute-start | bytes 2555912 | tf_op jit(solution)/shard_map/front_grads/ppermute | solution.py:45
  281.9 3.0 copy-start.6
  281.9 3.0 collective-permute-start.7
  281.9 2.9 copy-start.14
  282.0 2.9 copy-start.15
  282.0 2.6 collective-permute-start.4
  282.5 2.3 collective-permute-start.5
  284.6 0.7 copy-start.22
  284.8 0.7 copy-start.23
  284.9 1.0 copy-start.20
  285.8 0.9 copy-start.21
  291.5 25.7 %all-to-all-start.10 = ((bf16[4,96,2304]{2,1,0:T(8,128)(2,1)}), bf16[4,96,2304]{2,1,0:T(8,128)(2,1)S(1)}, u32[]{:S(2)}, u32[]{:S(2)}) async-start(bf16[4,96,2304]{2,1,0:T(8,128)(2,1)} %bitcast.21), calls=%async_computation.10 | async-start | bytes 3538944 | tf_op jit(solution)/shard_map/front_grads/all_to_all | solution.py:99
  304.4 19.5 %copy-start.12 = (bf16[128,768]{1,0:T(8,128)(2,1)S(1)}, bf16[128,768]{1,0:T(8,128)(2,1)}, u32[]{:S(2)}) copy-start(bf16[128,768]{1,0:T(8,128)(2,1)} %get-tuple-element.52) | copy-start | bytes 589828
  304.4 19.5 %copy-start.13 = (bf16[128,768]{1,0:T(8,128)(2,1)S(1)}, bf16[128,768]{1,0:T(8,128)(2,1)}, u32[]{:S(2)}) copy-start(bf16[128,768]{1,0:T(8,128)(2,1)} %get-tuple-element.53) | copy-start | bytes 589828
  318.4 16.8 %all-to-all-start.11 = ((bf16[4,24,2304]{2,1,0:T(8,128)(2,1)}), bf16[4,24,2304]{2,1,0:T(8,128)(2,1)S(1)}, u32[]{:S(2)}, u32[]{:S(2)}) async-start(bf16[4,24,2304]{2,1,0:T(8,128)(2,1)} %bitcast.42), calls=%async_computation.11 | async-start | bytes 884736 | tf_op jit(solution)/shard_map/front_grads/all_to_all | solution.py:99
  323.9 1.2 collective-permute-start.8
  335.2 0.8 copy-start.3
Sparse Core Ops, SparseCore 0:
  18.1 34.4 all-gather.2
  56.7 75.5 all-gather.4
  207.5 82.9 reduce-scatter.2
  292.6 31.3 reduce-scatter.4

commit v3 on v2

--- a/solution.py
+++ b/solution.py
@@ -15,7 +15,11 @@
 bf16 = jnp.bfloat16
 both = ("rows", "blk")
 chunk = 256
+feed_chunk = 512
+grad_chunk = 1024
+subs = 2
 vmem_bytes = 56 * 1024 * 1024
+few_bytes = 24 * 1024 * 1024
 
 
 def bucket_of(relative, total_buckets):
@@ -247,7 +251,7 @@
     )(head, table)
 
 
-def table_pieces(buckets, band_ref, far_ref, sums_ref):
+def table_sums(buckets, band_ref, far_ref, sums_ref):
     first, places = steps_of(buckets)
     edge = chunk // 2
     reach = -(-bucket_edges[-1] // 8) * 8
@@ -286,18 +290,21 @@
     found = jnp.sum(sums_ref[...], axis=1, keepdims=True)
     shape = (buckets, edge)
     spread = lax.broadcasted_iota(jnp.int32, shape, 0) == lax.broadcasted_iota(jnp.int32, shape, 1)
-    found = jnp.sum(jnp.where(spread, found, 0.0), axis=0, keepdims=True)
+    return jnp.sum(jnp.where(spread, found, 0.0), axis=0, keepdims=True)
+
+
+def table_pieces(found):
     high = found.astype(bf16).astype(f32)
     middle = (found - high).astype(bf16).astype(f32)
-    pieces = [high, middle, found - high - middle, jnp.zeros((13, edge), f32)]
+    pieces = [high, middle, found - high - middle, jnp.zeros((13, found.shape[1]), f32)]
     return jnp.concatenate(pieces, axis=0).astype(bf16)
 
 
 def attend_kernel(
-    size, blocks, docs, buckets, bounds_ref, head_ref, table_ref, taken_ref, band_ref, *refs
+    size, blocks, docs, buckets, first, bounds_ref, head_ref, table_ref, taken_ref, band_ref, *refs
 ):
-    sent_ref, context_ref, expo_ref, scale_ref, keys_ref, query_ref, score_ref = refs[-7:]
-    block = pl.program_id(0)
+    sent_ref, context_ref, expo_ref, scale_ref, keys_ref, *scratch = refs[-5 - 2 * subs :]
+    step = pl.program_id(0) + first
     chunks = blocks // 2
     tok = chunk // 2
     bounds = [bounds_ref[0]]
@@ -305,11 +312,8 @@
         bounds.append(bounds[-1] + bounds_ref[d])
     heads = table_ref.shape[0] // buckets
     entry = lambda bucket: table_ref[bucket * heads + head_ref[0]]
-    highest = jnp.float32(0.0)
-    for bucket in range(buckets):
-        highest = jnp.maximum(highest, entry(bucket))
-
-    @pl.when(block == 0)
+
+    @pl.when(step == first)
     def _():
         for s in range(blocks):
             position = s * tok + lax.broadcasted_iota(jnp.int32, (1, tok), 1)
@@ -327,61 +331,72 @@
                 axis=0,
             )
             keys_ref[s * tok : (s + 1) * tok, :] = tall.T.astype(bf16)
-        query_ref[size:, :] = jnp.zeros((size, chunk), bf16)
-
-    position = block * chunk + lax.broadcasted_iota(jnp.int32, (1, chunk), 1)
-    segment = segments_at(bounds, position)
-    row = lax.broadcasted_iota(jnp.int32, (16, chunk), 0)
-    query_ref[:size, :] = tile_rows(taken_ref, block, 0, size)
-    query_ref[size : size + 16, :] = jnp.where(row == segment, 0.0, masked_score).astype(bf16)
-    far = jnp.where(
-        row <= block - 2,
-        entry(buckets // 2 - 1),
-        jnp.where(row >= block + 2, entry(buckets - 1), 0.0),
-    )
-    query_ref[size + 16 : size + 32, :] = far.astype(bf16)
-    query = query_ref[...]
-    top = jnp.full((8, chunk), masked_score, f32)
-    for c in range(chunks):
-        scores = jnp.dot(
-            keys_ref[c * chunk : (c + 1) * chunk, :], query, preferred_element_type=f32
+        for query_ref in scratch[::2]:
+            query_ref[size:, :] = jnp.zeros((size, chunk), bf16)
+
+    def turned(block, d):
+        c = block + d
+        return jnp.where(c >= chunks, c - chunks, c)
+
+    blocks_here = [step * subs + k for k in range(subs)]
+    tops = []
+    for k, block in enumerate(blocks_here):
+        query_ref, score_ref = scratch[2 * k : 2 * k + 2]
+        position = block * chunk + lax.broadcasted_iota(jnp.int32, (1, chunk), 1)
+        segment = segments_at(bounds, position)
+        row = lax.broadcasted_iota(jnp.int32, (16, chunk), 0)
+        query_ref[:size, :] = tile_rows(taken_ref, block, 0, size)
+        query_ref[size : size + 16, :] = jnp.where(row == segment, 0.0, masked_score).astype(bf16)
+        far = jnp.where(
+            row <= block - 2,
+            entry(buckets // 2 - 1),
+            jnp.where(row >= block + 2, entry(buckets - 1), 0.0),
         )
-        score_ref[c * chunk : (c + 1) * chunk, :] = scores
-        top = jnp.maximum(top, jnp.max(scores.reshape(chunk // 8, 8, chunk), axis=0))
-    for j in (-1, 0, 1):
-
-        @pl.when((block + j >= 0) & (block + j < chunks))
-        def _():
-            spot = pl.ds(pl.multiple_of((block + j) * chunk, chunk), chunk)
-            score_ref[spot, :] = score_ref[spot, :] + band_ref[j + 1]
-
-    top = jnp.max(top, axis=0, keepdims=True) + highest
-    total = jnp.zeros((8, chunk), f32)
-    context = jnp.zeros((size, chunk), f32)
-    for c in range(chunks):
-        expo = jnp.exp(score_ref[c * chunk : (c + 1) * chunk, :] - top)
-        total = total + jnp.sum(expo.reshape(chunk // 8, 8, chunk), axis=0)
-        low = expo.astype(bf16)
-        expo_ref[c * chunk : (c + 1) * chunk, :] = low
-        context = context + jnp.dot(
-            tile_rows(taken_ref, c, 2 * size, 3 * size), low, preferred_element_type=f32
-        )
-    scale = 1.0 / jnp.sum(total, axis=0, keepdims=True)
-    context = context * scale
-    context_ref[...] = context
-    scale_ref[...] = scale
-    sent_ref[0] = context[:, :tok].astype(bf16)
-    sent_ref[1] = context[:, tok:].astype(bf16)
-
-
-def attend(taken, lengths, head, table, band, buckets, *after):
+        query_ref[size + 16 : size + 32, :] = far.astype(bf16)
+        query = query_ref[...]
+        top = jnp.full((8, chunk), masked_score, f32)
+        for d in range(chunks):
+            spot = pl.ds(pl.multiple_of(turned(block, d) * chunk, chunk), chunk)
+            scores = jnp.dot(keys_ref[spot, :], query, preferred_element_type=f32)
+            if d == 0:
+                scores = scores + band_ref[1]
+            elif d == 1:
+                scores = scores + jnp.where(block + 1 < chunks, 1.0, 0.0) * band_ref[2]
+            elif d == chunks - 1:
+                scores = scores + jnp.where(block >= 1, 1.0, 0.0) * band_ref[0]
+            score_ref[d * chunk : (d + 1) * chunk, :] = scores
+            top = jnp.maximum(top, jnp.max(scores.reshape(chunk // 8, 8, chunk), axis=0))
+        tops.append(jnp.max(top, axis=0, keepdims=True))
+    for k, block in enumerate(blocks_here):
+        score_ref = scratch[2 * k + 1]
+        lanes = slice(k * chunk, (k + 1) * chunk)
+        total = jnp.zeros((8, chunk), f32)
+        context = jnp.zeros((size, chunk), f32)
+        for d in range(chunks):
+            c = turned(block, d)
+            expo = jnp.exp(score_ref[d * chunk : (d + 1) * chunk, :] - tops[k])
+            total = total + jnp.sum(expo.reshape(chunk // 8, 8, chunk), axis=0)
+            low = expo.astype(bf16)
+            expo_ref[pl.ds(pl.multiple_of(c * chunk, chunk), chunk), lanes] = low
+            context = context + jnp.dot(
+                tile_rows(taken_ref, c, 2 * size, 3 * size), low, preferred_element_type=f32
+            )
+        scale = 1.0 / jnp.sum(total, axis=0, keepdims=True)
+        context = context * scale
+        context_ref[:, lanes] = context
+        scale_ref[:, lanes] = scale
+        sent_ref[2 * k] = context[:, :tok].astype(bf16)
+        sent_ref[2 * k + 1] = context[:, tok:].astype(bf16)
+
+
+def attend(taken, lengths, head, table, band, buckets, first, stop, given, *after):
     blocks, size, tok = taken.shape
     size = size // 3
     length = blocks * tok
     smem = pl.BlockSpec(memory_space=pltpu.SMEM)
     return pl.pallas_call(
-        functools.partial(attend_kernel, size, blocks, lengths.shape[0], buckets),
-        grid=(blocks // 2,),
+        functools.partial(attend_kernel, size, blocks, lengths.shape[0], buckets, first),
+        grid=((stop or blocks // 2 // subs) - first,),
         in_specs=[
             smem,
             smem,
@@ -389,12 +404,12 @@
             pl.BlockSpec((blocks, 3 * size, tok), lambda q: (0, 0, 0)),
             pl.BlockSpec((3, chunk, chunk), lambda q: (0, 0, 0)),
         ]
-        + [pl.BlockSpec(memory_space=pl.ANY)] * len(after),
+        + [pl.BlockSpec(memory_space=pl.ANY)] * (len(given) + len(after)),
         out_specs=[
-            pl.BlockSpec((2, size, tok), lambda q: (q, 0, 0)),
-            pl.BlockSpec((size, chunk), lambda q: (0, q)),
-            pl.BlockSpec((length, chunk), lambda q: (0, q)),
-            pl.BlockSpec((1, chunk), lambda q: (0, q)),
+            pl.BlockSpec((2 * subs, size, tok), lambda q: (first + q, 0, 0)),
+            pl.BlockSpec((size, subs * chunk), lambda q: (0, first + q)),
+            pl.BlockSpec((length, subs * chunk), lambda q: (0, first + q)),
+            pl.BlockSpec((1, subs * chunk), lambda q: (0, first + q)),
         ],
         out_shape=[
             jax.ShapeDtypeStruct((blocks, size, tok), bf16),
@@ -404,131 +419,156 @@
         ],
         scratch_shapes=[
             pltpu.VMEM((length, 2 * size), bf16),
+        ]
+        + [
             pltpu.VMEM((2 * size, chunk), bf16),
             pltpu.VMEM((length, chunk), f32),
-        ],
+        ]
+        * subs,
         compiler_params=pltpu.CompilerParams(vmem_limit_bytes=vmem_bytes),
-        cost_estimate=cost(11),
+        input_output_aliases={5 + k: k for k in range(len(given))},
+        cost_estimate=cost(6),
         name="attend",
-    )(lengths, head, table, taken, band, *after)
+    )(lengths, head, table, taken, band, *given, *after)
 
 
 def attend_back_kernel(
-    size, blocks, buckets, after, taken_ref, grad_ref, context_ref, expo_ref, scale_ref, *refs
+    size, blocks, buckets, last, after, taken_ref, grad_ref, context_ref, expo_ref, scale_ref,
+    *refs,
 ):
-    sent_ref, band_ref, far_ref, sums_ref, *refs = refs[after:]
-    attend_back_steps(
-        size, blocks, buckets, taken_ref, grad_ref, context_ref, expo_ref, scale_ref,
-        sent_ref, band_ref, far_ref, sums_ref, *refs,
-    )
-
-
-def attend_back_steps(
-    size, blocks, buckets, taken_ref, grad_ref, context_ref, expo_ref, scale_ref,
-    sent_ref, band_ref, far_ref, sums_ref,
-    queries_ref, tall_ref, wide_ref, delta_ref, grad_queries_ref, grad_scores_ref,
-):
-    c = pl.program_id(0)
+    before_ref, *refs = refs
+    (
+        sent_ref, found_ref, band_ref, far_ref, sums_ref,
+        queries_ref, wide_ref, delta_ref, grad_queries_ref, grad_scores_ref,
+    ) = refs[after:]
+    step = pl.program_id(0)
     chunks = blocks // 2
     tok = chunk // 2
 
-    @pl.when(c == 0)
+    @pl.when(step == 0)
     def _():
         for s in range(blocks):
             spot = slice(s * tok, (s + 1) * tok)
             scaled = grad_ref[s].astype(f32) * scale_ref[:, spot]
             wide_ref[:, spot] = scaled.astype(bf16)
-            tall_ref[spot, :] = scaled.T.astype(bf16)
             delta_ref[:, spot] = jnp.sum(scaled * context_ref[:, spot], axis=0, keepdims=True)
-            queries_ref[spot, :] = taken_ref[s, :size, :].astype(f32).T.astype(bf16)
+            queries_ref[:, spot] = taken_ref[s, :size, :]
         grad_queries_ref[...] = jnp.zeros_like(grad_queries_ref)
         band_ref[...] = jnp.zeros_like(band_ref)
         far_ref[...] = jnp.zeros_like(far_ref)
-
-    values = tile_rows(taken_ref, c, 2 * size, 3 * size).astype(f32).T.astype(bf16)
+        for k in range(subs):
+            grad_scores_ref[k, :, :chunk] = jnp.zeros((chunk, chunk), bf16)
+            grad_scores_ref[k, :, (chunks + 1) * chunk :] = jnp.zeros((chunk, chunk), bf16)
+
+    keys = []
+    for k in range(subs):
+        c = step * subs + k
+        rows = slice(k * chunk, (k + 1) * chunk)
+        values = tile_rows(taken_ref, c, 2 * size, 3 * size).astype(f32).T.astype(bf16)
+        for q in range(chunks):
+            spot = slice(q * chunk, (q + 1) * chunk)
+            grad_weights = jnp.dot(values, wide_ref[:, spot], preferred_element_type=f32)
+            weights = expo_ref[rows, spot].astype(f32)
+            grad_scores = (weights * (grad_weights - delta_ref[:, spot])).astype(bf16)
+            grad_scores_ref[k, :, (q + 1) * chunk : (q + 2) * chunk] = grad_scores
+        grad_values = dot_on(wide_ref[...], expo_ref[rows, :], 1, 1).astype(bf16)
+        grad_keys = dot_on(
+            queries_ref[...], grad_scores_ref[k, :, chunk : (chunks + 1) * chunk], 1, 1
+        ).astype(bf16)
+        for t in range(2):
+            sent_ref[2 * c + t, size : 2 * size, :] = grad_keys[:, t * tok : (t + 1) * tok]
+            sent_ref[2 * c + t, 2 * size : 3 * size, :] = grad_values[:, t * tok : (t + 1) * tok]
+        keys.append(
+            jnp.concatenate(
+                [tile_rows(taken_ref, c, size, 2 * size), jnp.ones((16, chunk), bf16)], axis=0
+            )
+        )
     for q in range(chunks):
         spot = slice(q * chunk, (q + 1) * chunk)
-        grad_weights = jnp.dot(values, wide_ref[:, spot], preferred_element_type=f32)
-        weights = expo_ref[:, spot].astype(f32)
-        grad_scores_ref[:, spot] = (weights * (grad_weights - delta_ref[:, spot])).astype(bf16)
-    grad_values = jnp.dot(expo_ref[...], tall_ref[...], preferred_element_type=f32).T.astype(bf16)
-    grad_keys = jnp.dot(
-        grad_scores_ref[...], queries_ref[...], preferred_element_type=f32
-    ).T.astype(bf16)
-    for t in range(2):
-        sent_ref[2 * c + t, size : 2 * size, :] = grad_keys[:, t * tok : (t + 1) * tok]
-        sent_ref[2 * c + t, 2 * size : 3 * size, :] = grad_values[:, t * tok : (t + 1) * tok]
-    keys = jnp.concatenate(
-        [tile_rows(taken_ref, c, size, 2 * size), jnp.ones((16, chunk), bf16)], axis=0
-    )
-    for q in range(chunks):
-        spot = slice(q * chunk, (q + 1) * chunk)
-        part = jnp.dot(keys, grad_scores_ref[:, spot], preferred_element_type=f32)
-        grad_queries_ref[:, spot] = grad_queries_ref[:, spot] + part[:size]
-        sums = part[size : size + 8]
-        far_ref[0, :, spot] = far_ref[0, :, spot] + jnp.where(c <= q - 2, sums, 0.0)
-        far_ref[1, :, spot] = far_ref[1, :, spot] + jnp.where(c >= q + 2, sums, 0.0)
-    for j in (-1, 0, 1):
-
-        @pl.when((c - j >= 0) & (c - j < chunks))
-        def _():
-            spot = pl.ds(pl.multiple_of((c - j) * chunk, chunk), chunk)
-            band_ref[j + 1] = band_ref[j + 1] + grad_scores_ref[:, spot].astype(f32)
-
-    @pl.when(c == chunks - 1)
+        total = grad_queries_ref[:, spot]
+        for k in range(subs):
+            c = step * subs + k
+            part = jnp.dot(
+                keys[k],
+                grad_scores_ref[k, :, (q + 1) * chunk : (q + 2) * chunk],
+                preferred_element_type=f32,
+            )
+            total = total + part[:size]
+            sums = part[size : size + 8]
+            far_ref[0, :, spot] = far_ref[0, :, spot] + jnp.where(c <= q - 2, sums, 0.0)
+            far_ref[1, :, spot] = far_ref[1, :, spot] + jnp.where(c >= q + 2, sums, 0.0)
+        grad_queries_ref[:, spot] = total
+    for k in range(subs):
+        c = step * subs + k
+        for j in (-1, 0, 1):
+            spot = pl.ds(pl.multiple_of((c - j + 1) * chunk, chunk), chunk)
+            band_ref[j + 1] = band_ref[j + 1] + grad_scores_ref[k, :, spot].astype(f32)
+
+    @pl.when(step == chunks // subs - 1)
     def _():
         for s in range(blocks):
             sent_ref[s, :size, :] = grad_queries_ref[:, s * tok : (s + 1) * tok].astype(bf16)
-        pieces = table_pieces(buckets, band_ref, far_ref, sums_ref)
-        for s in range(blocks):
-            sent_ref[s, 3 * size :, :] = pieces
-
-
-def attend_back(taken, grads, context, expo, scale, buckets, *after):
-    blocks, size, tok = grads.shape
+        found = before_ref[...] + table_sums(buckets, band_ref, far_ref, sums_ref)
+        found_ref[...] = found
+        if last:
+            pieces = table_pieces(found)
+            for s in range(blocks):
+                sent_ref[s, 3 * size :, :] = pieces
+
+
+def attend_back(taken, grads, context, expo, scale, buckets, m, last, before, *after):
+    blocks, size, _ = grads.shape
+    tok = taken.shape[2]
     length = expo.shape[0]
+    height = 3 * size + 16 if last else 3 * size
     return pl.pallas_call(
-        functools.partial(attend_back_kernel, size, blocks, buckets, len(after)),
-        grid=(blocks // 2,),
+        functools.partial(attend_back_kernel, size, blocks, buckets, last, len(after)),
+        grid=(blocks // 2 // subs,),
         in_specs=[
             pl.BlockSpec((blocks, 3 * size, tok), lambda c: (0, 0, 0)),
-            pl.BlockSpec((blocks, size, tok), lambda c: (0, 0, 0)),
+            pl.BlockSpec((blocks, size, tok), lambda c: (0, 0, m)),
             pl.BlockSpec((size, length), lambda c: (0, 0)),
-            pl.BlockSpec((chunk, length), lambda c: (c, 0)),
+            pl.BlockSpec((subs * chunk, length), lambda c: (c, 0)),
             pl.BlockSpec((1, length), lambda c: (0, 0)),
+            pl.BlockSpec((1, chunk // 2), lambda c: (0, 0)),
         ]
         + [pl.BlockSpec(memory_space=pl.ANY)] * len(after),
-        out_specs=pl.BlockSpec((blocks, 3 * size + 16, tok), lambda c: (0, 0, 0)),
-        out_shape=jax.ShapeDtypeStruct((blocks, 3 * size + 16, tok), bf16),
+        out_specs=[
+            pl.BlockSpec((blocks, height, tok), lambda c: (0, 0, 0)),
+            pl.BlockSpec((1, chunk // 2), lambda c: (0, 0)),
+        ],
+        out_shape=[
+            jax.ShapeDtypeStruct((blocks, height, tok), bf16),
+            jax.ShapeDtypeStruct((1, chunk // 2), f32),
+        ],
         scratch_shapes=[
             pltpu.VMEM((3, chunk, chunk), f32),
             pltpu.VMEM((2, 8, length), f32),
             pltpu.VMEM((buckets, chunk // 2), f32),
-            pltpu.VMEM((length, size), bf16),
-            pltpu.VMEM((length, size), bf16),
+            pltpu.VMEM((size, length), bf16),
             pltpu.VMEM((size, length), bf16),
             pltpu.VMEM((1, length), f32),
             pltpu.VMEM((size, length), f32),
-            pltpu.VMEM((chunk, length), bf16),
+            pltpu.VMEM((subs, chunk, length + 2 * chunk), bf16),
         ],
         compiler_params=pltpu.CompilerParams(vmem_limit_bytes=vmem_bytes),
         cost_estimate=cost(13),
         name="attend_back",
-    )(taken, grads, context, expo, scale, *after)
+    )(taken, grads, context, expo, scale, before, *after)
 
 
 def feed_kernel(
-    heads, steps, flipped_ref, matrix_ref, hidden_ref, context_ref, given_ref, gain_ref, *refs
+    heads, steps, micro, flipped_ref, matrix_ref, hidden_ref, given_ref, gain_ref, *refs
 ):
+    contexts, refs = refs[:micro], refs[micro:]
     outs, gates, ups, downs = (refs[2 * k : 2 * k + 2] for k in range(4))
     (
-        result_ref, grad_mid_ref, grad_context_ref, packet_ref, left_ref,
+        result_ref, grad_mid_ref, grad_context_ref, packet_ref, left_ref, other_left_ref,
         normed_ref, branch_ref, cot_ref, mid_ref, total_ref, grad_ref,
-    ) = refs[-11:]
-    units = steps * chunk
-    lead = packet_ref.shape[1] - 3 * units - context_ref.shape[0] * context_ref.shape[1]
+    ) = refs[-12:]
+    units = steps * feed_chunk
     j = pl.program_id(0)
-    size, tok = context_ref.shape[1:]
+    size = contexts[0].shape[1]
     sides = side(flipped_ref[0], hidden_ref.shape[1] // 2)
 
     @pl.when(j == 0)
@@ -536,9 +576,10 @@
         cot_ref[...] = jnp.dot(
             given_ref[...], matrix_ref[...], preferred_element_type=f32
         ).astype(bf16)
-        context = context_ref[...].reshape(-1, tok)
-        context = context.astype(f32).T.astype(bf16)
-        packet_ref[:, packet_ref.shape[1] - context.shape[1] :] = context
+        context = jnp.concatenate(
+            [ref[...].reshape(-1, ref.shape[2]).astype(f32).T for ref in contexts], axis=0
+        ).astype(bf16)
+        packet_ref[:, 3 * units :] = context
         context = context[:, : heads * size]
         for lanes, ref in zip(sides, outs):
             mid_ref[:, lanes] = dot_on(context, ref[...], 1, 1)
@@ -570,7 +611,9 @@
     grad_gate = (grad_inner * up * gelu_grad).astype(bf16)
     grad_up = (grad_inner * gelu).astype(bf16)
     for k, part in enumerate((grad_gate, grad_up, inner)):
-        packet_ref[:, pl.ds(pl.multiple_of(lead + k * units + j * chunk, chunk), chunk)] = part
+        packet_ref[
+            :, pl.ds(pl.multiple_of(k * units + j * feed_chunk, feed_chunk), feed_chunk)
+        ] = part
     for k, lanes in enumerate(sides):
         total_ref[:, lanes] = total_ref[:, lanes] + dot_on(inner, downs[k][...], 1, 1)
         grad_ref[:, lanes] = (
@@ -598,34 +641,34 @@
         half = hidden_ref.shape[1] // 2
         for k, ref in enumerate((normed_ref, cot_ref, branch_ref)):
             left_ref[:, k * half : (k + 1) * half] = ref[:, own]
-            packet_ref[:, k * half : (k + 1) * half] = ref[:, other]
-        packet_ref[:, 3 * half : lead] = jnp.zeros((tok, lead - 3 * half), bf16)
-
-
-def feed(flipped, matrix, hidden, context, cot, gain, weights, heads, *after):
+            other_left_ref[:, k * half : (k + 1) * half] = ref[:, other]
+
+
+def feed(flipped, matrix, hidden, contexts, cot, gain, weights, heads, *after):
     tok, width = hidden.shape
-    blocks, size, _ = context.shape
+    blocks, size, _ = contexts[0].shape
+    micro = len(contexts)
     inner_width = heads * size
     units = (weights[0].shape[1] - inner_width) // 3
-    steps = units // chunk
-    first = inner_width // chunk
+    steps = units // feed_chunk
+    assert 3 * units % inner_width == 0
     whole = lambda *shape: pl.BlockSpec(shape, lambda j: (0,) * len(shape))
-    column = lambda offset: pl.BlockSpec((width // 2, chunk), lambda j: (0, offset + j))
-    lead = -(-3 * (width // 2) // (2 * chunk)) * 2 * chunk
-    packet = lead + 3 * units + blocks * size
-    weight_specs = [whole(width // 2, inner_width)] * 2
+    column = lambda offset: pl.BlockSpec((width // 2, feed_chunk), lambda j: (0, offset + j))
+    packet = 3 * units + blocks * size
+    spot = 3 * units // inner_width
+    weight_specs = [pl.BlockSpec((width // 2, inner_width), lambda j: (0, spot))] * 2
     for k in range(3):
-        weight_specs += [column(first + k * steps)] * 2
+        weight_specs += [column(k * steps)] * 2
     return pl.pallas_call(
-        functools.partial(feed_kernel, heads, steps),
+        functools.partial(feed_kernel, heads, steps, micro),
         grid=(steps,),
         in_specs=[
             pl.BlockSpec(memory_space=pltpu.SMEM),
             whole(width, width),
             whole(tok, width),
-            whole(blocks, size, tok),
             whole(tok, width),
             whole(1, width),
+            *[whole(*context.shape) for context in contexts],
             *weight_specs,
         ]
         + [pl.BlockSpec(memory_space=pl.ANY)] * len(after),
@@ -635,6 +678,7 @@
             whole(blocks, size, tok),
             whole(tok, packet),
             whole(tok, 3 * (width // 2)),
+            whole(tok, 3 * (width // 2)),
         ],
         out_shape=[
             jax.ShapeDtypeStruct((tok, width), bf16),
@@ -642,12 +686,13 @@
             jax.ShapeDtypeStruct((blocks, size, tok), bf16),
             jax.ShapeDtypeStruct((tok, packet), bf16),
             jax.ShapeDtypeStruct((tok, 3 * (width // 2)), bf16),
+            jax.ShapeDtypeStruct((tok, 3 * (width // 2)), bf16),
         ],
         scratch_shapes=[pltpu.VMEM((tok, width), bf16)] * 3 + [pltpu.VMEM((tok, width), f32)] * 3,
         compiler_params=pltpu.CompilerParams(vmem_limit_bytes=vmem_bytes),
         cost_estimate=cost(8),
         name="feed",
-    )(flipped, matrix, hidden, context, cot, gain, *weights * 4, *after)
+    )(flipped, matrix, hidden, cot, gain, *contexts, *weights * 4, *after)
 
 
 def store_tall(ref, parts):
@@ -673,19 +718,16 @@
 
 
 def weight_grads(lefts, rights, half, units, inner_width, *after):
-    tok, block = lefts[0].shape[0], 2 * chunk
+    tok, block = lefts[0].shape[0], grad_chunk
     steps = units // block
     counts = [(0, 2 * steps), (1, steps), (2, inner_width // block)]
     total = 3 * steps + inner_width // block
-    lead = rights[0].shape[1] - total * block
     anywhere = pl.BlockSpec(memory_space=pl.ANY)
     return pl.pallas_call(
         functools.partial(weight_grad_kernel, counts, len(lefts), half),
         grid=(total,),
-        in_specs=[
-            pl.BlockSpec((tok, min(left.shape[1], lead)), lambda j: (0, 0)) for left in lefts
-        ]
-        + [pl.BlockSpec((tok, block), lambda j: (0, lead // block + j))] * len(rights)
+        in_specs=[pl.BlockSpec((tok, 3 * half), lambda j: (0, 0))] * len(lefts)
+        + [pl.BlockSpec((tok, block), lambda j: (0, j))] * len(rights)
         + [anywhere] * len(after),
         out_specs=pl.BlockSpec((half, block), lambda j: (0, j)),
         out_shape=jax.ShapeDtypeStruct((half, total * block), bf16),
@@ -756,7 +798,7 @@
             jax.ShapeDtypeStruct((1, width), f32),
         ],
         scratch_shapes=[pltpu.VMEM((8, width), f32)],
-        compiler_params=pltpu.CompilerParams(vmem_limit_bytes=vmem_bytes),
+        compiler_params=pltpu.CompilerParams(vmem_limit_bytes=few_bytes),
         cost_estimate=cost(3),
         name="project",
     )(flipped, matrix, inputs, *weights, after)
@@ -776,7 +818,7 @@
 
 def input_grad_kernel(heads, micro, *refs):
     flipped_ref, matrix_ref, inputs_ref, own_weights, other_weights, gains_ref = refs[:6]
-    grads, mids = (refs[6 + k * micro : 6 + (k + 1) * micro] for k in range(2))
+    mid_ref, *grads = refs[6 : 7 + micro]
     input_grad_ref, wide_ref, lined_ref = refs[-3:]
     tok, width = inputs_ref.shape[1:]
     inner_width = (own_weights.shape[1] - 128) // 3
@@ -793,7 +835,7 @@
         scale = lax.rsqrt(jnp.mean(hidden * hidden, axis=-1, keepdims=True) + norm_eps)
         gained = grad * gain
         inward = jnp.mean(gained * hidden, axis=-1, keepdims=True)
-        found = mids[m][...] + scale * gained - hidden * (scale * scale * scale * inward)
+        found = mid_ref[m * tok : (m + 1) * tok, :] + scale * gained - hidden * (scale * scale * scale * inward)
         high = found.astype(bf16)
         rest = found - high.astype(f32)
         middle = rest.astype(bf16)
@@ -803,55 +845,61 @@
         )
 
 
-def input_grads(flipped, matrix, inputs, weights, gains, grads, mids, heads, *after):
+def input_grads(flipped, matrix, inputs, weights, gains, grads, mid, heads, *after):
     micro, tok, width = inputs.shape
     inner_width = (weights[0].shape[1] - 128) // 3
     vmem = pl.BlockSpec(memory_space=pltpu.VMEM)
     return pl.pallas_call(
         functools.partial(input_grad_kernel, heads, micro),
         in_specs=[pl.BlockSpec(memory_space=pltpu.SMEM)]
-        + [vmem] * (5 + 2 * micro)
+        + [vmem] * (6 + micro)
         + [pl.BlockSpec(memory_space=pl.ANY)] * len(after),
         out_shape=jax.ShapeDtypeStruct((micro, tok, width), f32),
         scratch_shapes=[
             pltpu.VMEM((width, micro * tok), f32),
             pltpu.VMEM((3 * inner_width, micro * tok), bf16),
         ],
-        compiler_params=pltpu.CompilerParams(vmem_limit_bytes=vmem_bytes),
+        compiler_params=pltpu.CompilerParams(vmem_limit_bytes=few_bytes),
         cost_estimate=cost(6),
         name="input_grads",
-    )(flipped, matrix, inputs, *weights, gains, *grads, *mids, *after)
+    )(flipped, matrix, inputs, *weights, gains, mid, *grads, *after)
 
 
 def front_grad_kernel(heads, parts, half, which, *refs):
     flipped_ref = refs[0]
     lefts, grads = refs[1 : 1 + parts], refs[1 + parts : 1 + 2 * parts]
     out_ref, tall_ref, lined_ref = refs[-3:]
-    tok = grads[0].shape[2]
-    inner_width = out_ref.shape[1] // 3
-    lined(grads, heads, inner_width // heads, lined_ref)
-    lanes = side(flipped_ref[0], half)[which]
-    for p, ref in enumerate(lefts):
-        tall = ref[:, lanes].astype(f32).T.astype(bf16)
-        tall_ref[:, p * tok : (p + 1) * tok] = tall
-    for k in range(3):
-        spot = slice(k * inner_width, (k + 1) * inner_width)
-        out_ref[:, spot] = dot_on(tall_ref[...], lined_ref[spot, :], 1, 1).astype(bf16)
+    _, size, tok = grads[0].shape
+
+    @pl.when(pl.program_id(0) == 0)
+    def _():
+        lanes = side(flipped_ref[0], half)[which]
+        for p, ref in enumerate(lefts):
+            tall = ref[:, lanes].astype(f32).T.astype(bf16)
+            tall_ref[:, p * tok : (p + 1) * tok] = tall
+
+    for p, ref in enumerate(grads):
+        lined_ref[:, p * tok : (p + 1) * tok] = ref[:heads].reshape(heads * size, tok)
+    out_ref[...] = dot_on(tall_ref[...], lined_ref[...], 1, 1).astype(bf16)
 
 
 def front_grads(flipped, lefts, grads, inner_width, heads, which):
     tok, width = lefts[0].shape
     parts = len(lefts)
-    vmem = pl.BlockSpec(memory_space=pltpu.VMEM)
+    part = pl.BlockSpec((grads[0].shape[0], inner_width // heads, tok), lambda k: (0, k, 0))
     return pl.pallas_call(
         functools.partial(front_grad_kernel, heads, parts, width // 2, which),
-        in_specs=[pl.BlockSpec(memory_space=pltpu.SMEM)] + [vmem] * (2 * parts),
+        grid=(3,),
+        in_specs=[pl.BlockSpec(memory_space=pltpu.SMEM)]
+        + [pl.BlockSpec((tok, width), lambda k: (0, 0))] * parts
+        + [part] * parts,
+        out_specs=pl.BlockSpec((width // 2, inner_width), lambda k: (0, k)),
         out_shape=jax.ShapeDtypeStruct((width // 2, 3 * inner_width), bf16),
         scratch_shapes=[
             pltpu.VMEM((width // 2, parts * tok), bf16),
-            pltpu.VMEM((3 * inner_width, parts * tok), bf16),
+            pltpu.VMEM((inner_width, parts * tok), bf16),
         ],
-        compiler_params=pltpu.CompilerParams(vmem_limit_bytes=vmem_bytes),
+        compiler_params=pltpu.CompilerParams(vmem_limit_bytes=few_bytes),
         cost_estimate=cost(5),
         name="front_grads",
     )(flipped, *lefts, *grads)
@@ -886,7 +934,7 @@
     gate, up, down, out, gain_grad = pl.pallas_call(
         unpack_back_kernel,
         out_shape=[jax.ShapeDtypeStruct(shape, f32) for shape in shapes],
-        compiler_params=pltpu.CompilerParams(vmem_limit_bytes=vmem_bytes),
+        compiler_params=pltpu.CompilerParams(vmem_limit_bytes=few_bytes),
         name="unpack_back",
     )(sums, w_gate, w_up, gain[None, :])
     return gate, up, down.T, out.T, gain_grad[0]
@@ -909,7 +957,7 @@
         unpack_front_kernel,
         in_specs=[vmem] * 5 + [pl.BlockSpec(memory_space=pl.ANY)],
         out_shape=[jax.ShapeDtypeStruct(shape, f32) for shape in shapes],
-        compiler_params=pltpu.CompilerParams(vmem_limit_bytes=vmem_bytes),
+        compiler_params=pltpu.CompilerParams(vmem_limit_bytes=few_bytes),
         name="unpack_front",
     )(parts, w_query, w_key, w_value, gain[None, :], after)
     return query, key, value, gain_grad[0]
@@ -938,7 +986,7 @@
 
     with jax.named_scope("weights"):
         front_full = gather_front(w_query, w_key, w_value, attn_gain, ff_gain)
-        back_own = gather_back(jnp.concatenate([w_out.T, w_gate, w_up, w_down.T], axis=1), front_full[0])
+        back_own = gather_back(jnp.concatenate([w_gate, w_up, w_down.T, w_out.T], axis=1), front_full[0])
 
     band = bias_tiles(head, table, buckets)
     sent, tokens, normed_a, gain_a, gain_f = project(
@@ -950,57 +998,55 @@
             part = tie(sent[m], taken[-1]) if m else sent[m]
             taken.append(lax.all_to_all(part, "blk", 0, 0, tiled=True))
 
-    kept, contexts = [], []
+    kept, contexts, half = [], [], blocks // 4 // subs
     for m in micros:
-        part, *rest = attend(
-            taken[m], doc_lengths[m, 0], head, table, band, buckets, *[k[0] for k in kept]
-        )
-        kept.append(rest)
+        given = taken[m], doc_lengths[m, 0], head, table, band, buckets
+        outs = [k[0] for k in kept]
+        if m:
+            outs = attend(*given, 0, half, [], *outs)
+            outs = attend(*given, half, None, outs, *contexts)
+        else:
+            outs = attend(*given, 0, None, [])
+        kept.append(outs[1:])
         with jax.named_scope("context"):
-            contexts.append(lax.all_to_all(part, "blk", 0, 0, tiled=True))
+            contexts.append(lax.all_to_all(outs[0], "blk", 0, 0, tiled=True))
     with jax.named_scope("weights"):
-        back_full = gather_other(back_own, part)
-
-    fed, grads, packets = [], [], []
+        back_full = gather_other(back_own, outs[0])
+
     fits = staged(rows, blocks, share)
-    for m in micros:
-        outs = list(
-            feed(
-                flipped, matrix, tokens[m], contexts[m], cotangent[m, 0], gain_f, back_full, heads,
-            )
-        )
-        with jax.named_scope("grad_context"):
-            part = tie(outs[2], *grads) if m else outs[2]
-            grads.append(lax.all_to_all(part, "blk", 0, 0, tiled=True))
-        if fits:
-            with jax.named_scope("packet"):
-                outs[3] = tie(outs[3], grads[0]) if m else outs[3]
-                packets.append(flip(outs[3], "rows", 1))
-        fed.append(outs)
-    result, grad_mid, _, mine, left = zip(*fed)
+    here = micro * tok
+    result, grad_mid, grad_context, mine, left, left_other = feed(
+        flipped, matrix, tokens.reshape(here, width), contexts,
+        cotangent[:, 0].reshape(here, width), gain_f, back_full, heads,
+    )
+    with jax.named_scope("grad_context"):
+        grads = lax.all_to_all(grad_context, "blk", 0, 0, tiled=True)
+    if fits:
+        with jax.named_scope("packet"):
+            packet, near_left = flip(mine, "rows", 1), flip(left_other, "rows", 1)
 
     wide = blocks * size
     with jax.named_scope("back_grads"):
         sizes = width // 2, hidden_units, wide
         if fits:
-            own = weight_grads([*left, *packets], [*mine, *packets], *sizes)
+            parts = [left, near_left], [mine, packet]
+            own = tie(weight_grads(*parts, *sizes), grads)
             back_grad = scatter_back(own)
         else:
-            own, other = (weight_grads(lefts, mine, *sizes) for lefts in (left, mine))
+            own, other = (weight_grads([lefts], [mine], *sizes) for lefts in (left, left_other))
             back_grad = scatter_whole(own, other)
-    grad_qkv = []
+    grad_qkv, found = [], jnp.zeros((1, chunk // 2), f32)
     for m in micros:
-        returned = attend_back(taken[m], grads[m], *kept[m], buckets, own)
+        returned, found = attend_back(
+            taken[m], grads, *kept[m], buckets, m, m == micro - 1, found, own
+        )
         with jax.named_scope("grad_qkv"):
             returned = tie(returned, *grad_qkv) if m else returned
             grad_qkv.append(lax.all_to_all(returned, "blk", 0, 0, tiled=True))
 
     with jax.named_scope("table"):
-        sums = sum(
-            jnp.sum(g[:heads, 3 * size : 3 * size + 3, :buckets].astype(f32), axis=1)
-            for g in grad_qkv
-        )
-        table_grad = sums.T
+        pieces = grad_qkv[-1][:heads, 3 * size : 3 * size + 3, :buckets]
+        table_grad = jnp.sum(pieces.astype(f32), axis=1).T
         for bit in bits_of(rows):
             table_grad = table_grad + flip(table_grad, "rows", bit)
 
@@ -1034,7 +1080,7 @@
     )
 
     return (
-        jnp.stack(result).reshape(micro, 1, tok, width),
+        result.reshape(micro, 1, tok, width),
         input_grad[:, None],
         attn_gain_grad,
         query_grad,

time: 347 us -> 321 us (0.925)
  blocking collectives: 26.2 us -> 66.5 us
  Pallas kernels: 123 us -> 96.4 us
  waiting for transfers between devices: 104 us -> 81.2 us
  starting transfers between devices: 58.4 us -> 37.2 us
  local copies, waits for them, and re-layouts: 12.7 us -> 19.2 us
    all_to_all x0 -> x2, blocking collectives: none -> 41.3 us  [the longest x1 26.5 us: body(): grad_qkv.append(lax.all_to_all(returned, 'blk', 0, 0, tiled=True))]
    all_to_all x2 -> x1, waiting for transfers between devices: 25.3 us -> 5.42 us  [body(): grad_qkv.append(lax.all_to_all(returned, 'blk', 0, 0, tiled=True))]
    all_to_all x4 -> x2, starting transfers between devices: 23.1 us -> 8.66 us  [the longest x1 5.09 us: body(): contexts.append(lax.all_to_all(outs[0], 'blk', 0, 0, tiled=True))]
    pallas_call x2 -> x1, Pallas kernels: 28.1 us -> 16.2 us  [feed(): pl.pallas_call(functools.partial(feed_kernel, heads, steps, micro), grid=...]
    all_to_all x2 -> x1, starting transfers between devices: 12.3 us -> 4.02 us  [body(): grad_qkv.append(lax.all_to_all(returned, 'blk', 0, 0, tiled=True))]
    unnamed x48 -> x62, local copies, waits for them, and re-layouts: 8.42 us -> 15.9 us
    all_to_all x4 -> x2, waiting for transfers between devices: 8.85 us -> 3.77 us  [the longest x1 2.05 us: body(): grads = lax.all_to_all(grad_context, 'blk', 0, 0, tiled=True)]
    reduce_scatter x1, waiting for transfers between devices: 0.01 us -> 3.97 us  [scatter_back(): lax.psum_scatter(own, 'blk', scatter_dimension=0, axis_index_groups=withi...]
  transfers between devices with their start and end apart: 24 -> 21, of which waited for: 15 -> 15; matrix products, arithmetic and copies ran while one was open for 3% -> 3% of each run, Pallas kernels for 31% -> 24%
where the time goes in v3:
time: 321 us; the launch traced here: 320 us
  Pallas kernels  96.4 us (30%)
  waiting for transfers between devices  81.2 us (25%)
  blocking collectives  66.5 us (21%)
  starting transfers between devices  37.2 us (12%)
  local copies, waits for them, and re-layouts  19.2 us (6%)
  between operations  14.1 us (4%)
  other arithmetic  5.01 us (2%)
    all_to_all x4, waiting for transfers between devices, exchange(): lax.all_to_all(array, 'blk', 0, 0, tiled=True, axis_index_groups=groups)  32.1 us
    pallas_call x2, Pallas kernels, attend_back(): pl.pallas_call(functools.partial(attend_back_kernel, size, blocks, bucket...  26.9 us
    all_to_all x1, blocking collectives, body(): grad_qkv.append(lax.all_to_all(returned, 'blk', 0, 0, tiled=True))  26.5 us
    all_to_all x1, blocking collectives, body(): taken.append(lax.all_to_all(part, 'blk', 0, 0, tiled=True))  25.3 us
    pallas_call x3, Pallas kernels, attend(): pl.pallas_call(functools.partial(attend_kernel, size, blocks, lengths.sha...  24.3 us
    all_gather x1, waiting for transfers between devices, gather_back(): lax.all_gather(shard, 'blk', axis=0, tiled=True, axis_index_groups=across)  19.1 us
    all_to_all x4, starting transfers between devices, exchange(): lax.all_to_all(array, 'blk', 0, 0, tiled=True, axis_index_groups=groups)  18.9 us
    pallas_call x1, Pallas kernels, feed(): pl.pallas_call(functools.partial(feed_kernel, heads, steps, micro), grid=...  16.2 us
  transfers between devices with their start and end apart: 21, of which 15 were waited for; matrix products, arithmetic and copies ran while one was open for 3% of the time, Pallas kernels for 24%

profile of v3, /device:TPU:0, one launch (start us, length us, event | category | flops | bytes accessed | tf_op | source)
XLA Modules:
  0.0 319.5 jit_solution(16067424951093349942)
XLA Ops:
  7.2 1.7 pack.1
  8.9 6.3 %all-to-all-start = ((bf16[4,24,2432]{2,1,0:T(8,128)(2,1)}), bf16[4,24,2432]{2,1,0:T(8,128)(2,1)S(1)}, u32[]{:S(2)}, u32[]{:S(2)}) async-start(bf16[4,24,2432]{2,1,0:T(8,128)(2,1)} %pack.1), calls=%async_computation | async-start | bytes 933888 | tf_op jit(solution)/shard_map/weights/all_to_all | solution.py:103
  15.2 1.8 pad_maximum_fusion
  17.0 11.5 %all-to-all-done = bf16[4,24,2432]{2,1,0:T(8,128)(2,1)S(1)} async-done(((bf16[4,24,2432]{2,1,0:T(8,128)(2,1)}), bf16[4,24,2432]{2,1,0:T(8,128)(2,1)S(1)}, u32[]{:S(2)}, u32[]{:S(2)}) %all-to-all-start) | async-done | bytes 466976 | tf_op jit(solution)/shard_map/weights/all_to_all | solution.py:103
  28.4 1.4 tile.10
  29.8 3.7 %all-to-all-start.1 = ((bf16[4,96,2432]{2,1,0:T(8,128)(2,1)}), bf16[4,96,2432]{2,1,0:T(8,128)(2,1)S(1)}, u32[]{:S(2)}, u32[]{:S(2)}) async-start(bf16[4,96,2432]{2,1,0:T(8,128)(2,1)} %tile.10), calls=%async_computation.1 | async-start | bytes 3735552 | tf_op jit(solution)/shard_map/weights/all_to_all | solution.py:103
  33.5 19.1 %all-gather.3.cloned.1.call-done.refs_0_ = bf16[96,6912]{1,0:T(8,128)(2,1)} async-done(((bf16[24,6912]{1,0:T(8,128)(2,1)}), bf16[96,6912]{1,0:T(8,128)(2,1)}) %all-gather.3.cloned.1.call-update) | async-done | bytes 1327120 | tf_op jit(solution)/shard_map/weights/all_gather | solution.py:154
  52.6 2.7 all-to-all-done.1
  55.3 1.3 copy-done
  56.8 0.7 reshape.64.table_ref
  57.5 2.0 bias_tiles.1.after_ref.band_ref
  59.5 1.4 collective-permute-done.other_ref.refs_4_
  60.9 1.2 copy-done.24
  62.1 4.2 %project.1 = (bf16[16,192,128]{2,1,0:T(8,128)(2,1)S(1)}, bf16[16,192,128]{2,1,0:T(8,128)(2,1)S(1)}, bf16[2,128,768]{2,1,0:T(8,128)(2,1)S(1)}, bf16[256,768]{1,0:...) custom-call(s32[1]{0:T(128)} %bitcast.flipped_ref.refs_0_, bf16[768,768]{1,0:T(8,128)(2,1)S(1)} %copy-done.8, ...), custom_call_target="tpu_custom_call" | custom-call | flops 3000000000 | tf_op jit(solution)/shard_map/project/pallas_call | solution.py:783
  66.3 0.9 copy-done.7
  67.2 25.3 %all_to_all.67.taken_ref.refs_1_ = bf16[16,192,128]{2,1,0:T(8,128)(2,1)} all-to-all(bf16[16,192,128]{2,1,0:T(8,128)(2,1)S(1)} %get-tuple-element.50), channel_id=1, replica_groups=mesh['rows'=2,'blk'=16] {'blk'}, dimensions={0} | all-to-all | bytes 1572864 | tf_op jit(solution)/shard_map/project/all_to_all | solution.py:999
  92.4 3.6 %all-to-all-start.4 = ((bf16[16,192,128]{2,1,0:T(8,128)(2,1)}), bf16[16,192,128]{2,1,0:T(8,128)(2,1)S(1)}, u32[]{:S(2)}, u32[]{:S(2)}) async-start(bf16[16,192,128]{2,1,0:T(8,128)(2,1)} %tie.7), calls=%async_computation.4 | async-start | bytes 1572864 | tf_op jit(solution)/shard_map/project/all_to_all | solution.py:999
  96.1 0.5 slice_bitcast_fusion
  96.6 10.6 %attend.3 = (bf16[16,64,128]{2,1,0:T(8,128)(2,1)}, f32[64,2048]{1,0:T(8,128)}, bf16[2048,2048]{1,0:T(8,128)(2,1)}, f32[1,2048]{1,0:T(1,128)}) custom-call(s32[6]{0:T(128)} %get-tuple-element.111.bounds_ref, s32[1]{0:T(128)} %bitcast.6.head_ref, f32[384]{0:T(512)} %reshape.64.table_ref, bf16[16,192,128]{2,1,0:T(8,128)(2,1)} %all_to_all.67.taken_ref.refs_1_, ...), custom_call_target="tpu_custom_call" | custom-call | flops 6000000000 | tf_op jit(solution)/shard_map/attend/pallas_call | solution.py:397
  107.2 7.8 %all-to-all-done.4.taken_ref = bf16[16,192,128]{2,1,0:T(8,128)(2,1)S(1)} async-done(((bf16[16,192,128]{2,1,0:T(8,128)(2,1)}), bf16[16,192,128]{2,1,0:T(8,128)(2,1)S(1)}, u32[]{:S(2)}, u32[]{:S(2)}) %all-to-all-start.4) | async-done | bytes 786464 | tf_op jit(solution)/shard_map/project/all_to_all | solution.py:999
  115.1 5.1 %all-to-all-start.3 = ((bf16[16,64,128]{2,1,0:T(8,128)(2,1)}), bf16[16,64,128]{2,1,0:T(8,128)(2,1)S(1)}, u32[]{:S(2)}, u32[]{:S(2)}) async-start(bf16[16,64,128]{2,1,0:T(8,128)(2,1)} %get-tuple-element.51), calls=%async_computation.3 | async-start | bytes 524288 | tf_op jit(solution)/shard_map/context/all_to_all | solution.py:1012
  120.2 6.9 %attend.4 = (bf16[16,64,128]{2,1,0:T(8,128)(2,1)}, f32[64,2048]{1,0:T(8,128)}, bf16[2048,2048]{1,0:T(8,128)(2,1)}, f32[1,2048]{1,0:T(1,128)}) custom-call(s32[6]{0:T(128)} %get-tuple-element.110.bounds_ref, s32[1]{0:T(128)} %bitcast.6.head_ref, f32[384]{0:T(512)} %reshape.64.table_ref, bf16[16,192,128]{2,1,0:T(8,128)(2,1)} %copy-done.28, ...), custom_call_target="tpu_custom_call" | custom-call | flops 6000000000 | tf_op jit(solution)/shard_map/attend/pallas_call | solution.py:397
  127.1 1.7 all-to-all-done.3.refs_4_.refs_0_
  128.8 0.7 copy-done.26
  129.5 6.8 %attend.5 = (bf16[16,64,128]{2,1,0:T(8,128)(2,1)}, f32[64,2048]{1,0:T(8,128)}, bf16[2048,2048]{1,0:T(8,128)(2,1)}, f32[1,2048]{1,0:T(1,128)}) custom-call(s32[6]{0:T(128)} %get-tuple-element.110.bounds_ref, s32[1]{0:T(128)} %bitcast.6.head_ref, f32[384]{0:T(512)} %reshape.64.table_ref, ...), custom_call_target="tpu_custom_call", output_to_operand_aliasing={{0}: (5, {}), {1}: (6, {}), {2}: (7, {}), {3}: (8, {})} | custom-call | flops 6000000000 | tf_op jit(solution)/shard_map/attend/pallas_call | solution.py:397
  136.4 0.9 copy-done.27
  137.3 14.8 %all_to_all.68.refs_1_ = bf16[16,64,128]{2,1,0:T(8,128)(2,1)} all-to-all(bf16[16,64,128]{2,1,0:T(8,128)(2,1)S(1)} %copy-done.27), channel_id=1, replica_groups=mesh['rows'=2,'blk'=16] {'blk'}, dimensions={0} | all-to-all | bytes 524288 | tf_op jit(solution)/shard_map/context/all_to_all | solution.py:1012
  152.0 16.2 %feed.1 = (bf16[256,768]{1,0:T(8,128)(2,1)}, f32[256,768]{1,0:T(8,128)}, bf16[16,64,256]{2,1,0:T(8,128)(2,1)}, bf16[256,7168]{1,0:T(8,128)(2,1)}, bf16[256,1152]{1,0:T(8,128)(2,1)}, /*index=5*/bf16[256,1152]{1,0:T(8,128)(2,1)}) custom-call(s32[1]{0:T(128)} %bitcast.flipped_ref.refs_0_, bf16[768,768]{1,0:T(8,128)(2,1)} %constant.18.clone.matrix_ref.refs_1_, ...), custom_call_target="tpu_custom_call" | custom-call | flops 8000000000 | tf_op jit(solution)/shard_map/feed/pallas_call | solution.py:662
  168.3 0.5 collective-permute-start.2
  168.8 3.6 %all-to-all-start.6 = ((bf16[16,64,256]{2,1,0:T(8,128)(2,1)}), bf16[16,64,256]{2,1,0:T(8,128)(2,1)S(1)}, u32[]{:S(2)}, u32[]{:S(2)}) async-start(bf16[16,64,256]{2,1,0:T(8,128)(2,1)} %get-tuple-element.62), calls=%async_computation.6 | async-start | bytes 1048576 | tf_op jit(solution)/shard_map/grad_context/all_to_all | solution.py:1023
  172.4 3.5 %collective-permute-done.2.refs_1_ = bf16[256,1152]{1,0:T(8,128)(2,1)} collective-permute-done((bf16[256,1152]{1,0:T(8,128)(2,1)}, bf16[256,1152]{1,0:T(8,128)(2,1)}, u32[]{:S(2)}, u32[]{:S(2)}) %collective-permute-start.2) | collective-permute-done | bytes 589856 | tf_op jit(solution)/shard_map/packet/ppermute | solution.py:49
  175.9 9.9 %weight_grads.1.refs_0_ = bf16[384,7168]{1,0:T(8,128)(2,1)} custom-call(bf16[256,1152]{1,0:T(8,128)(2,1)} %get-tuple-element.65.refs_0_, bf16[256,1152]{1,0:T(8,128)(2,1)} %collective-permute-done.2.refs_1_, bf16[256,7168]{1,0:T(8,128)(2,1)} %get-tuple-element.67.refs_2_, bf16[256,7168]{1,0:T(8,128)(2,1)} %collective-permute-done.3.refs_3_), custom_call_target="tpu_custom_call" | custom-call | flops 10000000000 | tf_op jit(solution)/shard_map/back_grads/weight_grads/pallas_call | solution.py:726
  185.7 2.0 all-to-all-done.6.refs_1_.grad_ref
  187.8 0.8 copy-done.25
  188.6 0.5 broadcast_in_dim.20.refs_0_
  189.1 13.4 %attend_back.2 = (bf16[16,192,128]{2,1,0:T(8,128)(2,1)}, f32[1,128]{1,0:T(1,128)}) custom-call(bf16[16,192,128]{2,1,0:T(8,128)(2,1)} %all_to_all.67.taken_ref.refs_1_, bf16[16,64,256]{2,1,0:T(8,128)(2,1)} %copy-done.25, f32[64,2048]{1,0:T(8,128)} %get-tuple-element.53.refs_0_.context_ref, bf16[2048,2048]{1,0:T(8,128)(2,1)} %get-tuple-element.63.expo_ref, ...), custom_call_target="tpu_custom_call" | custom-call | flops 12999999488 | tf_op jit(solution)/shard_map/attend_back/pallas_call | solution.py:524
  202.6 4.0 %all-to-all-start.7 = ((bf16[16,192,128]{2,1,0:T(8,128)(2,1)}), bf16[16,192,128]{2,1,0:T(8,128)(2,1)S(1)}, u32[]{:S(2)}, u32[]{:S(2)}) async-start(bf16[16,192,128]{2,1,0:T(8,128)(2,1)} %get-tuple-element.68), calls=%async_computation.7 | async-start | bytes 1572864 | tf_op jit(solution)/shard_map/grad_qkv/all_to_all | solution.py:1045
  206.6 13.5 %attend_back.3 = (bf16[16,208,128]{2,1,0:T(8,128)(2,1)}, f32[1,128]{1,0:T(1,128)}) custom-call(bf16[16,192,128]{2,1,0:T(8,128)(2,1)} %copy-done.28, bf16[16,64,256]{2,1,0:T(8,128)(2,1)} %copy-done.25, f32[64,2048]{1,0:T(8,128)} %get-tuple-element.69.context_ref, bf16[2048,2048]{1,0:T(8,128)(2,1)} %get-tuple-element.70.expo_ref, ...), custom_call_target="tpu_custom_call" | custom-call | flops 12999999488 | tf_op jit(solution)/shard_map/attend_back/pallas_call | solution.py:524
  220.2 5.4 %all-to-all-done.7.refs_1_.refs_5_.refs_7_ = bf16[16,192,128]{2,1,0:T(8,128)(2,1)S(1)} async-done(((bf16[16,192,128]{2,1,0:T(8,128)(2,1)}), bf16[16,192,128]{2,1,0:T(8,128)(2,1)S(1)}, u32[]{:S(2)}, u32[]{:S(2)}) %all-to-all-start.7) | async-done | bytes 786464 | tf_op jit(solution)/shard_map/grad_qkv/all_to_all | solution.py:1045
  225.6 0.9 copy-done.4
  226.5 26.5 %all_to_all.69.refs_6_.refs_8_ = bf16[16,208,128]{2,1,0:T(8,128)(2,1)S(1)} all-to-all(bf16[16,208,128]{2,1,0:T(8,128)(2,1)} %tie.11), channel_id=1, replica_groups=mesh['rows'=2,'blk'=16] {'blk'}, dimensions={0} | all-to-all | bytes 1703936 | tf_op jit(solution)/shard_map/grad_qkv/all_to_all | solution.py:1045
  253.0 0.5 collective-permute-start.6
  253.6 0.5 collective-permute-start.5
  254.1 2.7 collective-permute-done.4.refs_3_
  257.0 1.1 copy-done.5
  258.2 2.4 front_grads.1.refs_9_.refs_1_
  260.6 1.2 copy-done.2
  261.8 4.0 %reduce-scatter.3.cloned.1.call-done.refs_0_ = bf16[96,7168]{1,0:T(8,128)(2,1)} async-done(((bf16[384,7168]{1,0:T(8,128)(2,1)}), bf16[96,7168]{1,0:T(8,128)(2,1)}) %reduce-scatter.3.cloned.1.call-update) | async-done | bytes 1376272 | tf_op jit(solution)/shard_map/back_grads/reduce_scatter | solution.py:180
  265.8 4.5 %all-to-all-start.9 = ((bf16[4,96,2304]{2,1,0:T(8,128)(2,1)}), bf16[4,96,2304]{2,1,0:T(8,128)(2,1)}, u32[]{:S(2)}, u32[]{:S(2)}) async-start(bf16[4,96,2304]{2,1,0:T(8,128)(2,1)} %bitcast.33), calls=%async_computation.9 | async-start | bytes 3538944 | tf_op jit(solution)/shard_map/front_grads/all_to_all | solution.py:103
  270.3 1.5 copy-done.3
  271.8 1.3 copy-done.9
  273.1 1.1 copy-done.11
  274.2 1.1 copy-done.22
  275.3 7.2 %input_grads.1.refs_1_ = f32[2,128,768]{2,1,0:T(8,128)} custom-call(s32[1]{0:T(128)} %bitcast.flipped_ref.refs_0_, bf16[768,768]{1,0:T(8,128)(2,1)S(1)} %copy-done.9, bf16[2,128,768]{2,1,0:T(8,128)(2,1)S(1)} %copy-done.11, bf16[384,2432]{1,0:T(8,128)(2,1)S(1)} %bitcast.32, bf16[384,2432]{1,0:T(8,128)(2,1)} %collective-permute-done.other_ref.refs_4_, ...), custom_call_target="tpu_custom_call" | custom-call | flops 6000000000 | tf_op jit(solution)/shard_map/input_grads/pallas_call | solution.py:852
  282.6 9.6 %all-to-all-done.9 = bf16[4,96,2304]{2,1,0:T(8,128)(2,1)} async-done(((bf16[4,96,2304]{2,1,0:T(8,128)(2,1)}), bf16[4,96,2304]{2,1,0:T(8,128)(2,1)}, u32[]{:S(2)}, u32[]{:S(2)}) %all-to-all-start.9) | async-done | bytes 1769504 | tf_op jit(solution)/shard_map/front_grads/all_to_all | solution.py:103
  292.2 2.6 reduce_sum.21.refs_0_
  294.8 4.4 %all-to-all-start.10 = ((bf16[4,24,2304]{2,1,0:T(8,128)(2,1)}), bf16[4,24,2304]{2,1,0:T(8,128)(2,1)S(1)}, u32[]{:S(2)}, u32[]{:S(2)}) async-start(bf16[4,24,2304]{2,1,0:T(8,128)(2,1)} %bitcast.40), calls=%async_computation.10 | async-start | bytes 884736 | tf_op jit(solution)/shard_map/front_grads/all_to_all | solution.py:103
  299.3 1.2 collective-permute-done.8
  300.5 0.6 bitcast_add_fusion
  301.1 1.0 copy-done.14
  302.1 0.9 unpack_back.1
  302.9 8.4 %all-to-all-done.10.parts_ref = bf16[4,24,2304]{2,1,0:T(8,128)(2,1)S(1)} async-done(((bf16[4,24,2304]{2,1,0:T(8,128)(2,1)}), bf16[4,24,2304]{2,1,0:T(8,128)(2,1)S(1)}, u32[]{:S(2)}, u32[]{:S(2)}) %all-to-all-start.10) | async-done | bytes 442400 | tf_op jit(solution)/shard_map/front_grads/all_to_all | solution.py:103
  311.3 0.9 copy-done.15
  312.3 0.7 unpack_front.1
  (78 shorter events, 1.1 us)
Async XLA Ops:
  8.9 19.6 %all-to-all-start = ((bf16[4,24,2432]{2,1,0:T(8,128)(2,1)}), bf16[4,24,2432]{2,1,0:T(8,128)(2,1)S(1)}, u32[]{:S(2)}, u32[]{:S(2)}) async-start(bf16[4,24,2432]{2,1,0:T(8,128)(2,1)} %pack.1), calls=%async_computation | async-start | bytes 933888 | tf_op jit(solution)/shard_map/weights/all_to_all | solution.py:103
  15.2 37.4 %all-gather.3.cloned.1.call-start = ((), (), s32[]{:S(2)}) async-start(), calls=%async_computation.13 | async-start | bytes 1658880 | tf_op jit(solution)/shard_map/weights/all_gather | solution.py:154
  29.8 25.5 %all-to-all-start.1 = ((bf16[4,96,2432]{2,1,0:T(8,128)(2,1)}), bf16[4,96,2432]{2,1,0:T(8,128)(2,1)S(1)}, u32[]{:S(2)}, u32[]{:S(2)}) async-start(bf16[4,96,2432]{2,1,0:T(8,128)(2,1)} %tile.10), calls=%async_computation.1 | async-start | bytes 3735552 | tf_op jit(solution)/shard_map/weights/all_to_all | solution.py:103
  33.5 23.1 %copy-start.29 = (bf16[32,12]{0,1:T(8,128)(2,1)S(1)}, bf16[32,12]{0,1:T(8,128)(2,1)}, u32[]{:S(2)}) copy-start(bf16[32,12]{0,1:T(8,128)(2,1)} %param.25) | copy-start | bytes 2308
  33.5 102.8 %all-gather.5.cloned.1.call-start = ((), (), s32[]{:S(2)}) async-start(), calls=%async_computation.14 | async-start | bytes 6635520 | tf_op jit(solution)/shard_map/weights/all_gather | solution.py:156
  55.3 1.3 copy-start
  56.6 4.2 %collective-permute-start = (bf16[384,2432]{1,0:T(8,128)(2,1)}, bf16[384,2432]{1,0:T(8,128)(2,1)}, u32[]{:S(2)}, u32[]{:S(2)}) collective-permute-start(bf16[384,2432]{1,0:T(8,128)(2,1)} %bitcast.30), channel_id=1, source_target_pairs={{0,16},{16,0},{1,17},{17,1},{2,18},{18,2},{3,19},{19,3},{4,20},{20... | collective-permute-start | bytes 5603336 | tf_op jit(solution)/shard_map/weights/ppermute | solution.py:49
  57.5 3.4 %copy-start.1 = (bf16[4,96,2432]{2,1,0:T(8,128)(2,1)S(1)}, bf16[4,96,2432]{2,1,0:T(8,128)(2,1)}, u32[]{:S(2)}) copy-start(bf16[4,96,2432]{2,1,0:T(8,128)(2,1)} %copy-done) | copy-start | bytes 5603332
  57.5 3.4 %copy-start.8 = (bf16[768,768]{1,0:T(8,128)(2,1)S(1)}, bf16[768,768]{1,0:T(8,128)(2,1)}, u32[]{:S(2)}) copy-start(bf16[768,768]{1,0:T(8,128)(2,1)} %constant.18.clone.matrix_ref.refs_1_) | copy-start | bytes 3538948
  57.5 3.4 %copy-start.23 = (bf16[2,1,128,768]{3,2,1,0:T(8,128)(2,1)S(1)}, bf16[2,1,128,768]{3,2,1,0:T(8,128)(2,1)}, u32[]{:S(2)}) copy-start(bf16[2,1,128,768]{3,2,1,0:T(8,128)(2,1)} %param.14) | copy-start | bytes 1179652
  60.9 1.2 copy-start.24
  66.3 0.9 copy-start.7
  67.2 25.3 %copy-start.10 = (bf16[2,128,768]{2,1,0:T(8,128)(2,1)}, bf16[2,128,768]{2,1,0:T(8,128)(2,1)S(1)}, u32[]{:S(2)}) copy-start(bf16[2,128,768]{2,1,0:T(8,128)(2,1)S(1)} %get-tuple-element.48.refs_2_) | copy-start | bytes 1179652
  67.2 25.3 %copy-start.19 = (f32[1,768]{1,0:T(1,128)}, f32[1,768]{1,0:T(1,128)S(1)}, u32[]{:S(2)}) copy-start(f32[1,768]{1,0:T(1,128)S(1)} %get-tuple-element.49.gain_ref) | copy-start | bytes 9220
  67.2 28.9 %copy-start.30 = (s32[2,1,6]{2,1,0:T(1,128)S(1)}, s32[2,1,6]{2,1,0:T(1,128)}, u32[]{:S(2)}) copy-start(s32[2,1,6]{2,1,0:T(1,128)} %param.15) | copy-start | bytes 148
  92.4 22.6 %all-to-all-start.4 = ((bf16[16,192,128]{2,1,0:T(8,128)(2,1)}), bf16[16,192,128]{2,1,0:T(8,128)(2,1)S(1)}, u32[]{:S(2)}, u32[]{:S(2)}) async-start(bf16[16,192,128]{2,1,0:T(8,128)(2,1)} %tie.7), calls=%async_computation.4 | async-start | bytes 1572864 | tf_op jit(solution)/shard_map/project/all_to_all | solution.py:999
  115.1 5.1 %copy-start.28 = (bf16[16,192,128]{2,1,0:T(8,128)(2,1)}, bf16[16,192,128]{2,1,0:T(8,128)(2,1)S(1)}, u32[]{:S(2)}) copy-start(bf16[16,192,128]{2,1,0:T(8,128)(2,1)S(1)} %all-to-all-done.4.taken_ref) | copy-start | bytes 2359300
  115.1 13.7 %all-to-all-start.3 = ((bf16[16,64,128]{2,1,0:T(8,128)(2,1)}), bf16[16,64,128]{2,1,0:T(8,128)(2,1)S(1)}, u32[]{:S(2)}, u32[]{:S(2)}) async-start(bf16[16,64,128]{2,1,0:T(8,128)(2,1)} %get-tuple-element.51), calls=%async_computation.3 | async-start | bytes 524288 | tf_op jit(solution)/shard_map/context/all_to_all | solution.py:1012
  128.8 0.7 copy-start.26
  136.3 1.0 copy-start.27
  136.3 15.7 %collective-permute-start.1 = (bf16[384,6912]{1,0:T(8,128)(2,1)}, bf16[384,6912]{1,0:T(8,128)(2,1)}, u32[]{:S(2)}, u32[]{:S(2)}) collective-permute-start(bf16[384,6912]{1,0:T(8,128)(2,1)} %tie.9.refs_2_.refs_4_.refs_6_.refs_8_), channel_id=1, source_target_pairs={{0,16},{16,0},{1,17},{17,1},{2,18},{18,2},{3,19},{19,3},{4,20},{20... | collective-permute-start | bytes 15925256 | tf_op jit(solution)/shard_map/weights/ppermute | solution.py:49
  168.2 7.7 %collective-permute-start.3 = (bf16[256,7168]{1,0:T(8,128)(2,1)}, bf16[256,7168]{1,0:T(8,128)(2,1)}, u32[]{:S(2)}, u32[]{:S(2)}) collective-permute-start(bf16[256,7168]{1,0:T(8,128)(2,1)} %get-tuple-element.67.refs_2_), channel_id=1, source_target_pairs={{0,16},{16,0},{1,17},{17,1},{2,18},{18,2},{3,19},{19,3},{4,20},{20... | collective-permute-start | bytes 11010056 | tf_op jit(solution)/shard_map/packet/ppermute | solution.py:49
  168.3 7.6 %collective-permute-start.2 = (bf16[256,1152]{1,0:T(8,128)(2,1)}, bf16[256,1152]{1,0:T(8,128)(2,1)}, u32[]{:S(2)}, u32[]{:S(2)}) collective-permute-start(bf16[256,1152]{1,0:T(8,128)(2,1)} %get-tuple-element.66), channel_id=1, source_target_pairs={{0,16},{16,0},{1,17},{17,1},{2,18},{18,2},{3,19},{19,3},{4,20},{20... | collective-permute-start | bytes 1769480 | tf_op jit(solution)/shard_map/packet/ppermute | solution.py:49
  168.8 19.0 %all-to-all-start.6 = ((bf16[16,64,256]{2,1,0:T(8,128)(2,1)}), bf16[16,64,256]{2,1,0:T(8,128)(2,1)S(1)}, u32[]{:S(2)}, u32[]{:S(2)}) async-start(bf16[16,64,256]{2,1,0:T(8,128)(2,1)} %get-tuple-element.62), calls=%async_computation.6 | async-start | bytes 1048576 | tf_op jit(solution)/shard_map/grad_context/all_to_all | solution.py:1023
  172.4 93.5 %reduce-scatter.3.cloned.1.call-start = ((), (), s32[]{:S(2)}) async-start(), calls=%async_computation.15 | async-start | bytes 6881280 | tf_op jit(solution)/shard_map/back_grads/reduce_scatter | solution.py:180
  187.8 0.8 copy-start.25
  202.6 23.0 %all-to-all-start.7 = ((bf16[16,192,128]{2,1,0:T(8,128)(2,1)}), bf16[16,192,128]{2,1,0:T(8,128)(2,1)S(1)}, u32[]{:S(2)}, u32[]{:S(2)}) async-start(bf16[16,192,128]{2,1,0:T(8,128)(2,1)} %get-tuple-element.68), calls=%async_computation.7 | async-start | bytes 1572864 | tf_op jit(solution)/shard_map/grad_qkv/all_to_all | solution.py:1045
  206.6 94.5 %reduce-scatter.5.cloned.1.call-start = ((), (), s32[]{:S(2)}) async-start(), calls=%async_computation.16 | async-start | bytes 1720320 | tf_op jit(solution)/shard_map/front_grads/reduce_scatter | solution.py:187
  225.6 0.9 copy-start.4
  253.0 4.1 %collective-permute-start.7 = (bf16[16,208,128]{2,1,0:T(8,128)(2,1)S(1)}, bf16[16,208,128]{2,1,0:T(8,128)(2,1)S(1)}, u32[]{:S(2)}, u32[]{:S(2)}) collective-permute-start(bf16[16,208,128]{2,1,0:T(8,128)(2,1)S(1)} %all_to_all.69.refs_6_.refs_8_), channel_id=1, source_target_pairs={{0,16},{16,0},{1,17},{17,1},{2,18},{18,2},{3,19},{19,3},{4,20},{20... | collective-permute-start | bytes 2555912 | tf_op jit(solution)/shard_map/front_grads/ppermute | solution.py:49
  253.0 4.1 %collective-permute-start.6 = (bf16[16,192,128]{2,1,0:T(8,128)(2,1)}, bf16[16,192,128]{2,1,0:T(8,128)(2,1)S(1)}, u32[]{:S(2)}, u32[]{:S(2)}) collective-permute-start(bf16[16,192,128]{2,1,0:T(8,128)(2,1)} %copy-done.4), channel_id=1, source_target_pairs={{0,16},{16,0},{1,17},{17,1},{2,18},{18,2},{3,19},{19,3},{4,20},{20... | collective-permute-start | bytes 2359304 | tf_op jit(solution)/shard_map/front_grads/ppermute | solution.py:49
  253.5 3.2 %collective-permute-start.4 = (bf16[128,768]{1,0:T(8,128)(2,1)S(1)}, bf16[128,768]{1,0:T(8,128)(2,1)S(1)}, u32[]{:S(2)}, u32[]{:S(2)}) collective-permute-start(bf16[128,768]{1,0:T(8,128)(2,1)S(1)} %get-tuple-element.109.refs_1_), channel_id=1, source_target_pairs={{0,16},{16,0},{1,17},{17,1},{2,18},{18,2},{3,19},{19,3},{4,20},{20... | collective-permute-start | bytes 589832 | tf_op jit(solution)/shard_map/front_grads/ppermute | solution.py:49
  253.6 3.4 %collective-permute-start.5 = (bf16[128,768]{1,0:T(8,128)(2,1)S(1)}, bf16[128,768]{1,0:T(8,128)(2,1)S(1)}, u32[]{:S(2)}, u32[]{:S(2)}) collective-permute-start(bf16[128,768]{1,0:T(8,128)(2,1)S(1)} %get-tuple-element.108.refs_2_), channel_id=1, source_target_pairs={{0,16},{16,0},{1,17},{17,1},{2,18},{18,2},{3,19},{19,3},{4,20},{20... | collective-permute-start | bytes 589832 | tf_op jit(solution)/shard_map/front_grads/ppermute | solution.py:49
  257.0 1.1 copy-start.5
  260.6 1.2 copy-start.2
  261.8 8.5 %copy-start.6 = (bf16[16,192,128]{2,1,0:T(8,128)(2,1)S(1)}, bf16[16,192,128]{2,1,0:T(8,128)(2,1)}, u32[]{:S(2)}) copy-start(bf16[16,192,128]{2,1,0:T(8,128)(2,1)} %copy-done.4) | copy-start | bytes 2359300
  265.8 26.3 %all-to-all-start.9 = ((bf16[4,96,2304]{2,1,0:T(8,128)(2,1)}), bf16[4,96,2304]{2,1,0:T(8,128)(2,1)}, u32[]{:S(2)}, u32[]{:S(2)}) async-start(bf16[4,96,2304]{2,1,0:T(8,128)(2,1)} %bitcast.33), calls=%async_computation.9 | async-start | bytes 3538944 | tf_op jit(solution)/shard_map/front_grads/all_to_all | solution.py:103
  270.3 1.5 copy-start.3
  271.8 1.3 copy-start.9
  273.1 1.1 copy-start.11
  274.2 1.1 copy-start.22
  282.5 18.6 %copy-start.12 = (bf16[24,2048]{1,0:T(8,128)(2,1)S(1)}, bf16[24,2048]{1,0:T(8,128)(2,1)}, u32[]{:S(2)}) copy-start(bf16[24,2048]{1,0:T(8,128)(2,1)} %up_ref.1) | copy-start | bytes 294916
  282.5 18.6 %copy-start.13 = (bf16[24,2048]{1,0:T(8,128)(2,1)S(1)}, bf16[24,2048]{1,0:T(8,128)(2,1)}, u32[]{:S(2)}) copy-start(bf16[24,2048]{1,0:T(8,128)(2,1)} %gate_ref.1) | copy-start | bytes 294916
  282.5 18.6 %copy-start.20 = (bf16[24]{0:T(256)(128)(2,1)S(1)}, bf16[24]{0:T(256)(128)(2,1)}, u32[]{:S(2)}) copy-start(bf16[24]{0:T(256)(128)(2,1)} %param.21) | copy-start | bytes 148
  282.5 28.8 %copy-start.16 = (bf16[24,768]{1,0:T(8,128)(2,1)S(1)}, bf16[24,768]{1,0:T(8,128)(2,1)}, u32[]{:S(2)}) copy-start(bf16[24,768]{1,0:T(8,128)(2,1)} %query_ref.3) | copy-start | bytes 110596
  282.5 28.8 %copy-start.17 = (bf16[24,768]{1,0:T(8,128)(2,1)S(1)}, bf16[24,768]{1,0:T(8,128)(2,1)}, u32[]{:S(2)}) copy-start(bf16[24,768]{1,0:T(8,128)(2,1)} %key_ref.3) | copy-start | bytes 110596
  282.5 28.8 %copy-start.18 = (bf16[24,768]{1,0:T(8,128)(2,1)S(1)}, bf16[24,768]{1,0:T(8,128)(2,1)}, u32[]{:S(2)}) copy-start(bf16[24,768]{1,0:T(8,128)(2,1)} %value_ref.3) | copy-start | bytes 110596
  282.6 28.8 %copy-start.21 = (bf16[24]{0:T(256)(128)(2,1)S(1)}, bf16[24]{0:T(256)(128)(2,1)}, u32[]{:S(2)}) copy-start(bf16[24]{0:T(256)(128)(2,1)} %param.16) | copy-start | bytes 148
  294.8 16.5 %all-to-all-start.10 = ((bf16[4,24,2304]{2,1,0:T(8,128)(2,1)}), bf16[4,24,2304]{2,1,0:T(8,128)(2,1)S(1)}, u32[]{:S(2)}, u32[]{:S(2)}) async-start(bf16[4,24,2304]{2,1,0:T(8,128)(2,1)} %bitcast.40), calls=%async_computation.10 | async-start | bytes 884736 | tf_op jit(solution)/shard_map/front_grads/all_to_all | solution.py:103
  299.2 1.2 collective-permute-start.8
  301.1 1.0 copy-start.14
  311.3 0.9 copy-start.15
Sparse Core Ops, SparseCore 0:
  18.1 34.4 all-gather.2
  56.7 78.6 all-gather.4
  188.7 77.0 reduce-scatter.2
  268.0 31.9 reduce-scatter.4

commit v4 on v3

--- a/solution.py
+++ b/solution.py
@@ -563,10 +563,9 @@
     contexts, refs = refs[:micro], refs[micro:]
     outs, gates, ups, downs = (refs[2 * k : 2 * k + 2] for k in range(4))
     (
-        result_ref, grad_mid_ref, grad_context_ref, packet_ref, left_ref, other_left_ref,
+        result_ref, grad_mid_ref, grad_context_ref, packet_ref, heard_ref, left_ref, other_left_ref,
         normed_ref, branch_ref, cot_ref, mid_ref, total_ref, grad_ref,
-    ) = refs[-12:]
-    units = steps * feed_chunk
+    ) = refs[-13:]
     j = pl.program_id(0)
     size = contexts[0].shape[1]
     sides = side(flipped_ref[0], hidden_ref.shape[1] // 2)
@@ -579,7 +578,7 @@
         context = jnp.concatenate(
             [ref[...].reshape(-1, ref.shape[2]).astype(f32).T for ref in contexts], axis=0
         ).astype(bf16)
-        packet_ref[:, 3 * units :] = context
+        heard_ref[...] = context
         context = context[:, : heads * size]
         for lanes, ref in zip(sides, outs):
             mid_ref[:, lanes] = dot_on(context, ref[...], 1, 1)
@@ -611,9 +610,7 @@
     grad_gate = (grad_inner * up * gelu_grad).astype(bf16)
     grad_up = (grad_inner * gelu).astype(bf16)
     for k, part in enumerate((grad_gate, grad_up, inner)):
-        packet_ref[
-            :, pl.ds(pl.multiple_of(k * units + j * feed_chunk, feed_chunk), feed_chunk)
-        ] = part
+        packet_ref[k] = part
     for k, lanes in enumerate(sides):
         total_ref[:, lanes] = total_ref[:, lanes] + dot_on(inner, downs[k][...], 1, 1)
         grad_ref[:, lanes] = (
@@ -654,7 +651,6 @@
     assert 3 * units % inner_width == 0
     whole = lambda *shape: pl.BlockSpec(shape, lambda j: (0,) * len(shape))
     column = lambda offset: pl.BlockSpec((width // 2, feed_chunk), lambda j: (0, offset + j))
-    packet = 3 * units + blocks * size
     spot = 3 * units // inner_width
     weight_specs = [pl.BlockSpec((width // 2, inner_width), lambda j: (0, spot))] * 2
     for k in range(3):
@@ -676,7 +672,8 @@
             whole(tok, width),
             whole(tok, width),
             whole(blocks, size, tok),
-            whole(tok, packet),
+            pl.BlockSpec((3, tok, feed_chunk), lambda j: (0, 0, j)),
+            whole(tok, blocks * size),
             whole(tok, 3 * (width // 2)),
             whole(tok, 3 * (width // 2)),
         ],
@@ -684,7 +681,8 @@
             jax.ShapeDtypeStruct((tok, width), bf16),
             jax.ShapeDtypeStruct((tok, width), f32),
             jax.ShapeDtypeStruct((blocks, size, tok), bf16),
-            jax.ShapeDtypeStruct((tok, packet), bf16),
+            jax.ShapeDtypeStruct((3, tok, units), bf16),
+            jax.ShapeDtypeStruct((tok, blocks * size), bf16),
             jax.ShapeDtypeStruct((tok, 3 * (width // 2)), bf16),
             jax.ShapeDtypeStruct((tok, 3 * (width // 2)), bf16),
         ],
@@ -704,7 +702,7 @@
 def weight_grad_kernel(counts, parts, half, *refs):
     j = pl.program_id(0)
     out_ref, tall_ref = refs[-2:]
-    lefts, rights = refs[:parts], refs[parts : 2 * parts]
+    lefts, packets, heard = (refs[k * parts : (k + 1) * parts] for k in range(3))
     start = 0
     for k, count in counts:
 
@@ -713,29 +711,45 @@
             store_tall(tall_ref, [ref[:, k * half : (k + 1) * half] for ref in lefts])
 
         start += count
-    right = jnp.concatenate([ref[...] for ref in rights], axis=0)
-    out_ref[...] = jnp.dot(tall_ref[...], right, preferred_element_type=f32).astype(bf16)
-
-
-def weight_grads(lefts, rights, half, units, inner_width, *after):
-    tok, block = lefts[0].shape[0], grad_chunk
-    steps = units // block
-    counts = [(0, 2 * steps), (1, steps), (2, inner_width // block)]
-    total = 3 * steps + inner_width // block
-    anywhere = pl.BlockSpec(memory_space=pl.ANY)
+
+    def product(rights):
+        right = jnp.concatenate([ref[...] for ref in rights], axis=0)
+        out_ref[...] = jnp.dot(tall_ref[...], right, preferred_element_type=f32).astype(bf16)
+
+    @pl.when(j < start - counts[-1][1])
+    def _():
+        product(packets)
+
+    @pl.when(j >= start - counts[-1][1])
+    def _():
+        product(heard)
+
+
+def weight_grads(lefts, packets, heard, inner_width, *after):
+    tok, half = lefts[0].shape[0], lefts[0].shape[1] // 3
+    block = grad_chunk
+    units, wide = packets[0].shape[2], heard[0].shape[1]
+    steps, more = units // block, wide // block
+    counts = [(0, 2 * steps), (1, steps), (2, more)]
+    place = lambda j: jnp.minimum(j, 3 * steps - 1)
     return pl.pallas_call(
         functools.partial(weight_grad_kernel, counts, len(lefts), half),
-        grid=(total,),
+        grid=(3 * steps + more,),
         in_specs=[pl.BlockSpec((tok, 3 * half), lambda j: (0, 0))] * len(lefts)
-        + [pl.BlockSpec((tok, block), lambda j: (0, j))] * len(rights)
-        + [anywhere] * len(after),
+        + [
+            pl.BlockSpec((None, tok, block), lambda j: (place(j) // steps, 0, place(j) % steps))
+        ]
+        * len(packets)
+        + [pl.BlockSpec((tok, block), lambda j: (0, jnp.clip(j - 3 * steps, 0, more - 1)))]
+        * len(heard)
+        + [pl.BlockSpec(memory_space=pl.ANY)] * len(after),
         out_specs=pl.BlockSpec((half, block), lambda j: (0, j)),
-        out_shape=jax.ShapeDtypeStruct((half, total * block), bf16),
+        out_shape=jax.ShapeDtypeStruct((half, 3 * units + inner_width), bf16),
         scratch_shapes=[pltpu.VMEM((half, len(lefts) * tok), bf16)],
         compiler_params=pltpu.CompilerParams(vmem_limit_bytes=vmem_bytes),
         cost_estimate=cost(10),
         name="weight_grads",
-    )(*lefts, *rights, *after)
+    )(*lefts, *packets, *heard, *after)
 
 
 def project_kernel(
@@ -859,7 +873,7 @@
             pltpu.VMEM((width, micro * tok), f32),
             pltpu.VMEM((3 * inner_width, micro * tok), bf16),
         ],
-        compiler_params=pltpu.CompilerParams(vmem_limit_bytes=few_bytes),
+        compiler_params=pltpu.CompilerParams(vmem_limit_bytes=vmem_bytes),
         cost_estimate=cost(6),
         name="input_grads",
     )(flipped, matrix, inputs, *weights, gains, mid, *grads, *after)
@@ -1015,7 +1029,7 @@
 
     fits = staged(rows, blocks, share)
     here = micro * tok
-    result, grad_mid, grad_context, mine, left, left_other = feed(
+    result, grad_mid, grad_context, mine, heard, left, left_other = feed(
         flipped, matrix, tokens.reshape(here, width), contexts,
         cotangent[:, 0].reshape(here, width), gain_f, back_full, heads,
     )
@@ -1023,17 +1037,17 @@
         grads = lax.all_to_all(grad_context, "blk", 0, 0, tiled=True)
     if fits:
         with jax.named_scope("packet"):
-            packet, near_left = flip(mine, "rows", 1), flip(left_other, "rows", 1)
-
-    wide = blocks * size
+            packet, near_heard, near_left = (flip(a, "rows", 1) for a in (mine, heard, left_other))
+
     with jax.named_scope("back_grads"):
-        sizes = width // 2, hidden_units, wide
         if fits:
-            parts = [left, near_left], [mine, packet]
-            own = tie(weight_grads(*parts, *sizes), grads)
+            own = weight_grads([left, near_left], [mine, packet], [heard, near_heard], inner_width)
+            own = tie(own, grads)
             back_grad = scatter_back(own)
         else:
-            own, other = (weight_grads([lefts], [mine], *sizes) for lefts in (left, left_other))
+            own, other = (
+                weight_grads([lefts], [mine], [heard], inner_width) for lefts in (left, left_other)
+            )
             back_grad = scatter_whole(own, other)
     grad_qkv, found = [], jnp.zeros((1, chunk // 2), f32)
     for m in micros:

time: 321 us -> 314 us (0.978)
  local copies, waits for them, and re-layouts: 19.2 us -> 13.5 us
    unnamed x62 -> x58, local copies, waits for them, and re-layouts: 15.9 us -> 10.3 us
    reduce_scatter x1, waiting for transfers between devices: 3.97 us -> 0.01 us  [scatter_back(): lax.psum_scatter(own, 'blk', scatter_dimension=0, axis_index_groups=withi...]
    ppermute x9 -> x10, waiting for transfers between devices: 8.93 us -> 8.84 us  [flip(): return lax.ppermute(array, axis, [(i, i ^ bit) for i in range(count)])]
  transfers between devices with their start and end apart: 21 -> 22, of which waited for: 15 -> 15; matrix products, arithmetic and copies ran while one was open for 3% -> 2% of each run, Pallas kernels for 24% -> 26%
where the time goes in v4:
time: 314 us; the launch traced here: 312 us
  Pallas kernels  98.2 us (31%)
  waiting for transfers between devices  79.6 us (25%)
  blocking collectives  66.6 us (21%)
  starting transfers between devices  36 us (11%)
  between operations  14 us (4%)
  local copies, waits for them, and re-layouts  13.5 us (4%)
  other arithmetic  4.28 us (1%)
    all_to_all x4, waiting for transfers between devices, exchange(): lax.all_to_all(array, 'blk', 0, 0, tiled=True, axis_index_groups=groups)  35.1 us
    pallas_call x2, Pallas kernels, attend_back(): pl.pallas_call(functools.partial(attend_back_kernel, size, blocks, bucket...  27.1 us
    all_to_all x1, blocking collectives, body(): grad_qkv.append(lax.all_to_all(returned, 'blk', 0, 0, tiled=True))  26.5 us
    all_to_all x1, blocking collectives, body(): taken.append(lax.all_to_all(part, 'blk', 0, 0, tiled=True))  25.3 us
    pallas_call x3, Pallas kernels, attend(): pl.pallas_call(functools.partial(attend_kernel, size, blocks, lengths.sha...  24.4 us
    all_gather x1, waiting for transfers between devices, gather_back(): lax.all_gather(shard, 'blk', axis=0, tiled=True, axis_index_groups=across)  19.1 us
    all_to_all x4, starting transfers between devices, exchange(): lax.all_to_all(array, 'blk', 0, 0, tiled=True, axis_index_groups=groups)  17.3 us
    pallas_call x1, Pallas kernels, feed(): pl.pallas_call(functools.partial(feed_kernel, heads, steps, micro), grid=...  15.1 us
  transfers between devices with their start and end apart: 22, of which 15 were waited for; matrix products, arithmetic and copies ran while one was open for 2% of the time, Pallas kernels for 26%

profile of v4, /device:TPU:0, one launch (start us, length us, event | category | flops | bytes accessed | tf_op | source)
XLA Modules:
  0.0 312.2 jit_solution(14481703560496414380)
XLA Ops:
  7.2 1.7 pack.1
  8.9 6.3 %all-to-all-start = ((bf16[4,24,2432]{2,1,0:T(8,128)(2,1)}), bf16[4,24,2432]{2,1,0:T(8,128)(2,1)S(1)}, u32[]{:S(2)}, u32[]{:S(2)}) async-start(bf16[4,24,2432]{2,1,0:T(8,128)(2,1)} %pack.1), calls=%async_computation | async-start | bytes 933888 | tf_op jit(solution)/shard_map/weights/all_to_all | solution.py:103
  15.2 1.8 pad_maximum_fusion
  17.0 11.5 %all-to-all-done = bf16[4,24,2432]{2,1,0:T(8,128)(2,1)S(1)} async-done(((bf16[4,24,2432]{2,1,0:T(8,128)(2,1)}), bf16[4,24,2432]{2,1,0:T(8,128)(2,1)S(1)}, u32[]{:S(2)}, u32[]{:S(2)}) %all-to-all-start) | async-done | bytes 466976 | tf_op jit(solution)/shard_map/weights/all_to_all | solution.py:103
  28.4 1.4 tile.10
  29.8 3.7 %all-to-all-start.1 = ((bf16[4,96,2432]{2,1,0:T(8,128)(2,1)}), bf16[4,96,2432]{2,1,0:T(8,128)(2,1)S(1)}, u32[]{:S(2)}, u32[]{:S(2)}) async-start(bf16[4,96,2432]{2,1,0:T(8,128)(2,1)} %tile.10), calls=%async_computation.1 | async-start | bytes 3735552 | tf_op jit(solution)/shard_map/weights/all_to_all | solution.py:103
  33.6 19.1 %all-gather.3.cloned.1.call-done.refs_0_ = bf16[96,6912]{1,0:T(8,128)(2,1)} async-done(((bf16[24,6912]{1,0:T(8,128)(2,1)}), bf16[96,6912]{1,0:T(8,128)(2,1)}) %all-gather.3.cloned.1.call-update) | async-done | bytes 1327120 | tf_op jit(solution)/shard_map/weights/all_gather | solution.py:154
  52.6 2.7 all-to-all-done.1
  55.3 1.3 copy-done
  56.7 0.1 copy.39
  56.8 0.7 reshape.64.table_ref
  57.5 2.0 bias_tiles.1.after_ref.band_ref
  59.5 1.4 collective-permute-done.other_ref.refs_4_
  60.9 1.2 copy-done.19
  62.1 4.2 %project.1 = (bf16[16,192,128]{2,1,0:T(8,128)(2,1)S(1)}, bf16[16,192,128]{2,1,0:T(8,128)(2,1)S(1)}, bf16[2,128,768]{2,1,0:T(8,128)(2,1)S(1)}, bf16[256,768]{1,0:...) custom-call(s32[1]{0:T(128)} %bitcast.flipped_ref.refs_0_, bf16[768,768]{1,0:T(8,128)(2,1)S(1)} %copy-done.5, ...), custom_call_target="tpu_custom_call" | custom-call | flops 3000000000 | tf_op jit(solution)/shard_map/project/pallas_call | solution.py:797
  66.3 0.9 copy-done.4
  67.2 25.3 %all_to_all.67.taken_ref.refs_1_ = bf16[16,192,128]{2,1,0:T(8,128)(2,1)} all-to-all(bf16[16,192,128]{2,1,0:T(8,128)(2,1)S(1)} %get-tuple-element.51), channel_id=1, replica_groups=mesh['rows'=2,'blk'=16] {'blk'}, dimensions={0} | all-to-all | bytes 1572864 | tf_op jit(solution)/shard_map/project/all_to_all | solution.py:1013
  92.5 3.6 %all-to-all-start.4 = ((bf16[16,192,128]{2,1,0:T(8,128)(2,1)}), bf16[16,192,128]{2,1,0:T(8,128)(2,1)S(1)}, u32[]{:S(2)}, u32[]{:S(2)}) async-start(bf16[16,192,128]{2,1,0:T(8,128)(2,1)} %tie.7), calls=%async_computation.4 | async-start | bytes 1572864 | tf_op jit(solution)/shard_map/project/all_to_all | solution.py:1013
  96.2 0.5 slice_bitcast_fusion
  96.7 10.7 %attend.3 = (bf16[16,64,128]{2,1,0:T(8,128)(2,1)}, f32[64,2048]{1,0:T(8,128)}, bf16[2048,2048]{1,0:T(8,128)(2,1)}, f32[1,2048]{1,0:T(1,128)}) custom-call(s32[6]{0:T(128)} %get-tuple-element.113.bounds_ref, s32[1]{0:T(128)} %bitcast.6.head_ref, f32[384]{0:T(512)} %reshape.64.table_ref, bf16[16,192,128]{2,1,0:T(8,128)(2,1)} %all_to_all.67.taken_ref.refs_1_, ...), custom_call_target="tpu_custom_call" | custom-call | flops 6000000000 | tf_op jit(solution)/shard_map/attend/pallas_call | solution.py:397
  107.4 7.7 %all-to-all-done.4.taken_ref = bf16[16,192,128]{2,1,0:T(8,128)(2,1)S(1)} async-done(((bf16[16,192,128]{2,1,0:T(8,128)(2,1)}), bf16[16,192,128]{2,1,0:T(8,128)(2,1)S(1)}, u32[]{:S(2)}, u32[]{:S(2)}) %all-to-all-start.4) | async-done | bytes 786464 | tf_op jit(solution)/shard_map/project/all_to_all | solution.py:1013
  115.2 5.1 %all-to-all-start.3 = ((bf16[16,64,128]{2,1,0:T(8,128)(2,1)}), bf16[16,64,128]{2,1,0:T(8,128)(2,1)S(1)}, u32[]{:S(2)}, u32[]{:S(2)}) async-start(bf16[16,64,128]{2,1,0:T(8,128)(2,1)} %get-tuple-element.52), calls=%async_computation.3 | async-start | bytes 524288 | tf_op jit(solution)/shard_map/context/all_to_all | solution.py:1026
  120.3 6.9 %attend.4 = (bf16[16,64,128]{2,1,0:T(8,128)(2,1)}, f32[64,2048]{1,0:T(8,128)}, bf16[2048,2048]{1,0:T(8,128)(2,1)}, f32[1,2048]{1,0:T(1,128)}) custom-call(s32[6]{0:T(128)} %get-tuple-element.112.bounds_ref, s32[1]{0:T(128)} %bitcast.6.head_ref, f32[384]{0:T(512)} %reshape.64.table_ref, bf16[16,192,128]{2,1,0:T(8,128)(2,1)} %copy-done.24, ...), custom_call_target="tpu_custom_call" | custom-call | flops 6000000000 | tf_op jit(solution)/shard_map/attend/pallas_call | solution.py:397
  127.2 1.7 all-to-all-done.3.refs_4_.refs_0_
  128.9 0.7 copy-done.22
  129.6 6.8 %attend.5 = (bf16[16,64,128]{2,1,0:T(8,128)(2,1)}, f32[64,2048]{1,0:T(8,128)}, bf16[2048,2048]{1,0:T(8,128)(2,1)}, f32[1,2048]{1,0:T(1,128)}) custom-call(s32[6]{0:T(128)} %get-tuple-element.112.bounds_ref, s32[1]{0:T(128)} %bitcast.6.head_ref, f32[384]{0:T(512)} %reshape.64.table_ref, ...), custom_call_target="tpu_custom_call", output_to_operand_aliasing={{0}: (5, {}), {1}: (6, {}), {2}: (7, {}), {3}: (8, {})} | custom-call | flops 6000000000 | tf_op jit(solution)/shard_map/attend/pallas_call | solution.py:397
  136.5 0.9 copy-done.23
  137.3 14.8 %all_to_all.68.refs_1_ = bf16[16,64,128]{2,1,0:T(8,128)(2,1)} all-to-all(bf16[16,64,128]{2,1,0:T(8,128)(2,1)S(1)} %copy-done.23), channel_id=1, replica_groups=mesh['rows'=2,'blk'=16] {'blk'}, dimensions={0} | all-to-all | bytes 524288 | tf_op jit(solution)/shard_map/context/all_to_all | solution.py:1026
  152.1 15.1 %feed.1 = (bf16[256,768]{1,0:T(8,128)(2,1)}, f32[256,768]{1,0:T(8,128)}, bf16[16,64,256]{2,1,0:T(8,128)(2,1)}, bf16[3,256,2048]{2,1,0:T(8,128)(2,1)}, bf16[256,1...) custom-call(s32[1]{0:T(128)} %bitcast.flipped_ref.refs_0_, ...), custom_call_target="tpu_custom_call" | custom-call | flops 8000000000 | tf_op jit(solution)/shard_map/feed/pallas_call | solution.py:658
  167.2 0.5 collective-permute-start.2
  167.8 3.6 %all-to-all-start.6 = ((bf16[16,64,256]{2,1,0:T(8,128)(2,1)}), bf16[16,64,256]{2,1,0:T(8,128)(2,1)S(1)}, u32[]{:S(2)}, u32[]{:S(2)}) async-start(bf16[16,64,256]{2,1,0:T(8,128)(2,1)} %get-tuple-element.63), calls=%async_computation.6 | async-start | bytes 1048576 | tf_op jit(solution)/shard_map/grad_context/all_to_all | solution.py:1037
  171.4 2.9 collective-permute-done.4.refs_5_
  174.3 0.5 collective-permute-done.3.refs_3_
  174.8 0.3 copy-done.28
  175.1 0.2 copy-done.27
  175.3 9.8 %weight_grads.1.refs_0_ = bf16[384,6912]{1,0:T(8,128)(2,1)} custom-call(bf16[256,1152]{1,0:T(8,128)(2,1)} %get-tuple-element.66.refs_0_, bf16[256,1152]{1,0:T(8,128)(2,1)} %copy-done.27, bf16[3,256,2048]{2,1,0:T(8,128)(2,1)} %get-tuple-element.68.refs_2_, bf16[3,256,2048]{2,1,0:T(8,128)(2,1)} %collective-permute-done.3.refs_3_, ...), custom_call_target="tpu_custom_call" | custom-call | flops 10000000000 | tf_op jit(solution)/shard_map/back_grads/weight_grads/pallas_call | solution.py:735
  185.1 1.7 all-to-all-done.6.refs_1_.grad_ref
  186.8 0.8 copy-done.21
  187.7 0.5 broadcast_in_dim.20.refs_0_
  188.2 13.4 %attend_back.2 = (bf16[16,192,128]{2,1,0:T(8,128)(2,1)}, f32[1,128]{1,0:T(1,128)}) custom-call(bf16[16,192,128]{2,1,0:T(8,128)(2,1)} %all_to_all.67.taken_ref.refs_1_, bf16[16,64,256]{2,1,0:T(8,128)(2,1)} %copy-done.21, f32[64,2048]{1,0:T(8,128)} %get-tuple-element.54.refs_0_.context_ref, bf16[2048,2048]{1,0:T(8,128)(2,1)} %get-tuple-element.64.expo_ref, ...), custom_call_target="tpu_custom_call" | custom-call | flops 12999999488 | tf_op jit(solution)/shard_map/attend_back/pallas_call | solution.py:524
  201.6 4.4 %all-to-all-start.7 = ((bf16[16,192,128]{2,1,0:T(8,128)(2,1)}), bf16[16,192,128]{2,1,0:T(8,128)(2,1)S(1)}, u32[]{:S(2)}, u32[]{:S(2)}) async-start(bf16[16,192,128]{2,1,0:T(8,128)(2,1)} %get-tuple-element.70), calls=%async_computation.7 | async-start | bytes 1572864 | tf_op jit(solution)/shard_map/grad_qkv/all_to_all | solution.py:1059
  206.1 13.7 %attend_back.3 = (bf16[16,208,128]{2,1,0:T(8,128)(2,1)}, f32[1,128]{1,0:T(1,128)}) custom-call(bf16[16,192,128]{2,1,0:T(8,128)(2,1)} %copy-done.24, bf16[16,64,256]{2,1,0:T(8,128)(2,1)} %copy-done.21, f32[64,2048]{1,0:T(8,128)} %get-tuple-element.71.context_ref, bf16[2048,2048]{1,0:T(8,128)(2,1)} %get-tuple-element.72.expo_ref, ...), custom_call_target="tpu_custom_call" | custom-call | flops 12999999488 | tf_op jit(solution)/shard_map/attend_back/pallas_call | solution.py:524
  219.8 5.4 %all-to-all-done.7.refs_1_.refs_5_.refs_7_ = bf16[16,192,128]{2,1,0:T(8,128)(2,1)S(1)} async-done(((bf16[16,192,128]{2,1,0:T(8,128)(2,1)}), bf16[16,192,128]{2,1,0:T(8,128)(2,1)S(1)}, u32[]{:S(2)}, u32[]{:S(2)}) %all-to-all-start.7) | async-done | bytes 786464 | tf_op jit(solution)/shard_map/grad_qkv/all_to_all | solution.py:1059
  225.2 0.9 copy-done.2
  226.1 26.5 %all_to_all.69.refs_6_.refs_8_ = bf16[16,208,128]{2,1,0:T(8,128)(2,1)S(1)} all-to-all(bf16[16,208,128]{2,1,0:T(8,128)(2,1)} %tie.11), channel_id=1, replica_groups=mesh['rows'=2,'blk'=16] {'blk'}, dimensions={0} | all-to-all | bytes 1703936 | tf_op jit(solution)/shard_map/grad_qkv/all_to_all | solution.py:1059
  252.6 0.5 collective-permute-start.7
  253.2 0.5 collective-permute-start.6
  253.7 2.7 collective-permute-done.5.refs_3_
  256.4 0.3 collective-permute-done.6.refs_4_
  256.7 1.2 copy-done.3
  257.8 3.4 %front_grads.1.refs_9_.refs_1_ = bf16[384,2304]{1,0:T(8,128)(2,1)} custom-call(s32[1]{0:T(128)} %bitcast.flipped_ref.refs_0_, bf16[128,768]{1,0:T(8,128)(2,1)S(1)} %get-tuple-element.111.refs_1_, bf16[128,768]{1,0:T(8,128)(2,1)S(1)} %get-tuple-element.110.refs_2_, bf16[128,768]{1,0:T(8,128)(2,1)S(1)} %collective-permute-done.5.refs_3_, ...), custom_call_target="tpu_custom_call" | custom-call | flops 5000000000 | tf_op jit(solution)/shard_map/front_grads/front_grads/pallas_call | solution.py:904
  261.2 3.6 %all-to-all-start.9 = ((bf16[4,96,2304]{2,1,0:T(8,128)(2,1)}), bf16[4,96,2304]{2,1,0:T(8,128)(2,1)S(1)}, u32[]{:S(2)}, u32[]{:S(2)}) async-start(bf16[4,96,2304]{2,1,0:T(8,128)(2,1)} %bitcast.17), calls=%async_computation.9 | async-start | bytes 3538944 | tf_op jit(solution)/shard_map/front_grads/all_to_all | solution.py:103
  264.8 8.9 %input_grads.1.refs_1_ = f32[2,128,768]{2,1,0:T(8,128)} custom-call(s32[1]{0:T(128)} %bitcast.flipped_ref.refs_0_, bf16[768,768]{1,0:T(8,128)(2,1)} %constant.18.clone.matrix_ref.refs_1_, bf16[2,128,768]{2,1,0:T(8,128)(2,1)} %copy-done.7, bf16[384,2432]{1,0:T(8,128)(2,1)} %bitcast.31, bf16[384,2432]{1,0:T(8,128)(2,1)} %collective-permute-done.other_ref.refs_4_, ...), custom_call_target="tpu_custom_call" | custom-call | flops 6000000000 | tf_op jit(solution)/shard_map/input_grads/pallas_call | solution.py:866
  273.8 13.0 %all-to-all-done.9 = bf16[4,96,2304]{2,1,0:T(8,128)(2,1)S(1)} async-done(((bf16[4,96,2304]{2,1,0:T(8,128)(2,1)}), bf16[4,96,2304]{2,1,0:T(8,128)(2,1)S(1)}, u32[]{:S(2)}, u32[]{:S(2)}) %all-to-all-start.9) | async-done | bytes 1769504 | tf_op jit(solution)/shard_map/front_grads/all_to_all | solution.py:103
  286.8 1.2 reduce_sum.21.refs_0_
  287.9 3.7 %all-to-all-start.10 = ((bf16[4,24,2304]{2,1,0:T(8,128)(2,1)}), bf16[4,24,2304]{2,1,0:T(8,128)(2,1)S(1)}, u32[]{:S(2)}, u32[]{:S(2)}) async-start(bf16[4,24,2304]{2,1,0:T(8,128)(2,1)} %bitcast.39), calls=%async_computation.10 | async-start | bytes 884736 | tf_op jit(solution)/shard_map/front_grads/all_to_all | solution.py:103
  291.6 0.8 convert_reduce_fusion
  292.4 1.2 collective-permute-done.9
  293.6 0.6 bitcast_add_fusion
  294.2 1.0 copy-done.10
  295.2 0.9 unpack_back.1
  296.1 8.0 %all-to-all-done.10.parts_ref = bf16[4,24,2304]{2,1,0:T(8,128)(2,1)S(1)} async-done(((bf16[4,24,2304]{2,1,0:T(8,128)(2,1)}), bf16[4,24,2304]{2,1,0:T(8,128)(2,1)S(1)}, u32[]{:S(2)}, u32[]{:S(2)}) %all-to-all-start.10) | async-done | bytes 442400 | tf_op jit(solution)/shard_map/front_grads/all_to_all | solution.py:103
  304.0 0.9 copy-done.11
  305.0 0.7 unpack_front.1
  (76 shorter events, 0.7 us)
Async XLA Ops:
  8.9 19.6 %all-to-all-start = ((bf16[4,24,2432]{2,1,0:T(8,128)(2,1)}), bf16[4,24,2432]{2,1,0:T(8,128)(2,1)S(1)}, u32[]{:S(2)}, u32[]{:S(2)}) async-start(bf16[4,24,2432]{2,1,0:T(8,128)(2,1)} %pack.1), calls=%async_computation | async-start | bytes 933888 | tf_op jit(solution)/shard_map/weights/all_to_all | solution.py:103
  15.2 37.4 %all-gather.3.cloned.1.call-start = ((), (), s32[]{:S(2)}) async-start(), calls=%async_computation.13 | async-start | bytes 1658880 | tf_op jit(solution)/shard_map/weights/all_gather | solution.py:154
  29.8 25.5 %all-to-all-start.1 = ((bf16[4,96,2432]{2,1,0:T(8,128)(2,1)}), bf16[4,96,2432]{2,1,0:T(8,128)(2,1)S(1)}, u32[]{:S(2)}, u32[]{:S(2)}) async-start(bf16[4,96,2432]{2,1,0:T(8,128)(2,1)} %tile.10), calls=%async_computation.1 | async-start | bytes 3735552 | tf_op jit(solution)/shard_map/weights/all_to_all | solution.py:103
  33.5 23.1 %copy-start.25 = (bf16[32,12]{0,1:T(8,128)(2,1)S(1)}, bf16[32,12]{0,1:T(8,128)(2,1)}, u32[]{:S(2)}) copy-start(bf16[32,12]{0,1:T(8,128)(2,1)} %param.25) | copy-start | bytes 2308
  33.6 102.8 %all-gather.5.cloned.1.call-start = ((), (), s32[]{:S(2)}) async-start(), calls=%async_computation.14 | async-start | bytes 6635520 | tf_op jit(solution)/shard_map/weights/all_gather | solution.py:156
  55.3 1.3 copy-start
  56.6 4.2 %collective-permute-start = (bf16[384,2432]{1,0:T(8,128)(2,1)}, bf16[384,2432]{1,0:T(8,128)(2,1)}, u32[]{:S(2)}, u32[]{:S(2)}) collective-permute-start(bf16[384,2432]{1,0:T(8,128)(2,1)} %bitcast.30), channel_id=1, source_target_pairs={{0,16},{16,0},{1,17},{17,1},{2,18},{18,2},{3,19},{19,3},{4,20},{20... | collective-permute-start | bytes 5603336 | tf_op jit(solution)/shard_map/weights/ppermute | solution.py:49
  57.5 3.4 %copy-start.1 = (bf16[4,96,2432]{2,1,0:T(8,128)(2,1)S(1)}, bf16[4,96,2432]{2,1,0:T(8,128)(2,1)}, u32[]{:S(2)}) copy-start(bf16[4,96,2432]{2,1,0:T(8,128)(2,1)} %copy-done) | copy-start | bytes 5603332
  57.5 3.4 %copy-start.5 = (bf16[768,768]{1,0:T(8,128)(2,1)S(1)}, bf16[768,768]{1,0:T(8,128)(2,1)}, u32[]{:S(2)}) copy-start(bf16[768,768]{1,0:T(8,128)(2,1)} %constant.18.clone.matrix_ref.refs_1_) | copy-start | bytes 3538948
  57.5 3.4 %copy-start.18 = (bf16[2,1,128,768]{3,2,1,0:T(8,128)(2,1)S(1)}, bf16[2,1,128,768]{3,2,1,0:T(8,128)(2,1)}, u32[]{:S(2)}) copy-start(bf16[2,1,128,768]{3,2,1,0:T(8,128)(2,1)} %param.14) | copy-start | bytes 1179652
  60.9 1.2 copy-start.19
  66.3 0.9 copy-start.4
  67.2 25.3 %copy-start.7 = (bf16[2,128,768]{2,1,0:T(8,128)(2,1)}, bf16[2,128,768]{2,1,0:T(8,128)(2,1)S(1)}, u32[]{:S(2)}) copy-start(bf16[2,128,768]{2,1,0:T(8,128)(2,1)S(1)} %get-tuple-element.49.refs_2_) | copy-start | bytes 1179652
  67.2 25.3 %copy-start.15 = (f32[1,768]{1,0:T(1,128)}, f32[1,768]{1,0:T(1,128)S(1)}, u32[]{:S(2)}) copy-start(f32[1,768]{1,0:T(1,128)S(1)} %get-tuple-element.50.gain_ref) | copy-start | bytes 9220
  67.2 25.3 %copy-start.20 = (f32[1,768]{1,0:T(1,128)}, f32[1,768]{1,0:T(1,128)S(1)}, u32[]{:S(2)}) copy-start(f32[1,768]{1,0:T(1,128)S(1)} %get-tuple-element.61.refs_5_) | copy-start | bytes 9220
  67.2 29.0 %copy-start.26 = (s32[2,1,6]{2,1,0:T(1,128)S(1)}, s32[2,1,6]{2,1,0:T(1,128)}, u32[]{:S(2)}) copy-start(s32[2,1,6]{2,1,0:T(1,128)} %param.15) | copy-start | bytes 148
  92.5 22.6 %all-to-all-start.4 = ((bf16[16,192,128]{2,1,0:T(8,128)(2,1)}), bf16[16,192,128]{2,1,0:T(8,128)(2,1)S(1)}, u32[]{:S(2)}, u32[]{:S(2)}) async-start(bf16[16,192,128]{2,1,0:T(8,128)(2,1)} %tie.7), calls=%async_computation.4 | async-start | bytes 1572864 | tf_op jit(solution)/shard_map/project/all_to_all | solution.py:1013
  115.2 5.1 %copy-start.24 = (bf16[16,192,128]{2,1,0:T(8,128)(2,1)}, bf16[16,192,128]{2,1,0:T(8,128)(2,1)S(1)}, u32[]{:S(2)}) copy-start(bf16[16,192,128]{2,1,0:T(8,128)(2,1)S(1)} %all-to-all-done.4.taken_ref) | copy-start | bytes 2359300
  115.2 13.7 %all-to-all-start.3 = ((bf16[16,64,128]{2,1,0:T(8,128)(2,1)}), bf16[16,64,128]{2,1,0:T(8,128)(2,1)S(1)}, u32[]{:S(2)}, u32[]{:S(2)}) async-start(bf16[16,64,128]{2,1,0:T(8,128)(2,1)} %get-tuple-element.52), calls=%async_computation.3 | async-start | bytes 524288 | tf_op jit(solution)/shard_map/context/all_to_all | solution.py:1026
  128.9 0.7 copy-start.22
  136.4 1.0 copy-start.23
  136.4 15.7 %collective-permute-start.1 = (bf16[384,6912]{1,0:T(8,128)(2,1)}, bf16[384,6912]{1,0:T(8,128)(2,1)}, u32[]{:S(2)}, u32[]{:S(2)}) collective-permute-start(bf16[384,6912]{1,0:T(8,128)(2,1)} %tie.9.refs_2_.refs_4_.refs_6_.refs_8_), channel_id=1, source_target_pairs={{0,16},{16,0},{1,17},{17,1},{2,18},{18,2},{3,19},{19,3},{4,20},{20... | collective-permute-start | bytes 15925256 | tf_op jit(solution)/shard_map/weights/ppermute | solution.py:49
  167.2 7.7 %collective-permute-start.3 = (bf16[3,256,2048]{2,1,0:T(8,128)(2,1)}, bf16[3,256,2048]{2,1,0:T(8,128)(2,1)}, u32[]{:S(2)}, u32[]{:S(2)}) collective-permute-start(bf16[3,256,2048]{2,1,0:T(8,128)(2,1)} %get-tuple-element.68.refs_2_), channel_id=1, source_target_pairs={{0,16},{16,0},{1,17},{17,1},{2,18},{18,2},{3,19},{19,3},{4,20},{20... | collective-permute-start | bytes 9437192 | tf_op jit(solution)/shard_map/packet/ppermute | solution.py:49
  167.2 7.1 %collective-permute-start.2 = (bf16[256,1152]{1,0:T(8,128)(2,1)}, bf16[256,1152]{1,0:T(8,128)(2,1)S(1)}, u32[]{:S(2)}, u32[]{:S(2)}) collective-permute-start(bf16[256,1152]{1,0:T(8,128)(2,1)} %get-tuple-element.67), channel_id=1, source_target_pairs={{0,16},{16,0},{1,17},{17,1},{2,18},{18,2},{3,19},{19,3},{4,20},{20... | collective-permute-start | bytes 1769480 | tf_op jit(solution)/shard_map/packet/ppermute | solution.py:49
  167.7 6.6 %collective-permute-start.4 = (bf16[256,1024]{1,0:T(8,128)(2,1)}, bf16[256,1024]{1,0:T(8,128)(2,1)S(1)}, u32[]{:S(2)}, u32[]{:S(2)}) collective-permute-start(bf16[256,1024]{1,0:T(8,128)(2,1)} %get-tuple-element.69.refs_4_), channel_id=1, source_target_pairs={{0,16},{16,0},{1,17},{17,1},{2,18},{18,2},{3,19},{19,3},{4,20},{20... | collective-permute-start | bytes 1572872 | tf_op jit(solution)/shard_map/packet/ppermute | solution.py:49
  167.8 19.0 %all-to-all-start.6 = ((bf16[16,64,256]{2,1,0:T(8,128)(2,1)}), bf16[16,64,256]{2,1,0:T(8,128)(2,1)S(1)}, u32[]{:S(2)}, u32[]{:S(2)}) async-start(bf16[16,64,256]{2,1,0:T(8,128)(2,1)} %get-tuple-element.63), calls=%async_computation.6 | async-start | bytes 1048576 | tf_op jit(solution)/shard_map/grad_context/all_to_all | solution.py:1037
  171.4 89.8 %reduce-scatter.3.cloned.1.call-start = ((), (), s32[]{:S(2)}) async-start(), calls=%async_computation.15 | async-start | bytes 6635520 | tf_op jit(solution)/shard_map/back_grads/reduce_scatter | solution.py:180
  174.3 0.8 copy-start.28
  174.3 1.0 copy-start.27
  186.8 0.8 copy-start.21
  201.6 23.6 %all-to-all-start.7 = ((bf16[16,192,128]{2,1,0:T(8,128)(2,1)}), bf16[16,192,128]{2,1,0:T(8,128)(2,1)S(1)}, u32[]{:S(2)}, u32[]{:S(2)}) async-start(bf16[16,192,128]{2,1,0:T(8,128)(2,1)} %get-tuple-element.70), calls=%async_computation.7 | async-start | bytes 1572864 | tf_op jit(solution)/shard_map/grad_qkv/all_to_all | solution.py:1059
  206.0 88.2 %reduce-scatter.5.cloned.1.call-start = ((), (), s32[]{:S(2)}) async-start(), calls=%async_computation.16 | async-start | bytes 1658880 | tf_op jit(solution)/shard_map/front_grads/reduce_scatter | solution.py:187
  225.2 0.9 copy-start.2
  252.6 8.6 %copy-start.6 = (bf16[16,208,128]{2,1,0:T(8,128)(2,1)}, bf16[16,208,128]{2,1,0:T(8,128)(2,1)S(1)}, u32[]{:S(2)}) copy-start(bf16[16,208,128]{2,1,0:T(8,128)(2,1)S(1)} %all_to_all.69.refs_6_.refs_8_) | copy-start | bytes 2555908
  252.6 4.1 %collective-permute-start.8 = (bf16[16,208,128]{2,1,0:T(8,128)(2,1)S(1)}, bf16[16,208,128]{2,1,0:T(8,128)(2,1)S(1)}, u32[]{:S(2)}, u32[]{:S(2)}) collective-permute-start(bf16[16,208,128]{2,1,0:T(8,128)(2,1)S(1)} %all_to_all.69.refs_6_.refs_8_), channel_id=1, source_target_pairs={{0,16},{16,0},{1,17},{17,1},{2,18},{18,2},{3,19},{19,3},{4,20},{20... | collective-permute-start | bytes 2555912 | tf_op jit(solution)/shard_map/front_grads/ppermute | solution.py:49
  252.6 4.1 %collective-permute-start.7 = (bf16[16,192,128]{2,1,0:T(8,128)(2,1)}, bf16[16,192,128]{2,1,0:T(8,128)(2,1)S(1)}, u32[]{:S(2)}, u32[]{:S(2)}) collective-permute-start(bf16[16,192,128]{2,1,0:T(8,128)(2,1)} %copy-done.2), channel_id=1, source_target_pairs={{0,16},{16,0},{1,17},{17,1},{2,18},{18,2},{3,19},{19,3},{4,20},{20... | collective-permute-start | bytes 2359304 | tf_op jit(solution)/shard_map/front_grads/ppermute | solution.py:49
  253.1 3.2 %collective-permute-start.5 = (bf16[128,768]{1,0:T(8,128)(2,1)S(1)}, bf16[128,768]{1,0:T(8,128)(2,1)S(1)}, u32[]{:S(2)}, u32[]{:S(2)}) collective-permute-start(bf16[128,768]{1,0:T(8,128)(2,1)S(1)} %get-tuple-element.111.refs_1_), channel_id=1, source_target_pairs={{0,16},{16,0},{1,17},{17,1},{2,18},{18,2},{3,19},{19,3},{4,20},{20... | collective-permute-start | bytes 589832 | tf_op jit(solution)/shard_map/front_grads/ppermute | solution.py:49
  253.2 3.4 %collective-permute-start.6 = (bf16[128,768]{1,0:T(8,128)(2,1)S(1)}, bf16[128,768]{1,0:T(8,128)(2,1)S(1)}, u32[]{:S(2)}, u32[]{:S(2)}) collective-permute-start(bf16[128,768]{1,0:T(8,128)(2,1)S(1)} %get-tuple-element.110.refs_2_), channel_id=1, source_target_pairs={{0,16},{16,0},{1,17},{17,1},{2,18},{18,2},{3,19},{19,3},{4,20},{20... | collective-permute-start | bytes 589832 | tf_op jit(solution)/shard_map/front_grads/ppermute | solution.py:49
  256.7 1.2 copy-start.3
  261.2 25.5 %all-to-all-start.9 = ((bf16[4,96,2304]{2,1,0:T(8,128)(2,1)}), bf16[4,96,2304]{2,1,0:T(8,128)(2,1)S(1)}, u32[]{:S(2)}, u32[]{:S(2)}) async-start(bf16[4,96,2304]{2,1,0:T(8,128)(2,1)} %bitcast.17), calls=%async_computation.9 | async-start | bytes 3538944 | tf_op jit(solution)/shard_map/front_grads/all_to_all | solution.py:103
  273.8 20.4 %copy-start.8 = (bf16[24,2048]{1,0:T(8,128)(2,1)S(1)}, bf16[24,2048]{1,0:T(8,128)(2,1)}, u32[]{:S(2)}) copy-start(bf16[24,2048]{1,0:T(8,128)(2,1)} %up_ref.1) | copy-start | bytes 294916
  273.8 20.4 %copy-start.9 = (bf16[24,2048]{1,0:T(8,128)(2,1)S(1)}, bf16[24,2048]{1,0:T(8,128)(2,1)}, u32[]{:S(2)}) copy-start(bf16[24,2048]{1,0:T(8,128)(2,1)} %gate_ref.1) | copy-start | bytes 294916
  273.8 20.4 %copy-start.16 = (bf16[24]{0:T(256)(128)(2,1)S(1)}, bf16[24]{0:T(256)(128)(2,1)}, u32[]{:S(2)}) copy-start(bf16[24]{0:T(256)(128)(2,1)} %param.21) | copy-start | bytes 148
  273.8 30.2 %copy-start.12 = (bf16[24,768]{1,0:T(8,128)(2,1)S(1)}, bf16[24,768]{1,0:T(8,128)(2,1)}, u32[]{:S(2)}) copy-start(bf16[24,768]{1,0:T(8,128)(2,1)} %query_ref.3) | copy-start | bytes 110596
  273.8 30.2 %copy-start.13 = (bf16[24,768]{1,0:T(8,128)(2,1)S(1)}, bf16[24,768]{1,0:T(8,128)(2,1)}, u32[]{:S(2)}) copy-start(bf16[24,768]{1,0:T(8,128)(2,1)} %key_ref.3) | copy-start | bytes 110596
  273.8 30.2 %copy-start.14 = (bf16[24,768]{1,0:T(8,128)(2,1)S(1)}, bf16[24,768]{1,0:T(8,128)(2,1)}, u32[]{:S(2)}) copy-start(bf16[24,768]{1,0:T(8,128)(2,1)} %value_ref.3) | copy-start | bytes 110596
  273.8 30.2 %copy-start.17 = (bf16[24]{0:T(256)(128)(2,1)S(1)}, bf16[24]{0:T(256)(128)(2,1)}, u32[]{:S(2)}) copy-start(bf16[24]{0:T(256)(128)(2,1)} %param.16) | copy-start | bytes 148
  287.9 16.1 %all-to-all-start.10 = ((bf16[4,24,2304]{2,1,0:T(8,128)(2,1)}), bf16[4,24,2304]{2,1,0:T(8,128)(2,1)S(1)}, u32[]{:S(2)}, u32[]{:S(2)}) async-start(bf16[4,24,2304]{2,1,0:T(8,128)(2,1)} %bitcast.39), calls=%async_computation.10 | async-start | bytes 884736 | tf_op jit(solution)/shard_map/front_grads/all_to_all | solution.py:103
  292.4 1.2 collective-permute-start.9
  294.2 1.0 copy-start.10
  304.0 0.9 copy-start.11
Sparse Core Ops, SparseCore 0:
  18.1 34.4 all-gather.2
  56.7 78.6 all-gather.4
  187.8 72.7 reduce-scatter.2
  262.8 31.3 reduce-scatter.4

commit v5 on v4

--- a/solution.py
+++ b/solution.py
@@ -557,24 +557,37 @@
     )(taken, grads, context, expo, scale, before, *after)
 
 
+def reorder_kernel(array_ref, matrix_ref, out_ref):
+    out_ref[...] = jnp.dot(
+        array_ref[...], matrix_ref[...], preferred_element_type=f32
+    ).astype(bf16)
+
+
+def reorder(array, matrix):
+    return pl.pallas_call(
+        reorder_kernel,
+        out_shape=jax.ShapeDtypeStruct(array.shape, bf16),
+        compiler_params=pltpu.CompilerParams(vmem_limit_bytes=vmem_bytes),
+        cost_estimate=cost(2),
+        name="reorder",
+    )(array, matrix)
+
+
 def feed_kernel(
-    heads, steps, micro, flipped_ref, matrix_ref, hidden_ref, given_ref, gain_ref, *refs
+    heads, steps, micro, flipped_ref, hidden_ref, cot_ref, gain_ref, *refs
 ):
     contexts, refs = refs[:micro], refs[micro:]
     outs, gates, ups, downs = (refs[2 * k : 2 * k + 2] for k in range(4))
     (
         result_ref, grad_mid_ref, grad_context_ref, packet_ref, heard_ref, left_ref, other_left_ref,
-        normed_ref, branch_ref, cot_ref, mid_ref, total_ref, grad_ref,
-    ) = refs[-13:]
+        normed_ref, branch_ref, mid_ref, total_ref, grad_ref,
+    ) = refs[-12:]
     j = pl.program_id(0)
     size = contexts[0].shape[1]
     sides = side(flipped_ref[0], hidden_ref.shape[1] // 2)
 
     @pl.when(j == 0)
     def _():
-        cot_ref[...] = jnp.dot(
-            given_ref[...], matrix_ref[...], preferred_element_type=f32
-        ).astype(bf16)
         context = jnp.concatenate(
             [ref[...].reshape(-1, ref.shape[2]).astype(f32).T for ref in contexts], axis=0
         ).astype(bf16)
@@ -621,7 +634,7 @@
 
     @pl.when(j == steps - 1)
     def _():
-        result_ref[...] = dot_on(total_ref[...].astype(bf16), matrix_ref[...], 1, 1).astype(bf16)
+        result_ref[...] = total_ref[...].astype(bf16)
         mid = mid_ref[...]
         scale = lax.rsqrt(jnp.mean(mid * mid, axis=-1, keepdims=True) + norm_eps)
         grad_normed = grad_ref[...]
@@ -641,7 +654,7 @@
             other_left_ref[:, k * half : (k + 1) * half] = ref[:, other]
 
 
-def feed(flipped, matrix, hidden, contexts, cot, gain, weights, heads, *after):
+def feed(flipped, hidden, contexts, cot, gain, weights, heads, *after):
     tok, width = hidden.shape
     blocks, size, _ = contexts[0].shape
     micro = len(contexts)
@@ -660,7 +673,6 @@
         grid=(steps,),
         in_specs=[
             pl.BlockSpec(memory_space=pltpu.SMEM),
-            whole(width, width),
             whole(tok, width),
             whole(tok, width),
             whole(1, width),
@@ -686,11 +698,11 @@
             jax.ShapeDtypeStruct((tok, 3 * (width // 2)), bf16),
             jax.ShapeDtypeStruct((tok, 3 * (width // 2)), bf16),
         ],
-        scratch_shapes=[pltpu.VMEM((tok, width), bf16)] * 3 + [pltpu.VMEM((tok, width), f32)] * 3,
+        scratch_shapes=[pltpu.VMEM((tok, width), bf16)] * 2 + [pltpu.VMEM((tok, width), f32)] * 3,
         compiler_params=pltpu.CompilerParams(vmem_limit_bytes=vmem_bytes),
         cost_estimate=cost(8),
         name="feed",
-    )(flipped, matrix, hidden, cot, gain, *contexts, *weights * 4, *after)
+    )(flipped, hidden, cot, gain, *contexts, *weights * 4, *after)
 
 
 def store_tall(ref, parts):
@@ -833,7 +845,7 @@
 def input_grad_kernel(heads, micro, *refs):
     flipped_ref, matrix_ref, inputs_ref, own_weights, other_weights, gains_ref = refs[:6]
     mid_ref, *grads = refs[6 : 7 + micro]
-    input_grad_ref, wide_ref, lined_ref = refs[-3:]
+    result_ref, input_grad_ref, placed_ref, wide_ref, lined_ref = refs[6 + 1 + micro], *refs[-4:]
     tok, width = inputs_ref.shape[1:]
     inner_width = (own_weights.shape[1] - 128) // 3
     sides = side(flipped_ref[0], width // 2)
@@ -842,6 +854,7 @@
         wide_ref[rows, :] = jnp.dot(
             ref[:, : 3 * inner_width], lined_ref[...], preferred_element_type=f32
         )
+    placed_ref[...] = dot_on(result_ref[...], matrix_ref[...], 1, 1).astype(bf16)
     gain = gains_ref[...]
     for m in range(micro):
         grad = wide_ref[:, m * tok : (m + 1) * tok].T
@@ -859,16 +872,19 @@
         )
 
 
-def input_grads(flipped, matrix, inputs, weights, gains, grads, mid, heads, *after):
+def input_grads(flipped, matrix, inputs, weights, gains, grads, mid, result, heads, *after):
     micro, tok, width = inputs.shape
     inner_width = (weights[0].shape[1] - 128) // 3
     vmem = pl.BlockSpec(memory_space=pltpu.VMEM)
     return pl.pallas_call(
         functools.partial(input_grad_kernel, heads, micro),
         in_specs=[pl.BlockSpec(memory_space=pltpu.SMEM)]
-        + [vmem] * (6 + micro)
+        + [vmem] * (7 + micro)
         + [pl.BlockSpec(memory_space=pl.ANY)] * len(after),
-        out_shape=jax.ShapeDtypeStruct((micro, tok, width), f32),
+        out_shape=[
+            jax.ShapeDtypeStruct((micro, tok, width), f32),
+            jax.ShapeDtypeStruct(result.shape, bf16),
+        ],
         scratch_shapes=[
             pltpu.VMEM((width, micro * tok), f32),
             pltpu.VMEM((3 * inner_width, micro * tok), bf16),
@@ -876,7 +892,7 @@
         compiler_params=pltpu.CompilerParams(vmem_limit_bytes=vmem_bytes),
         cost_estimate=cost(6),
         name="input_grads",
-    )(flipped, matrix, inputs, *weights, gains, mid, *grads, *after)
+    )(flipped, matrix, inputs, *weights, gains, mid, *grads, result, *after)
 
 
 def front_grad_kernel(heads, parts, half, which, *refs):
@@ -1012,12 +1028,13 @@
             part = tie(sent[m], taken[-1]) if m else sent[m]
             taken.append(lax.all_to_all(part, "blk", 0, 0, tiled=True))
 
+    cots = reorder(cotangent[:, 0].reshape(micro * tok, width), matrix)
     kept, contexts, half = [], [], blocks // 4 // subs
     for m in micros:
         given = taken[m], doc_lengths[m, 0], head, table, band, buckets
         outs = [k[0] for k in kept]
         if m:
-            outs = attend(*given, 0, half, [], *outs)
+            outs = attend(*given, 0, half, [], *outs, cots)
             outs = attend(*given, half, None, outs, *contexts)
         else:
             outs = attend(*given, 0, None, [])
@@ -1030,8 +1047,7 @@
     fits = staged(rows, blocks, share)
     here = micro * tok
     result, grad_mid, grad_context, mine, heard, left, left_other = feed(
-        flipped, matrix, tokens.reshape(here, width), contexts,
-        cotangent[:, 0].reshape(here, width), gain_f, back_full, heads,
+        flipped, tokens.reshape(here, width), contexts, cots, gain_f, back_full, heads,
     )
     with jax.named_scope("grad_context"):
         grads = lax.all_to_all(grad_context, "blk", 0, 0, tiled=True)
@@ -1080,8 +1096,8 @@
                 for which in (0, 1)
             )
             front_parts = scatter_whole(own, other)[None]
-    input_grad = input_grads(
-        flipped, matrix, tokens, front_full, gain_a, grad_qkv, grad_mid, heads, own
+    input_grad, result = input_grads(
+        flipped, matrix, tokens, front_full, gain_a, grad_qkv, grad_mid, result, heads, own
     )
     if fits:
         with jax.named_scope("front_grads"):

time: 314 us -> 313 us (level)
    unnamed x58 -> x60, local copies, waits for them, and re-layouts: 10.3 us -> 11 us
  transfers between devices with their start and end apart: 22 -> 22, of which waited for: 15 -> 16; matrix products, arithmetic and copies ran while one was open for 2% -> 2% of each run, Pallas kernels for 26% -> 26%
where the time goes in v5:
time: 313 us; the launch traced here: 312 us
  Pallas kernels  98.6 us (32%)
  waiting for transfers between devices  77.5 us (25%)
  blocking collectives  67.1 us (21%)
  starting transfers between devices  36 us (12%)
  local copies, waits for them, and re-layouts  14.3 us (5%)
  between operations  14 us (4%)
  other arithmetic  4.29 us (1%)
    all_to_all x4, waiting for transfers between devices, exchange(): lax.all_to_all(array, 'blk', 0, 0, tiled=True, axis_index_groups=groups)  34.9 us
    pallas_call x2, Pallas kernels, attend_back(): pl.pallas_call(functools.partial(attend_back_kernel, size, blocks, bucket...  27.2 us
    all_to_all x1, blocking collectives, body(): grad_qkv.append(lax.all_to_all(returned, 'blk', 0, 0, tiled=True))  26.5 us
    all_to_all x1, blocking collectives, body(): taken.append(lax.all_to_all(part, 'blk', 0, 0, tiled=True))  25.1 us
    pallas_call x3, Pallas kernels, attend(): pl.pallas_call(functools.partial(attend_kernel, size, blocks, lengths.sha...  24.4 us
    all_gather x1, waiting for transfers between devices, gather_back(): lax.all_gather(shard, 'blk', axis=0, tiled=True, axis_index_groups=across)  19.1 us
    all_to_all x4, starting transfers between devices, exchange(): lax.all_to_all(array, 'blk', 0, 0, tiled=True, axis_index_groups=groups)  17.3 us
    all_to_all x1, blocking collectives, body(): contexts.append(lax.all_to_all(outs[0], 'blk', 0, 0, tiled=True))  15.5 us
  transfers between devices with their start and end apart: 22, of which 16 were waited for; matrix products, arithmetic and copies ran while one was open for 2% of the time, Pallas kernels for 26%

profile of v5, /device:TPU:0, one launch (start us, length us, event | category | flops | bytes accessed | tf_op | source)
XLA Modules:
  0.0 311.8 jit_solution(9040766934891673849)
XLA Ops:
  7.2 1.7 pack.1
  8.9 6.3 %all-to-all-start = ((bf16[4,24,2432]{2,1,0:T(8,128)(2,1)}), bf16[4,24,2432]{2,1,0:T(8,128)(2,1)S(1)}, u32[]{:S(2)}, u32[]{:S(2)}) async-start(bf16[4,24,2432]{2,1,0:T(8,128)(2,1)} %pack.1), calls=%async_computation | async-start | bytes 933888 | tf_op jit(solution)/shard_map/weights/all_to_all | solution.py:103
  15.2 1.8 pad_maximum_fusion
  17.0 11.5 %all-to-all-done = bf16[4,24,2432]{2,1,0:T(8,128)(2,1)S(1)} async-done(((bf16[4,24,2432]{2,1,0:T(8,128)(2,1)}), bf16[4,24,2432]{2,1,0:T(8,128)(2,1)S(1)}, u32[]{:S(2)}, u32[]{:S(2)}) %all-to-all-start) | async-done | bytes 466976 | tf_op jit(solution)/shard_map/weights/all_to_all | solution.py:103
  28.4 1.4 tile.10
  29.8 3.7 %all-to-all-start.1 = ((bf16[4,96,2432]{2,1,0:T(8,128)(2,1)}), bf16[4,96,2432]{2,1,0:T(8,128)(2,1)S(1)}, u32[]{:S(2)}, u32[]{:S(2)}) async-start(bf16[4,96,2432]{2,1,0:T(8,128)(2,1)} %tile.10), calls=%async_computation.1 | async-start | bytes 3735552 | tf_op jit(solution)/shard_map/weights/all_to_all | solution.py:103
  33.6 19.1 %all-gather.3.cloned.1.call-done.refs_0_ = bf16[96,6912]{1,0:T(8,128)(2,1)} async-done(((bf16[24,6912]{1,0:T(8,128)(2,1)}), bf16[96,6912]{1,0:T(8,128)(2,1)}) %all-gather.3.cloned.1.call-update) | async-done | bytes 1327120 | tf_op jit(solution)/shard_map/weights/all_gather | solution.py:154
  52.6 2.7 all-to-all-done.1
  55.3 1.3 copy-done
  56.8 0.7 reshape.64.table_ref
  57.5 2.0 bias_tiles.1.after_ref.band_ref
  59.5 1.2 collective-permute-done.other_ref.refs_4_
  60.7 1.8 copy-done.20
  62.6 2.5 project.1
  65.1 0.9 copy-done.4
  66.0 25.1 %all_to_all.67.taken_ref.refs_1_ = bf16[16,192,128]{2,1,0:T(8,128)(2,1)} all-to-all(bf16[16,192,128]{2,1,0:T(8,128)(2,1)S(1)} %get-tuple-element.54), channel_id=1, replica_groups=mesh['rows'=2,'blk'=16] {'blk'}, dimensions={0} | all-to-all | bytes 1572864 | tf_op jit(solution)/shard_map/project/all_to_all | solution.py:1029
  91.1 3.6 %all-to-all-start.4 = ((bf16[16,192,128]{2,1,0:T(8,128)(2,1)}), bf16[16,192,128]{2,1,0:T(8,128)(2,1)S(1)}, u32[]{:S(2)}, u32[]{:S(2)}) async-start(bf16[16,192,128]{2,1,0:T(8,128)(2,1)} %tie.7), calls=%async_computation.4 | async-start | bytes 1572864 | tf_op jit(solution)/shard_map/project/all_to_all | solution.py:1029
  94.7 2.7 reorder.1.refs_1_.cot_ref
  97.4 0.5 slice_bitcast_fusion
  97.9 10.7 %attend.3 = (bf16[16,64,128]{2,1,0:T(8,128)(2,1)}, f32[64,2048]{1,0:T(8,128)}, bf16[2048,2048]{1,0:T(8,128)(2,1)}, f32[1,2048]{1,0:T(1,128)}) custom-call(s32[6]{0:T(128)} %get-tuple-element.117.bounds_ref, s32[1]{0:T(128)} %bitcast.6.head_ref, f32[384]{0:T(512)} %reshape.64.table_ref, bf16[16,192,128]{2,1,0:T(8,128)(2,1)} %all_to_all.67.taken_ref.refs_1_, ...), custom_call_target="tpu_custom_call" | custom-call | flops 6000000000 | tf_op jit(solution)/shard_map/attend/pallas_call | solution.py:397
  108.7 5.1 %all-to-all-done.4.taken_ref = bf16[16,192,128]{2,1,0:T(8,128)(2,1)S(1)} async-done(((bf16[16,192,128]{2,1,0:T(8,128)(2,1)}), bf16[16,192,128]{2,1,0:T(8,128)(2,1)S(1)}, u32[]{:S(2)}, u32[]{:S(2)}) %all-to-all-start.4) | async-done | bytes 786464 | tf_op jit(solution)/shard_map/project/all_to_all | solution.py:1029
  113.7 5.1 %all-to-all-start.3 = ((bf16[16,64,128]{2,1,0:T(8,128)(2,1)}), bf16[16,64,128]{2,1,0:T(8,128)(2,1)S(1)}, u32[]{:S(2)}, u32[]{:S(2)}) async-start(bf16[16,64,128]{2,1,0:T(8,128)(2,1)} %get-tuple-element.55), calls=%async_computation.3 | async-start | bytes 524288 | tf_op jit(solution)/shard_map/context/all_to_all | solution.py:1043
  118.8 6.9 %attend.4 = (bf16[16,64,128]{2,1,0:T(8,128)(2,1)}, f32[64,2048]{1,0:T(8,128)}, bf16[2048,2048]{1,0:T(8,128)(2,1)}, f32[1,2048]{1,0:T(1,128)}) custom-call(s32[6]{0:T(128)} %get-tuple-element.116.bounds_ref, s32[1]{0:T(128)} %bitcast.6.head_ref, f32[384]{0:T(512)} %reshape.64.table_ref, bf16[16,192,128]{2,1,0:T(8,128)(2,1)} %copy-done.25, ...), custom_call_target="tpu_custom_call" | custom-call | flops 6000000000 | tf_op jit(solution)/shard_map/attend/pallas_call | solution.py:397
  125.8 1.7 all-to-all-done.3.refs_4_.refs_0_
  127.4 0.7 copy-done.23
  128.2 6.8 %attend.5 = (bf16[16,64,128]{2,1,0:T(8,128)(2,1)}, f32[64,2048]{1,0:T(8,128)}, bf16[2048,2048]{1,0:T(8,128)(2,1)}, f32[1,2048]{1,0:T(1,128)}) custom-call(s32[6]{0:T(128)} %get-tuple-element.116.bounds_ref, s32[1]{0:T(128)} %bitcast.6.head_ref, f32[384]{0:T(512)} %reshape.64.table_ref, ...), custom_call_target="tpu_custom_call", output_to_operand_aliasing={{0}: (5, {}), {1}: (6, {}), {2}: (7, {}), {3}: (8, {})} | custom-call | flops 6000000000 | tf_op jit(solution)/shard_map/attend/pallas_call | solution.py:397
  135.0 1.0 all-gather.5.cloned.1.call-done.refs_0_
  135.9 0.9 copy-done.24
  136.9 15.5 %all_to_all.68.refs_1_ = bf16[16,64,128]{2,1,0:T(8,128)(2,1)} all-to-all(bf16[16,64,128]{2,1,0:T(8,128)(2,1)S(1)} %copy-done.24), channel_id=1, replica_groups=mesh['rows'=2,'blk'=16] {'blk'}, dimensions={0} | all-to-all | bytes 524288 | tf_op jit(solution)/shard_map/context/all_to_all | solution.py:1043
  152.4 14.3 %feed.1 = (bf16[256,768]{1,0:T(8,128)(2,1)}, f32[256,768]{1,0:T(8,128)}, bf16[16,64,256]{2,1,0:T(8,128)(2,1)}, bf16[3,256,2048]{2,1,0:T(8,128)(2,1)}, bf16[256,1...) custom-call(s32[1]{0:T(128)} %bitcast.flipped_ref.refs_0_, bf16[256,768]{1,0:T(8,128)(2,1)} %bitcast.33, ...), custom_call_target="tpu_custom_call" | custom-call | flops 8000000000 | tf_op jit(solution)/shard_map/feed/pallas_call | solution.py:671
  166.8 0.5 collective-permute-start.2
  167.3 3.6 %all-to-all-start.6 = ((bf16[16,64,256]{2,1,0:T(8,128)(2,1)}), bf16[16,64,256]{2,1,0:T(8,128)(2,1)S(1)}, u32[]{:S(2)}, u32[]{:S(2)}) async-start(bf16[16,64,256]{2,1,0:T(8,128)(2,1)} %get-tuple-element.64), calls=%async_computation.6 | async-start | bytes 1048576 | tf_op jit(solution)/shard_map/grad_context/all_to_all | solution.py:1053
  171.0 2.9 collective-permute-done.4.refs_5_
  173.9 0.5 collective-permute-done.3.refs_3_
  174.4 0.3 copy-done.29
  174.8 9.7 %weight_grads.1.refs_0_ = bf16[384,6912]{1,0:T(8,128)(2,1)} custom-call(bf16[256,1152]{1,0:T(8,128)(2,1)} %get-tuple-element.67.refs_0_, bf16[256,1152]{1,0:T(8,128)(2,1)} %copy-done.28, bf16[3,256,2048]{2,1,0:T(8,128)(2,1)} %get-tuple-element.69.refs_2_, bf16[3,256,2048]{2,1,0:T(8,128)(2,1)} %collective-permute-done.3.refs_3_, ...), custom_call_target="tpu_custom_call" | custom-call | flops 10000000000 | tf_op jit(solution)/shard_map/back_grads/weight_grads/pallas_call | solution.py:747
  184.6 1.8 all-to-all-done.6.refs_1_.grad_ref
  186.3 0.8 copy-done.22
  187.2 0.5 broadcast_in_dim.20.refs_0_
  187.7 13.4 %attend_back.2 = (bf16[16,192,128]{2,1,0:T(8,128)(2,1)}, f32[1,128]{1,0:T(1,128)}) custom-call(bf16[16,192,128]{2,1,0:T(8,128)(2,1)} %all_to_all.67.taken_ref.refs_1_, bf16[16,64,256]{2,1,0:T(8,128)(2,1)} %copy-done.22, f32[64,2048]{1,0:T(8,128)} %get-tuple-element.57.refs_0_.context_ref, bf16[2048,2048]{1,0:T(8,128)(2,1)} %get-tuple-element.65.expo_ref, ...), custom_call_target="tpu_custom_call" | custom-call | flops 12999999488 | tf_op jit(solution)/shard_map/attend_back/pallas_call | solution.py:524
  201.1 4.4 %all-to-all-start.7 = ((bf16[16,192,128]{2,1,0:T(8,128)(2,1)}), bf16[16,192,128]{2,1,0:T(8,128)(2,1)S(1)}, u32[]{:S(2)}, u32[]{:S(2)}) async-start(bf16[16,192,128]{2,1,0:T(8,128)(2,1)} %get-tuple-element.71), calls=%async_computation.7 | async-start | bytes 1572864 | tf_op jit(solution)/shard_map/grad_qkv/all_to_all | solution.py:1075
  205.6 13.7 %attend_back.3 = (bf16[16,208,128]{2,1,0:T(8,128)(2,1)}, f32[1,128]{1,0:T(1,128)}) custom-call(bf16[16,192,128]{2,1,0:T(8,128)(2,1)} %copy-done.25, bf16[16,64,256]{2,1,0:T(8,128)(2,1)} %copy-done.22, f32[64,2048]{1,0:T(8,128)} %get-tuple-element.72.context_ref, bf16[2048,2048]{1,0:T(8,128)(2,1)} %get-tuple-element.73.expo_ref, ...), custom_call_target="tpu_custom_call" | custom-call | flops 12999999488 | tf_op jit(solution)/shard_map/attend_back/pallas_call | solution.py:524
  219.4 5.4 %all-to-all-done.7.refs_1_.refs_5_.refs_7_ = bf16[16,192,128]{2,1,0:T(8,128)(2,1)S(1)} async-done(((bf16[16,192,128]{2,1,0:T(8,128)(2,1)}), bf16[16,192,128]{2,1,0:T(8,128)(2,1)S(1)}, u32[]{:S(2)}, u32[]{:S(2)}) %all-to-all-start.7) | async-done | bytes 786464 | tf_op jit(solution)/shard_map/grad_qkv/all_to_all | solution.py:1075
  224.8 0.9 copy-done.2
  225.7 26.5 %all_to_all.69.refs_6_.refs_8_ = bf16[16,208,128]{2,1,0:T(8,128)(2,1)S(1)} all-to-all(bf16[16,208,128]{2,1,0:T(8,128)(2,1)} %tie.11), channel_id=1, replica_groups=mesh['rows'=2,'blk'=16] {'blk'}, dimensions={0} | all-to-all | bytes 1703936 | tf_op jit(solution)/shard_map/grad_qkv/all_to_all | solution.py:1075
  252.2 0.5 collective-permute-start.7
  252.8 0.5 collective-permute-start.6
  253.3 2.7 collective-permute-done.5.refs_3_
  256.0 0.3 collective-permute-done.6.refs_4_
  256.2 1.2 copy-done.3
  257.4 3.4 %front_grads.1.refs_10_.refs_1_ = bf16[384,2304]{1,0:T(8,128)(2,1)} custom-call(s32[1]{0:T(128)} %bitcast.flipped_ref.refs_0_, bf16[128,768]{1,0:T(8,128)(2,1)S(1)} %get-tuple-element.115.refs_1_, bf16[128,768]{1,0:T(8,128)(2,1)S(1)} %get-tuple-element.114.refs_2_, bf16[128,768]{1,0:T(8,128)(2,1)S(1)} %collective-permute-done.5.refs_3_, ...), custom_call_target="tpu_custom_call" | custom-call | flops 5000000000 | tf_op jit(solution)/shard_map/front_grads/front_grads/pallas_call | solution.py:920
  260.8 3.6 %all-to-all-start.9 = ((bf16[4,96,2304]{2,1,0:T(8,128)(2,1)}), bf16[4,96,2304]{2,1,0:T(8,128)(2,1)S(1)}, u32[]{:S(2)}, u32[]{:S(2)}) async-start(bf16[4,96,2304]{2,1,0:T(8,128)(2,1)} %bitcast.17), calls=%async_computation.9 | async-start | bytes 3538944 | tf_op jit(solution)/shard_map/front_grads/all_to_all | solution.py:103
  264.4 9.1 %input_grads.1 = (f32[2,128,768]{2,1,0:T(8,128)}, bf16[256,768]{1,0:T(8,128)(2,1)}) custom-call(s32[1]{0:T(128)} %bitcast.flipped_ref.refs_0_, bf16[768,768]{1,0:T(8,128)(2,1)} %constant.18.clone.matrix_ref.refs_1_, bf16[2,128,768]{2,1,0:T(8,128)(2,1)} %copy-done.8, bf16[384,2432]{1,0:T(8,128)(2,1)} %bitcast.31, bf16[384,2432]{1,0:T(8,128)(2,1)} %copy-done.17, ...), custom_call_target="tpu_custom_call" | custom-call | flops 6000000000 | tf_op jit(solution)/shard_map/input_grads/pallas_call | solution.py:879
  273.6 12.7 %all-to-all-done.9 = bf16[4,96,2304]{2,1,0:T(8,128)(2,1)S(1)} async-done(((bf16[4,96,2304]{2,1,0:T(8,128)(2,1)}), bf16[4,96,2304]{2,1,0:T(8,128)(2,1)S(1)}, u32[]{:S(2)}, u32[]{:S(2)}) %all-to-all-start.9) | async-done | bytes 1769504 | tf_op jit(solution)/shard_map/front_grads/all_to_all | solution.py:103
  286.3 1.2 reduce_sum.21.refs_0_
  287.5 3.7 %all-to-all-start.10 = ((bf16[4,24,2304]{2,1,0:T(8,128)(2,1)}), bf16[4,24,2304]{2,1,0:T(8,128)(2,1)S(1)}, u32[]{:S(2)}, u32[]{:S(2)}) async-start(bf16[4,24,2304]{2,1,0:T(8,128)(2,1)} %bitcast.39), calls=%async_computation.10 | async-start | bytes 884736 | tf_op jit(solution)/shard_map/front_grads/all_to_all | solution.py:103
  291.2 0.8 convert_reduce_fusion
  292.0 1.2 collective-permute-done.9
  293.2 0.6 bitcast_add_fusion
  293.8 1.0 copy-done.9
  294.8 0.9 unpack_back.1
  295.6 7.9 %all-to-all-done.10.parts_ref = bf16[4,24,2304]{2,1,0:T(8,128)(2,1)S(1)} async-done(((bf16[4,24,2304]{2,1,0:T(8,128)(2,1)}), bf16[4,24,2304]{2,1,0:T(8,128)(2,1)S(1)}, u32[]{:S(2)}, u32[]{:S(2)}) %all-to-all-start.10) | async-done | bytes 442400 | tf_op jit(solution)/shard_map/front_grads/all_to_all | solution.py:103
  303.6 0.9 copy-done.10
  304.5 0.7 unpack_front.1
  (79 shorter events, 0.9 us)
Async XLA Ops:
  8.9 19.6 %all-to-all-start = ((bf16[4,24,2432]{2,1,0:T(8,128)(2,1)}), bf16[4,24,2432]{2,1,0:T(8,128)(2,1)S(1)}, u32[]{:S(2)}, u32[]{:S(2)}) async-start(bf16[4,24,2432]{2,1,0:T(8,128)(2,1)} %pack.1), calls=%async_computation | async-start | bytes 933888 | tf_op jit(solution)/shard_map/weights/all_to_all | solution.py:103
  15.2 37.4 %all-gather.3.cloned.1.call-start = ((), (), s32[]{:S(2)}) async-start(), calls=%async_computation.13 | async-start | bytes 1658880 | tf_op jit(solution)/shard_map/weights/all_gather | solution.py:154
  29.8 25.5 %all-to-all-start.1 = ((bf16[4,96,2432]{2,1,0:T(8,128)(2,1)}), bf16[4,96,2432]{2,1,0:T(8,128)(2,1)S(1)}, u32[]{:S(2)}, u32[]{:S(2)}) async-start(bf16[4,96,2432]{2,1,0:T(8,128)(2,1)} %tile.10), calls=%async_computation.1 | async-start | bytes 3735552 | tf_op jit(solution)/shard_map/weights/all_to_all | solution.py:103
  33.6 23.1 %copy-start.26 = (bf16[32,12]{0,1:T(8,128)(2,1)S(1)}, bf16[32,12]{0,1:T(8,128)(2,1)}, u32[]{:S(2)}) copy-start(bf16[32,12]{0,1:T(8,128)(2,1)} %param.25) | copy-start | bytes 2308
  33.6 102.3 %all-gather.5.cloned.1.call-start = ((), (), s32[]{:S(2)}) async-start(), calls=%async_computation.14 | async-start | bytes 6635520 | tf_op jit(solution)/shard_map/weights/all_gather | solution.py:156
  55.3 1.3 copy-start
  56.6 4.1 %collective-permute-start = (bf16[384,2432]{1,0:T(8,128)(2,1)}, bf16[384,2432]{1,0:T(8,128)(2,1)S(1)}, u32[]{:S(2)}, u32[]{:S(2)}) collective-permute-start(bf16[384,2432]{1,0:T(8,128)(2,1)} %bitcast.30), channel_id=1, source_target_pairs={{0,16},{16,0},{1,17},{17,1},{2,18},{18,2},{3,19},{19,3},{4,20},{20... | collective-permute-start | bytes 5603336 | tf_op jit(solution)/shard_map/weights/ppermute | solution.py:49
  57.5 3.2 %copy-start.1 = (bf16[4,96,2432]{2,1,0:T(8,128)(2,1)S(1)}, bf16[4,96,2432]{2,1,0:T(8,128)(2,1)}, u32[]{:S(2)}) copy-start(bf16[4,96,2432]{2,1,0:T(8,128)(2,1)} %copy-done) | copy-start | bytes 5603332
  57.5 3.2 %copy-start.18 = (bf16[2,1,128,768]{3,2,1,0:T(8,128)(2,1)S(1)}, bf16[2,1,128,768]{3,2,1,0:T(8,128)(2,1)}, u32[]{:S(2)}) copy-start(bf16[2,1,128,768]{3,2,1,0:T(8,128)(2,1)} %param.14) | copy-start | bytes 1179652
  57.5 3.2 %copy-start.19 = (bf16[768,768]{1,0:T(8,128)(2,1)S(1)}, bf16[768,768]{1,0:T(8,128)(2,1)}, u32[]{:S(2)}) copy-start(bf16[768,768]{1,0:T(8,128)(2,1)} %constant.18.clone.matrix_ref.refs_1_) | copy-start | bytes 3538948
  60.7 4.4 %copy-start.17 = (bf16[384,2432]{1,0:T(8,128)(2,1)}, bf16[384,2432]{1,0:T(8,128)(2,1)S(1)}, u32[]{:S(2)}) copy-start(bf16[384,2432]{1,0:T(8,128)(2,1)S(1)} %collective-permute-done.other_ref.refs_4_) | copy-start | bytes 5603332
  60.7 1.8 copy-start.20
  65.1 0.9 copy-start.4
  66.0 25.1 %copy-start.8 = (bf16[2,128,768]{2,1,0:T(8,128)(2,1)}, bf16[2,128,768]{2,1,0:T(8,128)(2,1)S(1)}, u32[]{:S(2)}) copy-start(bf16[2,128,768]{2,1,0:T(8,128)(2,1)S(1)} %get-tuple-element.51.refs_2_) | copy-start | bytes 1179652
  66.0 25.1 %copy-start.14 = (f32[1,768]{1,0:T(1,128)}, f32[1,768]{1,0:T(1,128)S(1)}, u32[]{:S(2)}) copy-start(f32[1,768]{1,0:T(1,128)S(1)} %get-tuple-element.53.gain_ref) | copy-start | bytes 9220
  66.0 31.4 %copy-start.21 = (f32[1,768]{1,0:T(1,128)}, f32[1,768]{1,0:T(1,128)S(1)}, u32[]{:S(2)}) copy-start(f32[1,768]{1,0:T(1,128)S(1)} %get-tuple-element.52.refs_5_) | copy-start | bytes 9220
  91.1 22.6 %all-to-all-start.4 = ((bf16[16,192,128]{2,1,0:T(8,128)(2,1)}), bf16[16,192,128]{2,1,0:T(8,128)(2,1)S(1)}, u32[]{:S(2)}, u32[]{:S(2)}) async-start(bf16[16,192,128]{2,1,0:T(8,128)(2,1)} %tie.7), calls=%async_computation.4 | async-start | bytes 1572864 | tf_op jit(solution)/shard_map/project/all_to_all | solution.py:1029
  94.7 2.7 copy-start.27
  113.7 5.1 %copy-start.25 = (bf16[16,192,128]{2,1,0:T(8,128)(2,1)}, bf16[16,192,128]{2,1,0:T(8,128)(2,1)S(1)}, u32[]{:S(2)}) copy-start(bf16[16,192,128]{2,1,0:T(8,128)(2,1)S(1)} %all-to-all-done.4.taken_ref) | copy-start | bytes 2359300
  113.7 13.7 %all-to-all-start.3 = ((bf16[16,64,128]{2,1,0:T(8,128)(2,1)}), bf16[16,64,128]{2,1,0:T(8,128)(2,1)S(1)}, u32[]{:S(2)}, u32[]{:S(2)}) async-start(bf16[16,64,128]{2,1,0:T(8,128)(2,1)} %get-tuple-element.55), calls=%async_computation.3 | async-start | bytes 524288 | tf_op jit(solution)/shard_map/context/all_to_all | solution.py:1043
  127.4 0.7 copy-start.23
  135.9 0.9 copy-start.24
  135.9 16.5 %collective-permute-start.1 = (bf16[384,6912]{1,0:T(8,128)(2,1)}, bf16[384,6912]{1,0:T(8,128)(2,1)}, u32[]{:S(2)}, u32[]{:S(2)}) collective-permute-start(bf16[384,6912]{1,0:T(8,128)(2,1)} %tie.9.refs_2_.refs_4_.refs_6_.refs_8_), channel_id=1, source_target_pairs={{0,16},{16,0},{1,17},{17,1},{2,18},{18,2},{3,19},{19,3},{4,20},{20... | collective-permute-start | bytes 15925256 | tf_op jit(solution)/shard_map/weights/ppermute | solution.py:49
  166.7 7.7 %collective-permute-start.3 = (bf16[3,256,2048]{2,1,0:T(8,128)(2,1)}, bf16[3,256,2048]{2,1,0:T(8,128)(2,1)}, u32[]{:S(2)}, u32[]{:S(2)}) collective-permute-start(bf16[3,256,2048]{2,1,0:T(8,128)(2,1)} %get-tuple-element.69.refs_2_), channel_id=1, source_target_pairs={{0,16},{16,0},{1,17},{17,1},{2,18},{18,2},{3,19},{19,3},{4,20},{20... | collective-permute-start | bytes 9437192 | tf_op jit(solution)/shard_map/packet/ppermute | solution.py:49
  166.8 7.1 %collective-permute-start.2 = (bf16[256,1152]{1,0:T(8,128)(2,1)}, bf16[256,1152]{1,0:T(8,128)(2,1)S(1)}, u32[]{:S(2)}, u32[]{:S(2)}) collective-permute-start(bf16[256,1152]{1,0:T(8,128)(2,1)} %get-tuple-element.68), channel_id=1, source_target_pairs={{0,16},{16,0},{1,17},{17,1},{2,18},{18,2},{3,19},{19,3},{4,20},{20... | collective-permute-start | bytes 1769480 | tf_op jit(solution)/shard_map/packet/ppermute | solution.py:49
  167.3 6.6 %collective-permute-start.4 = (bf16[256,1024]{1,0:T(8,128)(2,1)}, bf16[256,1024]{1,0:T(8,128)(2,1)S(1)}, u32[]{:S(2)}, u32[]{:S(2)}) collective-permute-start(bf16[256,1024]{1,0:T(8,128)(2,1)} %get-tuple-element.70.refs_4_), channel_id=1, source_target_pairs={{0,16},{16,0},{1,17},{17,1},{2,18},{18,2},{3,19},{19,3},{4,20},{20... | collective-permute-start | bytes 1572872 | tf_op jit(solution)/shard_map/packet/ppermute | solution.py:49
  167.3 19.0 %all-to-all-start.6 = ((bf16[16,64,256]{2,1,0:T(8,128)(2,1)}), bf16[16,64,256]{2,1,0:T(8,128)(2,1)S(1)}, u32[]{:S(2)}, u32[]{:S(2)}) async-start(bf16[16,64,256]{2,1,0:T(8,128)(2,1)} %get-tuple-element.64), calls=%async_computation.6 | async-start | bytes 1048576 | tf_op jit(solution)/shard_map/grad_context/all_to_all | solution.py:1053
  170.9 89.8 %reduce-scatter.3.cloned.1.call-start = ((), (), s32[]{:S(2)}) async-start(), calls=%async_computation.15 | async-start | bytes 6635520 | tf_op jit(solution)/shard_map/back_grads/reduce_scatter | solution.py:180
  173.9 0.8 copy-start.29
  173.9 1.0 copy-start.28
  186.3 0.8 copy-start.22
  201.1 23.6 %all-to-all-start.7 = ((bf16[16,192,128]{2,1,0:T(8,128)(2,1)}), bf16[16,192,128]{2,1,0:T(8,128)(2,1)S(1)}, u32[]{:S(2)}, u32[]{:S(2)}) async-start(bf16[16,192,128]{2,1,0:T(8,128)(2,1)} %get-tuple-element.71), calls=%async_computation.7 | async-start | bytes 1572864 | tf_op jit(solution)/shard_map/grad_qkv/all_to_all | solution.py:1075
  205.6 88.2 %reduce-scatter.5.cloned.1.call-start = ((), (), s32[]{:S(2)}) async-start(), calls=%async_computation.16 | async-start | bytes 1658880 | tf_op jit(solution)/shard_map/front_grads/reduce_scatter | solution.py:187
  224.7 0.9 copy-start.2
  252.2 8.6 %copy-start.5 = (bf16[16,208,128]{2,1,0:T(8,128)(2,1)}, bf16[16,208,128]{2,1,0:T(8,128)(2,1)S(1)}, u32[]{:S(2)}) copy-start(bf16[16,208,128]{2,1,0:T(8,128)(2,1)S(1)} %all_to_all.69.refs_6_.refs_8_) | copy-start | bytes 2555908
  252.2 4.1 %collective-permute-start.8 = (bf16[16,208,128]{2,1,0:T(8,128)(2,1)S(1)}, bf16[16,208,128]{2,1,0:T(8,128)(2,1)S(1)}, u32[]{:S(2)}, u32[]{:S(2)}) collective-permute-start(bf16[16,208,128]{2,1,0:T(8,128)(2,1)S(1)} %all_to_all.69.refs_6_.refs_8_), channel_id=1, source_target_pairs={{0,16},{16,0},{1,17},{17,1},{2,18},{18,2},{3,19},{19,3},{4,20},{20... | collective-permute-start | bytes 2555912 | tf_op jit(solution)/shard_map/front_grads/ppermute | solution.py:49
  252.2 4.1 %collective-permute-start.7 = (bf16[16,192,128]{2,1,0:T(8,128)(2,1)}, bf16[16,192,128]{2,1,0:T(8,128)(2,1)S(1)}, u32[]{:S(2)}, u32[]{:S(2)}) collective-permute-start(bf16[16,192,128]{2,1,0:T(8,128)(2,1)} %copy-done.2), channel_id=1, source_target_pairs={{0,16},{16,0},{1,17},{17,1},{2,18},{18,2},{3,19},{19,3},{4,20},{20... | collective-permute-start | bytes 2359304 | tf_op jit(solution)/shard_map/front_grads/ppermute | solution.py:49
  252.7 3.2 %collective-permute-start.5 = (bf16[128,768]{1,0:T(8,128)(2,1)S(1)}, bf16[128,768]{1,0:T(8,128)(2,1)S(1)}, u32[]{:S(2)}, u32[]{:S(2)}) collective-permute-start(bf16[128,768]{1,0:T(8,128)(2,1)S(1)} %get-tuple-element.115.refs_1_), channel_id=1, source_target_pairs={{0,16},{16,0},{1,17},{17,1},{2,18},{18,2},{3,19},{19,3},{4,20},{20... | collective-permute-start | bytes 589832 | tf_op jit(solution)/shard_map/front_grads/ppermute | solution.py:49
  252.8 3.4 %collective-permute-start.6 = (bf16[128,768]{1,0:T(8,128)(2,1)S(1)}, bf16[128,768]{1,0:T(8,128)(2,1)S(1)}, u32[]{:S(2)}, u32[]{:S(2)}) collective-permute-start(bf16[128,768]{1,0:T(8,128)(2,1)S(1)} %get-tuple-element.114.refs_2_), channel_id=1, source_target_pairs={{0,16},{16,0},{1,17},{17,1},{2,18},{18,2},{3,19},{19,3},{4,20},{20... | collective-permute-start | bytes 589832 | tf_op jit(solution)/shard_map/front_grads/ppermute | solution.py:49
  256.2 1.2 copy-start.3
  260.8 25.5 %all-to-all-start.9 = ((bf16[4,96,2304]{2,1,0:T(8,128)(2,1)}), bf16[4,96,2304]{2,1,0:T(8,128)(2,1)S(1)}, u32[]{:S(2)}, u32[]{:S(2)}) async-start(bf16[4,96,2304]{2,1,0:T(8,128)(2,1)} %bitcast.17), calls=%async_computation.9 | async-start | bytes 3538944 | tf_op jit(solution)/shard_map/front_grads/all_to_all | solution.py:103
  273.5 20.3 %copy-start.6 = (bf16[24,2048]{1,0:T(8,128)(2,1)S(1)}, bf16[24,2048]{1,0:T(8,128)(2,1)}, u32[]{:S(2)}) copy-start(bf16[24,2048]{1,0:T(8,128)(2,1)} %up_ref.1) | copy-start | bytes 294916
  273.5 20.3 %copy-start.7 = (bf16[24,2048]{1,0:T(8,128)(2,1)S(1)}, bf16[24,2048]{1,0:T(8,128)(2,1)}, u32[]{:S(2)}) copy-start(bf16[24,2048]{1,0:T(8,128)(2,1)} %gate_ref.1) | copy-start | bytes 294916
  273.5 20.3 %copy-start.15 = (bf16[24]{0:T(256)(128)(2,1)S(1)}, bf16[24]{0:T(256)(128)(2,1)}, u32[]{:S(2)}) copy-start(bf16[24]{0:T(256)(128)(2,1)} %param.21) | copy-start | bytes 148
  273.5 30.0 %copy-start.11 = (bf16[24,768]{1,0:T(8,128)(2,1)S(1)}, bf16[24,768]{1,0:T(8,128)(2,1)}, u32[]{:S(2)}) copy-start(bf16[24,768]{1,0:T(8,128)(2,1)} %query_ref.3) | copy-start | bytes 110596
  273.5 30.0 %copy-start.12 = (bf16[24,768]{1,0:T(8,128)(2,1)S(1)}, bf16[24,768]{1,0:T(8,128)(2,1)}, u32[]{:S(2)}) copy-start(bf16[24,768]{1,0:T(8,128)(2,1)} %key_ref.3) | copy-start | bytes 110596
  273.6 30.0 %copy-start.13 = (bf16[24,768]{1,0:T(8,128)(2,1)S(1)}, bf16[24,768]{1,0:T(8,128)(2,1)}, u32[]{:S(2)}) copy-start(bf16[24,768]{1,0:T(8,128)(2,1)} %value_ref.3) | copy-start | bytes 110596
  273.6 30.0 %copy-start.16 = (bf16[24]{0:T(256)(128)(2,1)S(1)}, bf16[24]{0:T(256)(128)(2,1)}, u32[]{:S(2)}) copy-start(bf16[24]{0:T(256)(128)(2,1)} %param.16) | copy-start | bytes 148
  287.5 16.1 %all-to-all-start.10 = ((bf16[4,24,2304]{2,1,0:T(8,128)(2,1)}), bf16[4,24,2304]{2,1,0:T(8,128)(2,1)S(1)}, u32[]{:S(2)}, u32[]{:S(2)}) async-start(bf16[4,24,2304]{2,1,0:T(8,128)(2,1)} %bitcast.39), calls=%async_computation.10 | async-start | bytes 884736 | tf_op jit(solution)/shard_map/front_grads/all_to_all | solution.py:103
  291.9 1.2 collective-permute-start.9
  293.8 1.0 copy-start.9
  303.6 0.9 copy-start.10
Sparse Core Ops, SparseCore 0:
  18.1 34.4 all-gather.2
  56.7 79.1 all-gather.4
  187.3 72.7 reduce-scatter.2
  262.3 31.3 reduce-scatter.4

commit v6 on v5

--- a/solution.py
+++ b/solution.py
@@ -19,7 +19,7 @@
 grad_chunk = 1024
 subs = 2
 vmem_bytes = 56 * 1024 * 1024
-few_bytes = 24 * 1024 * 1024
+few_bytes = 40 * 1024 * 1024
 
 
 def bucket_of(relative, total_buckets):

time: 313 us -> 313 us (level)
  no operation moved by 1% of the time
where the time goes in v6:
time: 313 us; the launch traced here: 312 us
  Pallas kernels  98.6 us (32%)
  waiting for transfers between devices  77.5 us (25%)
  blocking collectives  67.1 us (21%)
  starting transfers between devices  36 us (12%)
  local copies, waits for them, and re-layouts  14.3 us (5%)
  between operations  14 us (4%)
  other arithmetic  4.29 us (1%)
    all_to_all x4, waiting for transfers between devices, exchange(): lax.all_to_all(array, 'blk', 0, 0, tiled=True, axis_index_groups=groups)  34.9 us
    pallas_call x2, Pallas kernels, attend_back(): pl.pallas_call(functools.partial(attend_back_kernel, size, blocks, bucket...  27.2 us
    all_to_all x1, blocking collectives, body(): grad_qkv.append(lax.all_to_all(returned, 'blk', 0, 0, tiled=True))  26.5 us
    all_to_all x1, blocking collectives, body(): taken.append(lax.all_to_all(part, 'blk', 0, 0, tiled=True))  25.1 us
    pallas_call x3, Pallas kernels, attend(): pl.pallas_call(functools.partial(attend_kernel, size, blocks, lengths.sha...  24.4 us
    all_gather x1, waiting for transfers between devices, gather_back(): lax.all_gather(shard, 'blk', axis=0, tiled=True, axis_index_groups=across)  19.1 us
    all_to_all x4, starting transfers between devices, exchange(): lax.all_to_all(array, 'blk', 0, 0, tiled=True, axis_index_groups=groups)  17.3 us
    all_to_all x1, blocking collectives, body(): contexts.append(lax.all_to_all(outs[0], 'blk', 0, 0, tiled=True))  15.5 us
  transfers between devices with their start and end apart: 22, of which 16 were waited for; matrix products, arithmetic and copies ran while one was open for 2% of the time, Pallas kernels for 26%

profile of v6, /device:TPU:0, one launch (start us, length us, event | category | flops | bytes accessed | tf_op | source)
XLA Modules:
  0.0 311.8 jit_solution(1333821093391705498)
XLA Ops:
  7.2 1.7 pack.1
  8.9 6.3 %all-to-all-start = ((bf16[4,24,2432]{2,1,0:T(8,128)(2,1)}), bf16[4,24,2432]{2,1,0:T(8,128)(2,1)S(1)}, u32[]{:S(2)}, u32[]{:S(2)}) async-start(bf16[4,24,2432]{2,1,0:T(8,128)(2,1)} %pack.1), calls=%async_computation | async-start | bytes 933888 | tf_op jit(solution)/shard_map/weights/all_to_all | solution.py:103
  15.2 1.8 pad_maximum_fusion
  17.0 11.5 %all-to-all-done = bf16[4,24,2432]{2,1,0:T(8,128)(2,1)S(1)} async-done(((bf16[4,24,2432]{2,1,0:T(8,128)(2,1)}), bf16[4,24,2432]{2,1,0:T(8,128)(2,1)S(1)}, u32[]{:S(2)}, u32[]{:S(2)}) %all-to-all-start) | async-done | bytes 466976 | tf_op jit(solution)/shard_map/weights/all_to_all | solution.py:103
  28.4 1.4 tile.10
  29.8 3.7 %all-to-all-start.1 = ((bf16[4,96,2432]{2,1,0:T(8,128)(2,1)}), bf16[4,96,2432]{2,1,0:T(8,128)(2,1)S(1)}, u32[]{:S(2)}, u32[]{:S(2)}) async-start(bf16[4,96,2432]{2,1,0:T(8,128)(2,1)} %tile.10), calls=%async_computation.1 | async-start | bytes 3735552 | tf_op jit(solution)/shard_map/weights/all_to_all | solution.py:103
  33.6 19.1 %all-gather.3.cloned.1.call-done.refs_0_ = bf16[96,6912]{1,0:T(8,128)(2,1)} async-done(((bf16[24,6912]{1,0:T(8,128)(2,1)}), bf16[96,6912]{1,0:T(8,128)(2,1)}) %all-gather.3.cloned.1.call-update) | async-done | bytes 1327120 | tf_op jit(solution)/shard_map/weights/all_gather | solution.py:154
  52.6 2.7 all-to-all-done.1
  55.3 1.3 copy-done
  56.8 0.7 reshape.64.table_ref
  57.5 2.0 bias_tiles.1.after_ref.band_ref
  59.5 1.2 collective-permute-done.other_ref.refs_4_
  60.7 1.8 copy-done.20
  62.6 2.5 project.1
  65.1 0.9 copy-done.4
  66.0 25.1 %all_to_all.67.taken_ref.refs_1_ = bf16[16,192,128]{2,1,0:T(8,128)(2,1)} all-to-all(bf16[16,192,128]{2,1,0:T(8,128)(2,1)S(1)} %get-tuple-element.54), channel_id=1, replica_groups=mesh['rows'=2,'blk'=16] {'blk'}, dimensions={0} | all-to-all | bytes 1572864 | tf_op jit(solution)/shard_map/project/all_to_all | solution.py:1029
  91.1 3.6 %all-to-all-start.4 = ((bf16[16,192,128]{2,1,0:T(8,128)(2,1)}), bf16[16,192,128]{2,1,0:T(8,128)(2,1)S(1)}, u32[]{:S(2)}, u32[]{:S(2)}) async-start(bf16[16,192,128]{2,1,0:T(8,128)(2,1)} %tie.7), calls=%async_computation.4 | async-start | bytes 1572864 | tf_op jit(solution)/shard_map/project/all_to_all | solution.py:1029
  94.7 2.7 reorder.1.refs_1_.cot_ref
  97.4 0.5 slice_bitcast_fusion
  97.9 10.7 %attend.3 = (bf16[16,64,128]{2,1,0:T(8,128)(2,1)}, f32[64,2048]{1,0:T(8,128)}, bf16[2048,2048]{1,0:T(8,128)(2,1)}, f32[1,2048]{1,0:T(1,128)}) custom-call(s32[6]{0:T(128)} %get-tuple-element.117.bounds_ref, s32[1]{0:T(128)} %bitcast.6.head_ref, f32[384]{0:T(512)} %reshape.64.table_ref, bf16[16,192,128]{2,1,0:T(8,128)(2,1)} %all_to_all.67.taken_ref.refs_1_, ...), custom_call_target="tpu_custom_call" | custom-call | flops 6000000000 | tf_op jit(solution)/shard_map/attend/pallas_call | solution.py:397
  108.7 5.1 %all-to-all-done.4.taken_ref = bf16[16,192,128]{2,1,0:T(8,128)(2,1)S(1)} async-done(((bf16[16,192,128]{2,1,0:T(8,128)(2,1)}), bf16[16,192,128]{2,1,0:T(8,128)(2,1)S(1)}, u32[]{:S(2)}, u32[]{:S(2)}) %all-to-all-start.4) | async-done | bytes 786464 | tf_op jit(solution)/shard_map/project/all_to_all | solution.py:1029
  113.7 5.1 %all-to-all-start.3 = ((bf16[16,64,128]{2,1,0:T(8,128)(2,1)}), bf16[16,64,128]{2,1,0:T(8,128)(2,1)S(1)}, u32[]{:S(2)}, u32[]{:S(2)}) async-start(bf16[16,64,128]{2,1,0:T(8,128)(2,1)} %get-tuple-element.55), calls=%async_computation.3 | async-start | bytes 524288 | tf_op jit(solution)/shard_map/context/all_to_all | solution.py:1043
  118.8 6.9 %attend.4 = (bf16[16,64,128]{2,1,0:T(8,128)(2,1)}, f32[64,2048]{1,0:T(8,128)}, bf16[2048,2048]{1,0:T(8,128)(2,1)}, f32[1,2048]{1,0:T(1,128)}) custom-call(s32[6]{0:T(128)} %get-tuple-element.116.bounds_ref, s32[1]{0:T(128)} %bitcast.6.head_ref, f32[384]{0:T(512)} %reshape.64.table_ref, bf16[16,192,128]{2,1,0:T(8,128)(2,1)} %copy-done.25, ...), custom_call_target="tpu_custom_call" | custom-call | flops 6000000000 | tf_op jit(solution)/shard_map/attend/pallas_call | solution.py:397
  125.8 1.7 all-to-all-done.3.refs_4_.refs_0_
  127.4 0.7 copy-done.23
  128.2 6.8 %attend.5 = (bf16[16,64,128]{2,1,0:T(8,128)(2,1)}, f32[64,2048]{1,0:T(8,128)}, bf16[2048,2048]{1,0:T(8,128)(2,1)}, f32[1,2048]{1,0:T(1,128)}) custom-call(s32[6]{0:T(128)} %get-tuple-element.116.bounds_ref, s32[1]{0:T(128)} %bitcast.6.head_ref, f32[384]{0:T(512)} %reshape.64.table_ref, ...), custom_call_target="tpu_custom_call", output_to_operand_aliasing={{0}: (5, {}), {1}: (6, {}), {2}: (7, {}), {3}: (8, {})} | custom-call | flops 6000000000 | tf_op jit(solution)/shard_map/attend/pallas_call | solution.py:397
  135.0 1.0 all-gather.5.cloned.1.call-done.refs_0_
  135.9 0.9 copy-done.24
  136.9 15.5 %all_to_all.68.refs_1_ = bf16[16,64,128]{2,1,0:T(8,128)(2,1)} all-to-all(bf16[16,64,128]{2,1,0:T(8,128)(2,1)S(1)} %copy-done.24), channel_id=1, replica_groups=mesh['rows'=2,'blk'=16] {'blk'}, dimensions={0} | all-to-all | bytes 524288 | tf_op jit(solution)/shard_map/context/all_to_all | solution.py:1043
  152.4 14.3 %feed.1 = (bf16[256,768]{1,0:T(8,128)(2,1)}, f32[256,768]{1,0:T(8,128)}, bf16[16,64,256]{2,1,0:T(8,128)(2,1)}, bf16[3,256,2048]{2,1,0:T(8,128)(2,1)}, bf16[256,1...) custom-call(s32[1]{0:T(128)} %bitcast.flipped_ref.refs_0_, bf16[256,768]{1,0:T(8,128)(2,1)} %bitcast.33, ...), custom_call_target="tpu_custom_call" | custom-call | flops 8000000000 | tf_op jit(solution)/shard_map/feed/pallas_call | solution.py:671
  166.8 0.5 collective-permute-start.2
  167.3 3.6 %all-to-all-start.6 = ((bf16[16,64,256]{2,1,0:T(8,128)(2,1)}), bf16[16,64,256]{2,1,0:T(8,128)(2,1)S(1)}, u32[]{:S(2)}, u32[]{:S(2)}) async-start(bf16[16,64,256]{2,1,0:T(8,128)(2,1)} %get-tuple-element.64), calls=%async_computation.6 | async-start | bytes 1048576 | tf_op jit(solution)/shard_map/grad_context/all_to_all | solution.py:1053
  171.0 2.9 collective-permute-done.4.refs_5_
  173.9 0.5 collective-permute-done.3.refs_3_
  174.4 0.3 copy-done.29
  174.8 9.7 %weight_grads.1.refs_0_ = bf16[384,6912]{1,0:T(8,128)(2,1)} custom-call(bf16[256,1152]{1,0:T(8,128)(2,1)} %get-tuple-element.67.refs_0_, bf16[256,1152]{1,0:T(8,128)(2,1)} %copy-done.28, bf16[3,256,2048]{2,1,0:T(8,128)(2,1)} %get-tuple-element.69.refs_2_, bf16[3,256,2048]{2,1,0:T(8,128)(2,1)} %collective-permute-done.3.refs_3_, ...), custom_call_target="tpu_custom_call" | custom-call | flops 10000000000 | tf_op jit(solution)/shard_map/back_grads/weight_grads/pallas_call | solution.py:747
  184.6 1.8 all-to-all-done.6.refs_1_.grad_ref
  186.3 0.8 copy-done.22
  187.2 0.5 broadcast_in_dim.20.refs_0_
  187.7 13.4 %attend_back.2 = (bf16[16,192,128]{2,1,0:T(8,128)(2,1)}, f32[1,128]{1,0:T(1,128)}) custom-call(bf16[16,192,128]{2,1,0:T(8,128)(2,1)} %all_to_all.67.taken_ref.refs_1_, bf16[16,64,256]{2,1,0:T(8,128)(2,1)} %copy-done.22, f32[64,2048]{1,0:T(8,128)} %get-tuple-element.57.refs_0_.context_ref, bf16[2048,2048]{1,0:T(8,128)(2,1)} %get-tuple-element.65.expo_ref, ...), custom_call_target="tpu_custom_call" | custom-call | flops 12999999488 | tf_op jit(solution)/shard_map/attend_back/pallas_call | solution.py:524
  201.1 4.4 %all-to-all-start.7 = ((bf16[16,192,128]{2,1,0:T(8,128)(2,1)}), bf16[16,192,128]{2,1,0:T(8,128)(2,1)S(1)}, u32[]{:S(2)}, u32[]{:S(2)}) async-start(bf16[16,192,128]{2,1,0:T(8,128)(2,1)} %get-tuple-element.71), calls=%async_computation.7 | async-start | bytes 1572864 | tf_op jit(solution)/shard_map/grad_qkv/all_to_all | solution.py:1075
  205.6 13.7 %attend_back.3 = (bf16[16,208,128]{2,1,0:T(8,128)(2,1)}, f32[1,128]{1,0:T(1,128)}) custom-call(bf16[16,192,128]{2,1,0:T(8,128)(2,1)} %copy-done.25, bf16[16,64,256]{2,1,0:T(8,128)(2,1)} %copy-done.22, f32[64,2048]{1,0:T(8,128)} %get-tuple-element.72.context_ref, bf16[2048,2048]{1,0:T(8,128)(2,1)} %get-tuple-element.73.expo_ref, ...), custom_call_target="tpu_custom_call" | custom-call | flops 12999999488 | tf_op jit(solution)/shard_map/attend_back/pallas_call | solution.py:524
  219.4 5.4 %all-to-all-done.7.refs_1_.refs_5_.refs_7_ = bf16[16,192,128]{2,1,0:T(8,128)(2,1)S(1)} async-done(((bf16[16,192,128]{2,1,0:T(8,128)(2,1)}), bf16[16,192,128]{2,1,0:T(8,128)(2,1)S(1)}, u32[]{:S(2)}, u32[]{:S(2)}) %all-to-all-start.7) | async-done | bytes 786464 | tf_op jit(solution)/shard_map/grad_qkv/all_to_all | solution.py:1075
  224.8 0.9 copy-done.2
  225.7 26.5 %all_to_all.69.refs_6_.refs_8_ = bf16[16,208,128]{2,1,0:T(8,128)(2,1)S(1)} all-to-all(bf16[16,208,128]{2,1,0:T(8,128)(2,1)} %tie.11), channel_id=1, replica_groups=mesh['rows'=2,'blk'=16] {'blk'}, dimensions={0} | all-to-all | bytes 1703936 | tf_op jit(solution)/shard_map/grad_qkv/all_to_all | solution.py:1075
  252.2 0.5 collective-permute-start.7
  252.8 0.5 collective-permute-start.6
  253.3 2.7 collective-permute-done.5.refs_3_
  256.0 0.3 collective-permute-done.6.refs_4_
  256.2 1.2 copy-done.3
  257.4 3.4 %front_grads.1.refs_10_.refs_1_ = bf16[384,2304]{1,0:T(8,128)(2,1)} custom-call(s32[1]{0:T(128)} %bitcast.flipped_ref.refs_0_, bf16[128,768]{1,0:T(8,128)(2,1)S(1)} %get-tuple-element.115.refs_1_, bf16[128,768]{1,0:T(8,128)(2,1)S(1)} %get-tuple-element.114.refs_2_, bf16[128,768]{1,0:T(8,128)(2,1)S(1)} %collective-permute-done.5.refs_3_, ...), custom_call_target="tpu_custom_call" | custom-call | flops 5000000000 | tf_op jit(solution)/shard_map/front_grads/front_grads/pallas_call | solution.py:920
  260.8 3.6 %all-to-all-start.9 = ((bf16[4,96,2304]{2,1,0:T(8,128)(2,1)}), bf16[4,96,2304]{2,1,0:T(8,128)(2,1)S(1)}, u32[]{:S(2)}, u32[]{:S(2)}) async-start(bf16[4,96,2304]{2,1,0:T(8,128)(2,1)} %bitcast.17), calls=%async_computation.9 | async-start | bytes 3538944 | tf_op jit(solution)/shard_map/front_grads/all_to_all | solution.py:103
  264.4 9.1 %input_grads.1 = (f32[2,128,768]{2,1,0:T(8,128)}, bf16[256,768]{1,0:T(8,128)(2,1)}) custom-call(s32[1]{0:T(128)} %bitcast.flipped_ref.refs_0_, bf16[768,768]{1,0:T(8,128)(2,1)} %constant.18.clone.matrix_ref.refs_1_, bf16[2,128,768]{2,1,0:T(8,128)(2,1)} %copy-done.8, bf16[384,2432]{1,0:T(8,128)(2,1)} %bitcast.31, bf16[384,2432]{1,0:T(8,128)(2,1)} %copy-done.17, ...), custom_call_target="tpu_custom_call" | custom-call | flops 6000000000 | tf_op jit(solution)/shard_map/input_grads/pallas_call | solution.py:879
  273.6 12.7 %all-to-all-done.9 = bf16[4,96,2304]{2,1,0:T(8,128)(2,1)S(1)} async-done(((bf16[4,96,2304]{2,1,0:T(8,128)(2,1)}), bf16[4,96,2304]{2,1,0:T(8,128)(2,1)S(1)}, u32[]{:S(2)}, u32[]{:S(2)}) %all-to-all-start.9) | async-done | bytes 1769504 | tf_op jit(solution)/shard_map/front_grads/all_to_all | solution.py:103
  286.3 1.2 reduce_sum.21.refs_0_
  287.5 3.7 %all-to-all-start.10 = ((bf16[4,24,2304]{2,1,0:T(8,128)(2,1)}), bf16[4,24,2304]{2,1,0:T(8,128)(2,1)S(1)}, u32[]{:S(2)}, u32[]{:S(2)}) async-start(bf16[4,24,2304]{2,1,0:T(8,128)(2,1)} %bitcast.39), calls=%async_computation.10 | async-start | bytes 884736 | tf_op jit(solution)/shard_map/front_grads/all_to_all | solution.py:103
  291.2 0.8 convert_reduce_fusion
  292.0 1.2 collective-permute-done.9
  293.2 0.6 bitcast_add_fusion
  293.8 1.0 copy-done.9
  294.8 0.9 unpack_back.1
  295.6 7.9 %all-to-all-done.10.parts_ref = bf16[4,24,2304]{2,1,0:T(8,128)(2,1)S(1)} async-done(((bf16[4,24,2304]{2,1,0:T(8,128)(2,1)}), bf16[4,24,2304]{2,1,0:T(8,128)(2,1)S(1)}, u32[]{:S(2)}, u32[]{:S(2)}) %all-to-all-start.10) | async-done | bytes 442400 | tf_op jit(solution)/shard_map/front_grads/all_to_all | solution.py:103
  303.6 0.9 copy-done.10
  304.5 0.7 unpack_front.1
  (79 shorter events, 0.9 us)
Async XLA Ops:
  8.9 19.6 %all-to-all-start = ((bf16[4,24,2432]{2,1,0:T(8,128)(2,1)}), bf16[4,24,2432]{2,1,0:T(8,128)(2,1)S(1)}, u32[]{:S(2)}, u32[]{:S(2)}) async-start(bf16[4,24,2432]{2,1,0:T(8,128)(2,1)} %pack.1), calls=%async_computation | async-start | bytes 933888 | tf_op jit(solution)/shard_map/weights/all_to_all | solution.py:103
  15.2 37.4 %all-gather.3.cloned.1.call-start = ((), (), s32[]{:S(2)}) async-start(), calls=%async_computation.13 | async-start | bytes 1658880 | tf_op jit(solution)/shard_map/weights/all_gather | solution.py:154
  29.8 25.5 %all-to-all-start.1 = ((bf16[4,96,2432]{2,1,0:T(8,128)(2,1)}), bf16[4,96,2432]{2,1,0:T(8,128)(2,1)S(1)}, u32[]{:S(2)}, u32[]{:S(2)}) async-start(bf16[4,96,2432]{2,1,0:T(8,128)(2,1)} %tile.10), calls=%async_computation.1 | async-start | bytes 3735552 | tf_op jit(solution)/shard_map/weights/all_to_all | solution.py:103
  33.6 23.1 %copy-start.26 = (bf16[32,12]{0,1:T(8,128)(2,1)S(1)}, bf16[32,12]{0,1:T(8,128)(2,1)}, u32[]{:S(2)}) copy-start(bf16[32,12]{0,1:T(8,128)(2,1)} %param.25) | copy-start | bytes 2308
  33.6 102.3 %all-gather.5.cloned.1.call-start = ((), (), s32[]{:S(2)}) async-start(), calls=%async_computation.14 | async-start | bytes 6635520 | tf_op jit(solution)/shard_map/weights/all_gather | solution.py:156
  55.3 1.3 copy-start
  56.6 4.1 %collective-permute-start = (bf16[384,2432]{1,0:T(8,128)(2,1)}, bf16[384,2432]{1,0:T(8,128)(2,1)S(1)}, u32[]{:S(2)}, u32[]{:S(2)}) collective-permute-start(bf16[384,2432]{1,0:T(8,128)(2,1)} %bitcast.30), channel_id=1, source_target_pairs={{0,16},{16,0},{1,17},{17,1},{2,18},{18,2},{3,19},{19,3},{4,20},{20... | collective-permute-start | bytes 5603336 | tf_op jit(solution)/shard_map/weights/ppermute | solution.py:49
  57.5 3.2 %copy-start.1 = (bf16[4,96,2432]{2,1,0:T(8,128)(2,1)S(1)}, bf16[4,96,2432]{2,1,0:T(8,128)(2,1)}, u32[]{:S(2)}) copy-start(bf16[4,96,2432]{2,1,0:T(8,128)(2,1)} %copy-done) | copy-start | bytes 5603332
  57.5 3.2 %copy-start.18 = (bf16[2,1,128,768]{3,2,1,0:T(8,128)(2,1)S(1)}, bf16[2,1,128,768]{3,2,1,0:T(8,128)(2,1)}, u32[]{:S(2)}) copy-start(bf16[2,1,128,768]{3,2,1,0:T(8,128)(2,1)} %param.14) | copy-start | bytes 1179652
  57.5 3.2 %copy-start.19 = (bf16[768,768]{1,0:T(8,128)(2,1)S(1)}, bf16[768,768]{1,0:T(8,128)(2,1)}, u32[]{:S(2)}) copy-start(bf16[768,768]{1,0:T(8,128)(2,1)} %constant.18.clone.matrix_ref.refs_1_) | copy-start | bytes 3538948
  60.7 4.4 %copy-start.17 = (bf16[384,2432]{1,0:T(8,128)(2,1)}, bf16[384,2432]{1,0:T(8,128)(2,1)S(1)}, u32[]{:S(2)}) copy-start(bf16[384,2432]{1,0:T(8,128)(2,1)S(1)} %collective-permute-done.other_ref.refs_4_) | copy-start | bytes 5603332
  60.7 1.8 copy-start.20
  65.1 0.9 copy-start.4
  66.0 25.1 %copy-start.8 = (bf16[2,128,768]{2,1,0:T(8,128)(2,1)}, bf16[2,128,768]{2,1,0:T(8,128)(2,1)S(1)}, u32[]{:S(2)}) copy-start(bf16[2,128,768]{2,1,0:T(8,128)(2,1)S(1)} %get-tuple-element.51.refs_2_) | copy-start | bytes 1179652
  66.0 25.1 %copy-start.14 = (f32[1,768]{1,0:T(1,128)}, f32[1,768]{1,0:T(1,128)S(1)}, u32[]{:S(2)}) copy-start(f32[1,768]{1,0:T(1,128)S(1)} %get-tuple-element.53.gain_ref) | copy-start | bytes 9220
  66.0 31.4 %copy-start.21 = (f32[1,768]{1,0:T(1,128)}, f32[1,768]{1,0:T(1,128)S(1)}, u32[]{:S(2)}) copy-start(f32[1,768]{1,0:T(1,128)S(1)} %get-tuple-element.52.refs_5_) | copy-start | bytes 9220
  91.1 22.6 %all-to-all-start.4 = ((bf16[16,192,128]{2,1,0:T(8,128)(2,1)}), bf16[16,192,128]{2,1,0:T(8,128)(2,1)S(1)}, u32[]{:S(2)}, u32[]{:S(2)}) async-start(bf16[16,192,128]{2,1,0:T(8,128)(2,1)} %tie.7), calls=%async_computation.4 | async-start | bytes 1572864 | tf_op jit(solution)/shard_map/project/all_to_all | solution.py:1029
  94.7 2.7 copy-start.27
  113.7 5.1 %copy-start.25 = (bf16[16,192,128]{2,1,0:T(8,128)(2,1)}, bf16[16,192,128]{2,1,0:T(8,128)(2,1)S(1)}, u32[]{:S(2)}) copy-start(bf16[16,192,128]{2,1,0:T(8,128)(2,1)S(1)} %all-to-all-done.4.taken_ref) | copy-start | bytes 2359300
  113.7 13.7 %all-to-all-start.3 = ((bf16[16,64,128]{2,1,0:T(8,128)(2,1)}), bf16[16,64,128]{2,1,0:T(8,128)(2,1)S(1)}, u32[]{:S(2)}, u32[]{:S(2)}) async-start(bf16[16,64,128]{2,1,0:T(8,128)(2,1)} %get-tuple-element.55), calls=%async_computation.3 | async-start | bytes 524288 | tf_op jit(solution)/shard_map/context/all_to_all | solution.py:1043
  127.4 0.7 copy-start.23
  135.9 0.9 copy-start.24
  135.9 16.5 %collective-permute-start.1 = (bf16[384,6912]{1,0:T(8,128)(2,1)}, bf16[384,6912]{1,0:T(8,128)(2,1)}, u32[]{:S(2)}, u32[]{:S(2)}) collective-permute-start(bf16[384,6912]{1,0:T(8,128)(2,1)} %tie.9.refs_2_.refs_4_.refs_6_.refs_8_), channel_id=1, source_target_pairs={{0,16},{16,0},{1,17},{17,1},{2,18},{18,2},{3,19},{19,3},{4,20},{20... | collective-permute-start | bytes 15925256 | tf_op jit(solution)/shard_map/weights/ppermute | solution.py:49
  166.7 7.7 %collective-permute-start.3 = (bf16[3,256,2048]{2,1,0:T(8,128)(2,1)}, bf16[3,256,2048]{2,1,0:T(8,128)(2,1)}, u32[]{:S(2)}, u32[]{:S(2)}) collective-permute-start(bf16[3,256,2048]{2,1,0:T(8,128)(2,1)} %get-tuple-element.69.refs_2_), channel_id=1, source_target_pairs={{0,16},{16,0},{1,17},{17,1},{2,18},{18,2},{3,19},{19,3},{4,20},{20... | collective-permute-start | bytes 9437192 | tf_op jit(solution)/shard_map/packet/ppermute | solution.py:49
  166.8 7.1 %collective-permute-start.2 = (bf16[256,1152]{1,0:T(8,128)(2,1)}, bf16[256,1152]{1,0:T(8,128)(2,1)S(1)}, u32[]{:S(2)}, u32[]{:S(2)}) collective-permute-start(bf16[256,1152]{1,0:T(8,128)(2,1)} %get-tuple-element.68), channel_id=1, source_target_pairs={{0,16},{16,0},{1,17},{17,1},{2,18},{18,2},{3,19},{19,3},{4,20},{20... | collective-permute-start | bytes 1769480 | tf_op jit(solution)/shard_map/packet/ppermute | solution.py:49
  167.3 6.6 %collective-permute-start.4 = (bf16[256,1024]{1,0:T(8,128)(2,1)}, bf16[256,1024]{1,0:T(8,128)(2,1)S(1)}, u32[]{:S(2)}, u32[]{:S(2)}) collective-permute-start(bf16[256,1024]{1,0:T(8,128)(2,1)} %get-tuple-element.70.refs_4_), channel_id=1, source_target_pairs={{0,16},{16,0},{1,17},{17,1},{2,18},{18,2},{3,19},{19,3},{4,20},{20... | collective-permute-start | bytes 1572872 | tf_op jit(solution)/shard_map/packet/ppermute | solution.py:49
  167.3 19.0 %all-to-all-start.6 = ((bf16[16,64,256]{2,1,0:T(8,128)(2,1)}), bf16[16,64,256]{2,1,0:T(8,128)(2,1)S(1)}, u32[]{:S(2)}, u32[]{:S(2)}) async-start(bf16[16,64,256]{2,1,0:T(8,128)(2,1)} %get-tuple-element.64), calls=%async_computation.6 | async-start | bytes 1048576 | tf_op jit(solution)/shard_map/grad_context/all_to_all | solution.py:1053
  170.9 89.8 %reduce-scatter.3.cloned.1.call-start = ((), (), s32[]{:S(2)}) async-start(), calls=%async_computation.15 | async-start | bytes 6635520 | tf_op jit(solution)/shard_map/back_grads/reduce_scatter | solution.py:180
  173.9 0.8 copy-start.29
  173.9 1.0 copy-start.28
  186.3 0.8 copy-start.22
  201.1 23.6 %all-to-all-start.7 = ((bf16[16,192,128]{2,1,0:T(8,128)(2,1)}), bf16[16,192,128]{2,1,0:T(8,128)(2,1)S(1)}, u32[]{:S(2)}, u32[]{:S(2)}) async-start(bf16[16,192,128]{2,1,0:T(8,128)(2,1)} %get-tuple-element.71), calls=%async_computation.7 | async-start | bytes 1572864 | tf_op jit(solution)/shard_map/grad_qkv/all_to_all | solution.py:1075
  205.6 88.2 %reduce-scatter.5.cloned.1.call-start = ((), (), s32[]{:S(2)}) async-start(), calls=%async_computation.16 | async-start | bytes 1658880 | tf_op jit(solution)/shard_map/front_grads/reduce_scatter | solution.py:187
  224.7 0.9 copy-start.2
  252.2 8.6 %copy-start.5 = (bf16[16,208,128]{2,1,0:T(8,128)(2,1)}, bf16[16,208,128]{2,1,0:T(8,128)(2,1)S(1)}, u32[]{:S(2)}) copy-start(bf16[16,208,128]{2,1,0:T(8,128)(2,1)S(1)} %all_to_all.69.refs_6_.refs_8_) | copy-start | bytes 2555908
  252.2 4.1 %collective-permute-start.8 = (bf16[16,208,128]{2,1,0:T(8,128)(2,1)S(1)}, bf16[16,208,128]{2,1,0:T(8,128)(2,1)S(1)}, u32[]{:S(2)}, u32[]{:S(2)}) collective-permute-start(bf16[16,208,128]{2,1,0:T(8,128)(2,1)S(1)} %all_to_all.69.refs_6_.refs_8_), channel_id=1, source_target_pairs={{0,16},{16,0},{1,17},{17,1},{2,18},{18,2},{3,19},{19,3},{4,20},{20... | collective-permute-start | bytes 2555912 | tf_op jit(solution)/shard_map/front_grads/ppermute | solution.py:49
  252.2 4.1 %collective-permute-start.7 = (bf16[16,192,128]{2,1,0:T(8,128)(2,1)}, bf16[16,192,128]{2,1,0:T(8,128)(2,1)S(1)}, u32[]{:S(2)}, u32[]{:S(2)}) collective-permute-start(bf16[16,192,128]{2,1,0:T(8,128)(2,1)} %copy-done.2), channel_id=1, source_target_pairs={{0,16},{16,0},{1,17},{17,1},{2,18},{18,2},{3,19},{19,3},{4,20},{20... | collective-permute-start | bytes 2359304 | tf_op jit(solution)/shard_map/front_grads/ppermute | solution.py:49
  252.7 3.2 %collective-permute-start.5 = (bf16[128,768]{1,0:T(8,128)(2,1)S(1)}, bf16[128,768]{1,0:T(8,128)(2,1)S(1)}, u32[]{:S(2)}, u32[]{:S(2)}) collective-permute-start(bf16[128,768]{1,0:T(8,128)(2,1)S(1)} %get-tuple-element.115.refs_1_), channel_id=1, source_target_pairs={{0,16},{16,0},{1,17},{17,1},{2,18},{18,2},{3,19},{19,3},{4,20},{20... | collective-permute-start | bytes 589832 | tf_op jit(solution)/shard_map/front_grads/ppermute | solution.py:49
  252.8 3.4 %collective-permute-start.6 = (bf16[128,768]{1,0:T(8,128)(2,1)S(1)}, bf16[128,768]{1,0:T(8,128)(2,1)S(1)}, u32[]{:S(2)}, u32[]{:S(2)}) collective-permute-start(bf16[128,768]{1,0:T(8,128)(2,1)S(1)} %get-tuple-element.114.refs_2_), channel_id=1, source_target_pairs={{0,16},{16,0},{1,17},{17,1},{2,18},{18,2},{3,19},{19,3},{4,20},{20... | collective-permute-start | bytes 589832 | tf_op jit(solution)/shard_map/front_grads/ppermute | solution.py:49
  256.2 1.2 copy-start.3
  260.8 25.5 %all-to-all-start.9 = ((bf16[4,96,2304]{2,1,0:T(8,128)(2,1)}), bf16[4,96,2304]{2,1,0:T(8,128)(2,1)S(1)}, u32[]{:S(2)}, u32[]{:S(2)}) async-start(bf16[4,96,2304]{2,1,0:T(8,128)(2,1)} %bitcast.17), calls=%async_computation.9 | async-start | bytes 3538944 | tf_op jit(solution)/shard_map/front_grads/all_to_all | solution.py:103
  273.5 20.3 %copy-start.6 = (bf16[24,2048]{1,0:T(8,128)(2,1)S(1)}, bf16[24,2048]{1,0:T(8,128)(2,1)}, u32[]{:S(2)}) copy-start(bf16[24,2048]{1,0:T(8,128)(2,1)} %up_ref.1) | copy-start | bytes 294916
  273.5 20.3 %copy-start.7 = (bf16[24,2048]{1,0:T(8,128)(2,1)S(1)}, bf16[24,2048]{1,0:T(8,128)(2,1)}, u32[]{:S(2)}) copy-start(bf16[24,2048]{1,0:T(8,128)(2,1)} %gate_ref.1) | copy-start | bytes 294916
  273.5 20.3 %copy-start.15 = (bf16[24]{0:T(256)(128)(2,1)S(1)}, bf16[24]{0:T(256)(128)(2,1)}, u32[]{:S(2)}) copy-start(bf16[24]{0:T(256)(128)(2,1)} %param.21) | copy-start | bytes 148
  273.5 30.0 %copy-start.11 = (bf16[24,768]{1,0:T(8,128)(2,1)S(1)}, bf16[24,768]{1,0:T(8,128)(2,1)}, u32[]{:S(2)}) copy-start(bf16[24,768]{1,0:T(8,128)(2,1)} %query_ref.3) | copy-start | bytes 110596
  273.5 30.0 %copy-start.12 = (bf16[24,768]{1,0:T(8,128)(2,1)S(1)}, bf16[24,768]{1,0:T(8,128)(2,1)}, u32[]{:S(2)}) copy-start(bf16[24,768]{1,0:T(8,128)(2,1)} %key_ref.3) | copy-start | bytes 110596
  273.6 30.0 %copy-start.13 = (bf16[24,768]{1,0:T(8,128)(2,1)S(1)}, bf16[24,768]{1,0:T(8,128)(2,1)}, u32[]{:S(2)}) copy-start(bf16[24,768]{1,0:T(8,128)(2,1)} %value_ref.3) | copy-start | bytes 110596
  273.6 30.0 %copy-start.16 = (bf16[24]{0:T(256)(128)(2,1)S(1)}, bf16[24]{0:T(256)(128)(2,1)}, u32[]{:S(2)}) copy-start(bf16[24]{0:T(256)(128)(2,1)} %param.16) | copy-start | bytes 148
  287.5 16.1 %all-to-all-start.10 = ((bf16[4,24,2304]{2,1,0:T(8,128)(2,1)}), bf16[4,24,2304]{2,1,0:T(8,128)(2,1)S(1)}, u32[]{:S(2)}, u32[]{:S(2)}) async-start(bf16[4,24,2304]{2,1,0:T(8,128)(2,1)} %bitcast.39), calls=%async_computation.10 | async-start | bytes 884736 | tf_op jit(solution)/shard_map/front_grads/all_to_all | solution.py:103
  291.9 1.2 collective-permute-start.9
  293.8 1.0 copy-start.9
  303.6 0.9 copy-start.10
Sparse Core Ops, SparseCore 0:
  18.1 34.4 all-gather.2
  56.7 79.1 all-gather.4
  187.3 72.7 reduce-scatter.2
  262.3 31.3 reduce-scatter.4
